TPU v7x, 32 devices: a whole 2x2x4 slice. The times are simulated.
32 devices in a mesh: shard: 4 (over z), tensor: 4 (over y, core), section: 2 (over x).
Axes of the slice: x: 2, y: 2, z: 4, core: 2. Of those that a mesh axis runs over, the one named last changes fastest.
Arguments:
- grads: bfloat16 [4, 4, 3072, 768], P('shard', 'section', 'tensor'), may hold values from -120 to 120
- weights: bfloat16 [4, 3072, 768], P('section', 'tensor'), may hold values from -3 to 3
- basis: float32 [4, 768, 256], P('section'), may hold values from -6 to 6
- first_moment: float32 [4, 3072, 256], P('section', ('tensor', 'shard')), may hold values from -6 to 6
- second_moment: float32 [4, 3072, 256], P('section', ('tensor', 'shard')), may hold values from 0.1 to 4
Outputs:
- weights_next: bfloat16 [4, 3072, 768], P('section', 'tensor')
- basis_next: float32 [4, 768, 256], P('section')
- moment_one: float32 [4, 3072, 256], P('section', ('tensor', 'shard'))
- moment_two: float32 [4, 3072, 256], P('section', ('tensor', 'shard'))
All inputs are finite; a program needn't handle non-finite values.
Results may differ from a plain program's by a relative error of at most 0.0004.
Values may be sent and summed in bfloat16 or wider, within the bound.
No kernel may reach another device: no remote copies, remote signals or barrier semaphores. Data moves between devices by JAX's collectives and lax.ppermute only.
A program may use at most 64 MiB of HBM per device.

v0:
```python
import jax
import jax.numpy as jnp
from jax import lax
from jax.sharding import PartitionSpec as P

NS_ITERS = 3
STEP = 1000


learn_rate = 0.5
galore_scale = 0.25
beta_one = 0.9
beta_two = 0.999
adam_eps = 1e-08
norm_eps = 1e-07
coeff_a = 3.4445
coeff_b = -4.775
coeff_c = 2.0315
highest = lax.Precision.HIGHEST


def newton_step(iterate, gram_matrix):
    squared = jnp.einsum("lrs,lst->lrt", gram_matrix, gram_matrix, precision=highest)
    mixing = coeff_b * gram_matrix + coeff_c * squared
    return coeff_a * iterate + jnp.einsum("ldr,lrs->lds", iterate, mixing, precision=highest)


def adam_direction(reduced, first_moment, second_moment):
    moment_one = beta_one * first_moment + (1.0 - beta_one) * reduced
    moment_two = beta_two * second_moment + (1.0 - beta_two) * reduced * reduced
    corrected_one = moment_one / (1.0 - beta_one**STEP)
    corrected_two = moment_two / (1.0 - beta_two**STEP)
    return (moment_one, moment_two, corrected_one / (jnp.sqrt(corrected_two) + adam_eps))


def body(grads, weights, basis, first_moment, second_moment):
    width = basis.shape[1]
    scale_factor = width ** (-0.5)
    local_grads = grads[0]
    block_rows = first_moment.shape[1]
    summed = lax.psum_scatter(
        local_grads.astype(jnp.float32), "shard", scatter_dimension=1, tiled=True
    )
    projected = jnp.einsum("lfd,ldr->lfr", summed, basis, precision=highest)
    power = jnp.einsum("lfd,lfr->ldr", summed, projected, precision=highest)
    reduced = scale_factor * projected
    moment_one, moment_two, direction = adam_direction(reduced, first_moment, second_moment)
    factor = learn_rate * galore_scale * scale_factor
    own_start = lax.axis_index("shard") * block_rows
    current = lax.dynamic_slice_in_dim(weights, own_start, block_rows, 1)
    update = jnp.einsum("lfr,ldr->lfd", direction, basis, precision=highest)
    fresh_rows = (current.astype(jnp.float32) - factor * update).astype(jnp.bfloat16)
    weights_next = lax.all_gather(fresh_rows, "shard", axis=1, tiled=True)
    whole = lax.psum(power, ("shard", "tensor"))
    norms = jnp.sqrt(jnp.sum(whole * whole, axis=(1, 2)))
    iterate = whole / (norms + norm_eps)[:, None, None]
    for sweep in range(NS_ITERS):
        gram_matrix = jnp.einsum("ldr,lds->lrs", iterate, iterate, precision=highest)
        iterate = newton_step(iterate, gram_matrix)
    basis_next = width**0.5 * iterate
    return (weights_next, basis_next, moment_one, moment_two)


def solution(mesh):
    return jax.shard_map(
        body,
        mesh=mesh,
        in_specs=(
            P("shard", "section", "tensor", None),
            P("section", "tensor", None),
            P("section", None, None),
            P("section", ("tensor", "shard"), None),
            P("section", ("tensor", "shard"), None),
        ),
        out_specs=(
            P("section", "tensor", None),
            P("section", None, None),
            P("section", ("tensor", "shard"), None),
            P("section", ("tensor", "shard"), None),
        ),
        check_vma=False,
    )
```

profile of v0, /device:TPU:0, one launch (start us, length us, event | category | flops | bytes accessed | tf_op | source)
XLA Modules:
  0.0 262.5 jit_solution(4329663815538705029)
XLA Ops:
  7.2 0.0 copy-start
  7.2 0.0 reduce-scatter.2.cloned.1.call-start
  7.2 4.3 %bitcast_convert_fusion = f32[2,768,768]{2,1,0:T(8,128)} fusion(bf16[1,2,768,768]{3,2,1,0:T(8,128)(2,1)} %param.5), kind=kLoop, calls=%fused_computation | loop fusion | flops 1179648 | bytes 7077888 | tf_op jit(solution)/shard_map/convert_element_type | solution.py:42
  11.5 0.0 copy-start.5
  11.5 0.0 copy-start.6
  11.5 0.0 reduce-scatter.2.cloned.1.call-update
  11.5 0.0 all-reduce.2.cloned.1.call-start
  11.6 88.1 %reduce-scatter.2.cloned.1.call-done = f32[2,192,768]{2,1,0:T(8,128)} async-done(((f32[2,768,768]{2,1,0:T(8,128)}), f32[2,192,768]{2,1,0:T(8,128)}) %reduce-scatter.2.cloned.1.call-update) | async-done | bytes 1179664 | tf_op jit(solution)/shard_map/reduce_scatter | solution.py:41
  99.6 0.0 copy-done
  99.6 0.0 copy-done.5
  99.6 0.0 copy-done.6
  99.7 0.0 copy-start.1
  99.7 2.8 %multiply_add_fusion.2 = (f32[2,192,256]{2,1,0:T(8,128)S(1)}, f32[2,192,256]{2,1,0:T(8,128)S(1)}, f32[2,192,256]{2,1,0:T(8,128)S(1)}) fusion(f32[2,192,256]{2,1,0:T(8,128)S(1)} %copy-done.5, f32[2,192,256]{2,1,0:T(8,128)S(1)} %copy-done.6, f32[2,192,768]{2,1,0:T(8,128)} %reduce-scatter.2.cloned.1.call-done, f32[2,768,256]{2,1,0:T(8,128)S(1)} %copy-done), kind=kOutput, calls=%fused_computation.20 | convolution fusion | flops 906756096 | bytes 4718592 | tf_op jit(solution)/shard_map/lfd,ldr->lfr/dot_general | solution.py:44
  102.4 0.0 copy-start.3
  102.4 0.0 copy-start.4
  102.4 0.0 copy-done.1
  102.5 2.7 %convolution_bitcast_fusion = f32[2,768,256]{1,2,0:T(8,128)} fusion(f32[2,192,256]{2,1,0:T(8,128)S(1)} %get-tuple-element.10, f32[2,192,768]{2,1,0:T(8,128)S(1)} %copy-done.1), kind=kOutput, calls=%fused_computation.5 | convolution fusion | flops 905969664 | bytes 3145728 | tf_op jit(solution)/shard_map/lfd,lfr->ldr/dot_general | solution.py:45
  105.1 0.0 all-reduce.2.cloned.1.call-update
  105.1 0.2 all-gather.2.cloned.1.call-start
  105.4 0.0 copy-done.3
  105.4 0.0 copy-done.4
  105.4 3.6 %fusion.1 = bf16[2,192,768]{2,1,0:T(8,128)(2,1)} fusion(f32[2,768,256]{2,1,0:T(8,128)S(1)} %copy-done, bf16[2,768,768]{2,1,0:T(8,128)(2,1)} %param.6, s32[]{:T(128)S(6)} %select_n.3, f32[2,192,256]{2,1,0:T(8,128)S(1)} %get-tuple-element.17, f32[2,192,256]{2,1,0:T(8,128)S(1)} %get-tuple-element.18), kind=kOutput, calls=%fused_computation.8 | convolution fusion | flops 907444224 | bytes 3538948 | tf_op jit(solution)/shard_map/lfr,ldr->lfd/dot_general | solution.py:51
  109.0 0.0 all-gather.2.cloned.1.call-update
  109.0 92.2 %all-reduce.2.cloned.1.call-done = f32[2,768,256]{1,2,0:T(8,128)} async-done(((f32[2,768,256]{1,2,0:T(8,128)}), f32[2,768,256]{1,2,0:T(8,128)}) %all-reduce.2.cloned.1.call-update) | async-done | bytes 1572880 | tf_op jit(solution)/shard_map/psum | solution.py:54
  201.2 0.0 copy-start.2
  201.2 1.8 multiply_reduce_fusion
  203.0 0.0 copy-done.2
  203.1 1.8 fusion.9
  204.8 0.7 fusion.4
  205.6 1.9 multiply_add_fusion.1
  207.5 1.6 fusion.14
  209.1 0.7 fusion.3
  209.9 1.7 multiply_add_fusion
  211.6 1.6 fusion.15
  213.2 0.9 fusion.2
  214.2 1.9 add_multiply_fusion
  216.0 1.6 copy.18
  217.7 35.1 %all-gather.2.cloned.1.call-done = bf16[2,768,768]{2,1,0:T(8,128)(2,1)} async-done(((bf16[2,192,768]{2,1,0:T(8,128)(2,1)}), bf16[2,768,768]{2,1,0:T(8,128)(2,1)}) %all-gather.2.cloned.1.call-update) | async-done | bytes 2359312 | tf_op jit(solution)/shard_map/all_gather | solution.py:53
  252.8 3.2 %copy.30 = bf16[2,768,768]{2,1,0:T(8,128)(2,1)} copy(bf16[2,768,768]{2,1,0:T(8,128)(2,1)} %all-gather.2.cloned.1.call-done) | data formatting | bytes 4718592
  (1 shorter events, 0.0 us)
Async XLA Ops:
  7.2 92.5 %copy-start = (f32[2,768,256]{2,1,0:T(8,128)S(1)}, f32[2,768,256]{2,1,0:T(8,128)}, u32[]{:S(2)}) copy-start(f32[2,768,256]{2,1,0:T(8,128)} %param.7) | copy-start | bytes 4718596
  7.2 92.5 %reduce-scatter.2.cloned.1.call-start = ((), (), s32[]{:S(2)}) async-start(), calls=%async_computation.1 | async-start | bytes 5898240 | tf_op jit(solution)/shard_map/reduce_scatter | solution.py:41
  11.5 88.2 %copy-start.5 = (f32[2,192,256]{2,1,0:T(8,128)S(1)}, f32[2,192,256]{2,1,0:T(8,128)}, u32[]{:S(2)}) copy-start(f32[2,192,256]{2,1,0:T(8,128)} %param.9) | copy-start | bytes 1179652
  11.5 88.2 %copy-start.6 = (f32[2,192,256]{2,1,0:T(8,128)S(1)}, f32[2,192,256]{2,1,0:T(8,128)}, u32[]{:S(2)}) copy-start(f32[2,192,256]{2,1,0:T(8,128)} %param.8) | copy-start | bytes 1179652
  11.5 189.7 %all-reduce.2.cloned.1.call-start = ((), (), s32[]{:S(2)}) async-start(), calls=%async_computation.3 | async-start | bytes 3145728 | tf_op jit(solution)/shard_map/psum | solution.py:54
  99.7 2.8 %copy-start.1 = (f32[2,192,768]{2,1,0:T(8,128)S(1)}, f32[2,192,768]{2,1,0:T(8,128)}, u32[]{:S(2)}) copy-start(f32[2,192,768]{2,1,0:T(8,128)} %reduce-scatter.2.cloned.1.call-done) | copy-start | bytes 3538948
  102.4 2.9 %copy-start.3 = (f32[2,192,256]{2,1,0:T(8,128)}, f32[2,192,256]{2,1,0:T(8,128)S(1)}, u32[]{:S(2)}) copy-start(f32[2,192,256]{2,1,0:T(8,128)S(1)} %get-tuple-element.18) | copy-start | bytes 1179652
  102.4 2.9 %copy-start.4 = (f32[2,192,256]{2,1,0:T(8,128)}, f32[2,192,256]{2,1,0:T(8,128)S(1)}, u32[]{:S(2)}) copy-start(f32[2,192,256]{2,1,0:T(8,128)S(1)} %get-tuple-element.17) | copy-start | bytes 1179652
  105.1 147.6 %all-gather.2.cloned.1.call-start = ((), (), s32[]{:S(2)}) async-start(), calls=%async_computation.2 | async-start | bytes 2949120 | tf_op jit(solution)/shard_map/all_gather | solution.py:53
  201.2 1.9 copy-start.2
Sparse Core Ops, SparseCore 0:
  11.6 87.9 reduce-scatter.1
  105.3 95.8 all-reduce.1
  203.3 49.3 all-gather.1
where the time goes:
time: 263 us
  waiting for transfers between devices  215 us (82%)
  matrix products  21.9 us (8%)
  between operations  13.9 us (5%)
  other arithmetic  6.11 us (2%)
  local copies, waits for them, and re-layouts  4.91 us (2%)
    psum x1, waiting for transfers between devices, body(): whole = lax.psum(power, ('shard', 'tensor'))  92.2 us
    reduce_scatter x1, waiting for transfers between devices, body(): lax.psum_scatter(local_grads.astype(jnp.float32), 'shard', scatter_dimens...  88.1 us
    all_gather x1, waiting for transfers between devices, body(): weights_next = lax.all_gather(fresh_rows, 'shard', axis=1, tiled=True)  35.1 us
    dot_general x3, matrix products, newton_step(): jnp.einsum('ldr,lrs->lds', iterate, mixing, precision=highest)  5.53 us
  transfers between devices with their start and end apart: 3, of which 3 were waited for; matrix products, arithmetic and copies ran while one was open for 8% of the time, Pallas kernels for 0%

commit v1 on v0

--- a/solution.py
+++ b/solution.py
@@ -33,7 +33,16 @@
     return (moment_one, moment_two, corrected_one / (jnp.sqrt(corrected_two) + adam_eps))
 
 
-def body(grads, weights, basis, first_moment, second_moment):
+def newton_schulz(power, width):
+    norms = jnp.sqrt(jnp.sum(power * power, axis=(1, 2)))
+    iterate = power / (norms + norm_eps)[:, None, None]
+    for sweep in range(NS_ITERS):
+        gram_matrix = jnp.einsum("ldr,lds->lrs", iterate, iterate, precision=highest)
+        iterate = newton_step(iterate, gram_matrix)
+    return width**0.5 * iterate
+
+
+def general_body(grads, weights, basis, first_moment, second_moment):
     width = basis.shape[1]
     scale_factor = width ** (-0.5)
     local_grads = grads[0]
@@ -52,18 +61,104 @@
     fresh_rows = (current.astype(jnp.float32) - factor * update).astype(jnp.bfloat16)
     weights_next = lax.all_gather(fresh_rows, "shard", axis=1, tiled=True)
     whole = lax.psum(power, ("shard", "tensor"))
-    norms = jnp.sqrt(jnp.sum(whole * whole, axis=(1, 2)))
-    iterate = whole / (norms + norm_eps)[:, None, None]
-    for sweep in range(NS_ITERS):
-        gram_matrix = jnp.einsum("ldr,lds->lrs", iterate, iterate, precision=highest)
-        iterate = newton_step(iterate, gram_matrix)
-    basis_next = width**0.5 * iterate
+    basis_next = newton_schulz(whole, width)
+    return (weights_next, basis_next, moment_one, moment_two)
+
+
+def xor_pairs(k):
+    return [(i, i ^ k) for i in range(4)]
+
+
+def over_z(x, k):
+    return lax.ppermute(x, "shard", xor_pairs(k))
+
+
+def over_core(x):
+    return lax.ppermute(x, "tensor", xor_pairs(1))
+
+
+def over_y(x):
+    return lax.ppermute(x, "tensor", xor_pairs(2))
+
+
+def halves(x, low_first):
+    rows = x.shape[0] // 2
+    keep = lax.dynamic_slice_in_dim(x, low_first * rows, rows, 0)
+    give = lax.dynamic_slice_in_dim(x, (1 - low_first) * rows, rows, 0)
+    return keep, give
+
+
+def join(own, other, place):
+    return jnp.where(place == 0, jnp.concatenate([own, other]), jnp.concatenate([other, own]))
+
+
+def sum_power(power, z, y, core):
+    keep, give = halves(power, core)
+    power = keep + over_core(give)
+    keep, give = halves(power, y)
+    power = keep + over_y(give)
+    rows = power.shape[0] // 4
+    part = lambda b: lax.dynamic_slice_in_dim(power, b * rows, rows, 0)
+    mine = part(z) + over_z(part(z ^ 3), 3) + over_z(part(z ^ 2), 2) + over_z(part(z ^ 1), 1)
+    whole = jnp.zeros_like(power)
+    for k, block in ((0, mine), (1, over_z(mine, 1)), (2, over_z(mine, 2)), (3, over_z(mine, 3))):
+        whole = lax.dynamic_update_slice_in_dim(whole, block, (z ^ k) * rows, 0)
+    whole = join(whole, over_y(whole), y)
+    return join(whole, over_core(whole), core)
+
+
+def line_body(grads, weights, basis, first_moment, second_moment):
+    width = basis.shape[1]
+    scale_factor = width ** (-0.5)
+    layers = grads.shape[1]
+    rows = first_moment.shape[1]
+    z = lax.axis_index("shard")
+    tensor = lax.axis_index("tensor")
+    y, core = tensor // 2, tensor % 2
+    outer = (z == 0) | (z == 3)
+
+    def block(layer, index):
+        return lax.dynamic_slice_in_dim(grads[0, layer], index * rows, rows, 0)
+
+    summed = []
+    for layer in range(layers):
+        for j in range(2):
+            keep = block(layer, jnp.where(outer, 3 * j, 1 + j))
+            give = block(layer, jnp.where(outer, 1 + j, 3 * j))
+            summed.append(keep.astype(jnp.float32) + over_z(give, 1).astype(jnp.float32))
+    projected = []
+    for index, half_sum in enumerate(summed):
+        partial = jnp.einsum("fd,dr->fr", half_sum, basis[index // 2], precision=highest)
+        projected.append(partial + over_z(partial, 3))
+
+    powers = []
+    for layer in range(layers):
+        own = sum(
+            jnp.einsum("fd,fr->dr", summed[2 * layer + j], projected[2 * layer + j], precision=highest)
+            for j in range(2)
+        )
+        powers.append(sum_power(own, z, y, core))
+
+    mine = jnp.stack([jnp.where(z < 2, projected[2 * l], projected[2 * l + 1]) for l in range(layers)])
+    reduced = scale_factor * mine
+    moment_one, moment_two, direction = adam_direction(reduced, first_moment, second_moment)
+    factor = learn_rate * galore_scale * scale_factor
+    far = over_z(direction, 3)
+    parts = ((0, direction), (1, over_z(direction, 1)), (3, far), (2, over_z(far, 1)))
+    directions = jnp.zeros((layers, 4 * rows, direction.shape[2]), jnp.float32)
+    for k, part in parts:
+        directions = lax.dynamic_update_slice_in_dim(directions, part, (z ^ k) * rows, 1)
+    update = jnp.einsum("lfr,ldr->lfd", directions, basis, precision=highest)
+    weights_next = (weights.astype(jnp.float32) - factor * update).astype(jnp.bfloat16)
+
+    basis_next = jnp.concatenate([newton_schulz(power[None], width) for power in powers])
     return (weights_next, basis_next, moment_one, moment_two)
 
 
 def solution(mesh):
+    line = mesh.shape["shard"] == 4 and mesh.shape["tensor"] == 4
     return jax.shard_map(
-        body,
+        line_body if line else general_body,
         mesh=mesh,
         in_specs=(
             P("shard", "section", "tensor", None),

time: 263 us -> 144 us (0.55)
  waiting for transfers between devices: 215 us -> 33.2 us
  starting transfers between devices: 0.3 us -> 62.7 us
  matrix products: 21.9 us -> 34.7 us
  between operations: 13.9 us -> 2.56 us
    psum x1 -> x0, waiting for transfers between devices: 92.2 us -> none  [body(): whole = lax.psum(power, ('shard', 'tensor'))]
    reduce_scatter x1 -> x0, waiting for transfers between devices: 88.1 us -> none  [body(): lax.psum_scatter(local_grads.astype(jnp.float32), 'shard', scatter_dimens...]
    ppermute x0 -> x31, starting transfers between devices: none -> 62.7 us  [the longest x23 56.4 us: over_z(): return lax.ppermute(x, 'shard', xor_pairs(k))]
    all_gather x1 -> x0, waiting for transfers between devices: 35.1 us -> none  [body(): weights_next = lax.all_gather(fresh_rows, 'shard', axis=1, tiled=True)]
    ppermute x0 -> x31, waiting for transfers between devices: none -> 33.2 us  [the longest x23 33.1 us: over_z(): return lax.ppermute(x, 'shard', xor_pairs(k))]
    dot_general x6 -> x15, matrix products: 14 us -> 27.4 us  [the longest x6 9.08 us: newton_schulz(): jnp.einsum('ldr,lds->lrs', iterate, iterate, precision=highest)]
    unnamed x16 -> x10, local copies, waits for them, and re-layouts: 4.91 us -> 0.34 us
    convert_element_type x1 -> x0, other arithmetic: 4.27 us -> none  [body(): local_grads.astype(jnp.float32)]
  transfers between devices with their start and end apart: 3 -> 31, of which waited for: 3 -> 9; matrix products, arithmetic and copies ran while one was open for 8% -> 21% of each run, Pallas kernels for 0% -> 0%
where the time goes in v1:
time: 144 us
  starting transfers between devices  62.7 us (44%)
  matrix products  34.7 us (24%)
  waiting for transfers between devices  33.2 us (23%)
  local copies, waits for them, and re-layouts  6.43 us (4%)
  other arithmetic  4.34 us (3%)
  between operations  2.56 us (2%)
    ppermute x23, starting transfers between devices, over_z(): return lax.ppermute(x, 'shard', xor_pairs(k))  56.4 us
    ppermute x23, waiting for transfers between devices, over_z(): return lax.ppermute(x, 'shard', xor_pairs(k))  33.1 us
    dot_general x6, matrix products, newton_schulz(): jnp.einsum('ldr,lds->lrs', iterate, iterate, precision=highest)  9.08 us
    dot_general x4, matrix products, line_body(): jnp.einsum('fd,fr->dr', summed[2 * layer + j], projected[2 * layer + j],...  7.79 us
    dot_general x1, matrix products, line_body(): update = jnp.einsum('lfr,ldr->lfd', directions, basis, precision=highest)  5.66 us
    ppermute x4, starting transfers between devices, over_y(): return lax.ppermute(x, 'tensor', xor_pairs(2))  5.26 us
    dot_general x6, matrix products, newton_step(): jnp.einsum('ldr,lrs->lds', iterate, mixing, precision=highest)  4.99 us
    dot_general x4, matrix products, line_body(): jnp.einsum('fd,dr->fr', half_sum, basis[index // 2], precision=highest)  4.86 us
  transfers between devices with their start and end apart: 31, of which 9 were waited for; matrix products, arithmetic and copies ran while one was open for 21% of the time, Pallas kernels for 0%

profile of v1, /device:TPU:0, one launch (start us, length us, event | category | flops | bytes accessed | tf_op | source)
XLA Modules:
  0.0 143.8 jit_solution(1179502396715175542)
XLA Ops:
  0.6 2.8 %fusion.76 = (bf16[1,1,768,768]{3,2,1,0:T(8,128)(2,1)}, bf16[1,1,768,768]{3,2,1,0:T(8,128)(2,1)S(1)}) fusion(bf16[1,2,768,768]{3,2,1,0:T(8,128)(2,1)} %param.5), kind=kLoop, calls=%fused_computation.132 | loop fusion | bytes 4718592 | tf_op jit(solution)/shard_map/slice | solution.py:121
  3.4 2.0 %dynamic-slice_bitcast_fusion.3 = (bf16[192,768]{1,0:T(8,128)(2,1)}, bf16[192,768]{1,0:T(8,128)(2,1)}) fusion(bf16[1,1,768,768]{3,2,1,0:T(8,128)(2,1)} %get-tuple-element.12, s32[]{:T(128)S(6)} %select_n.182, s32[]{:T(128)S(6)} %select_n.186), kind=kLoop, calls=%fused_computation.75 | loop fusion | bytes 1179656 | tf_op jit(solution)/shard_map/dynamic_slice | solution.py:121
  5.5 3.0 %collective-permute-start.2 = (bf16[192,768]{1,0:T(8,128)(2,1)}, bf16[192,768]{1,0:T(8,128)(2,1)}, u32[]{:S(2)}, u32[]{:S(2)}) collective-permute-start(bf16[192,768]{1,0:T(8,128)(2,1)} %get-tuple-element.15), channel_id=1, source_target_pairs={{0,8},{8,0},{16,24},{24,16},{1,9},{9,1},{17,25},{25,17},{2,10},{10... | collective-permute-start | bytes 884744 | tf_op jit(solution)/shard_map/ppermute | solution.py:73
  8.5 0.8 dynamic-slice_bitcast_fusion.1
  9.4 2.0 %collective-permute-start.6 = (bf16[192,768]{1,0:T(8,128)(2,1)}, bf16[192,768]{1,0:T(8,128)(2,1)S(1)}, u32[]{:S(2)}, u32[]{:S(2)}) collective-permute-start(bf16[192,768]{1,0:T(8,128)(2,1)} %get-tuple-element.17), channel_id=1, source_target_pairs={{0,8},{8,0},{16,24},{24,16},{1,9},{9,1},{17,25},{25,17},{2,10},{10... | collective-permute-start | bytes 884744 | tf_op jit(solution)/shard_map/ppermute | solution.py:73
  11.4 5.2 %collective-permute-done.2 = bf16[192,768]{1,0:T(8,128)(2,1)} collective-permute-done((bf16[192,768]{1,0:T(8,128)(2,1)}, bf16[192,768]{1,0:T(8,128)(2,1)}, u32[]{:S(2)}, u32[]{:S(2)}) %collective-permute-start.2) | collective-permute-done | bytes 294944 | tf_op jit(solution)/shard_map/ppermute | solution.py:73
  16.6 1.8 %fusion.20 = f32[192,256]{1,0:T(8,128)S(1)} fusion(f32[2,768,256]{2,1,0:T(8,128)S(1)} %copy-done, bf16[192,768]{1,0:T(8,128)(2,1)} %collective-permute-done.2, bf16[1,1,768,768]{3,2,1,0:T(8,128)(2,1)} %get-tuple-element.12, s32[]{:T(128)S(6)} %select_n.184), kind=kOutput, calls=%fused_computation.38 | convolution fusion | flops 453427200 | bytes 1572868 | tf_op jit(solution)/shard_map/fd,dr->fr/dot_general | solution.py:131
  18.4 4.2 %collective-permute-start.3 = (f32[192,256]{1,0:T(8,128)S(1)}, f32[192,256]{1,0:T(8,128)S(1)}, u32[]{:S(2)}, u32[]{:S(2)}) collective-permute-start(f32[192,256]{1,0:T(8,128)S(1)} %fusion.20), channel_id=1, source_target_pairs={{0,24},{8,16},{16,8},{24,0},{1,25},{9,17},{17,9},{25,1},{2,26},{10... | collective-permute-start | bytes 589832 | tf_op jit(solution)/shard_map/ppermute | solution.py:73
  23.0 1.7 %fusion.22 = f32[192,256]{1,0:T(8,128)S(1)} fusion(f32[2,768,256]{2,1,0:T(8,128)S(1)} %copy-done, bf16[192,768]{1,0:T(8,128)(2,1)} %collective-permute-done, bf16[1,1,768,768]{3,2,1,0:T(8,128)(2,1)S(1)} %copy-done.1, s32[]{:T(128)S(6)} %select_n.180), kind=kOutput, calls=%fused_computation.40 | convolution fusion | flops 453427200 | bytes 1572868 | tf_op jit(solution)/shard_map/fd,dr->fr/dot_general | solution.py:131
  24.6 4.2 %collective-permute-start.1 = (f32[192,256]{1,0:T(8,128)S(1)}, f32[192,256]{1,0:T(8,128)S(1)}, u32[]{:S(2)}, u32[]{:S(2)}) collective-permute-start(f32[192,256]{1,0:T(8,128)S(1)} %fusion.22), channel_id=1, source_target_pairs={{0,24},{8,16},{16,8},{24,0},{1,25},{9,17},{17,9},{25,1},{2,26},{10... | collective-permute-start | bytes 589832 | tf_op jit(solution)/shard_map/ppermute | solution.py:73
  29.9 4.2 %collective-permute-start.7 = (f32[192,256]{1,0:T(8,128)S(1)}, f32[192,256]{1,0:T(8,128)S(1)}, u32[]{:S(2)}, u32[]{:S(2)}) collective-permute-start(f32[192,256]{1,0:T(8,128)S(1)} %fusion.16), channel_id=1, source_target_pairs={{0,24},{8,16},{16,8},{24,0},{1,25},{9,17},{17,9},{25,1},{2,26},{10... | collective-permute-start | bytes 589832 | tf_op jit(solution)/shard_map/ppermute | solution.py:73
  34.0 1.1 collective-permute-done.4
  35.9 18.1 %collective-permute-start.5 = (f32[192,256]{1,0:T(8,128)S(1)}, f32[192,256]{1,0:T(8,128)S(1)}, u32[]{:S(2)}, u32[]{:S(2)}) collective-permute-start(f32[192,256]{1,0:T(8,128)S(1)} %fusion.18), channel_id=1, source_target_pairs={{0,24},{8,16},{16,8},{24,0},{1,25},{9,17},{17,9},{25,1},{2,26},{10... | collective-permute-start | bytes 589832 | tf_op jit(solution)/shard_map/ppermute | solution.py:73
  54.0 2.4 %fusion.28 = f32[768,256]{1,0:T(8,128)S(1)} fusion(bf16[192,768]{1,0:T(8,128)(2,1)} %collective-permute-done.2, bf16[1,1,768,768]{3,2,1,0:T(8,128)(2,1)S(1)} %copy-done.1, s32[]{:T(128)S(6)} %select_n.184, f32[192,256]{1,0:T(8,128)S(1)} %fusion.20, f32[192,256]{1,0:T(8,128)S(1)} %collective-permute-done.3), kind=kOutput, calls=%fused_computation.52 | convolution fusion | flops 453476352 | bytes 1769476 | tf_op jit(solution)/shard_map/fd,fr->dr/dot_general | solution.py:137
  56.4 2.4 %convolution_add_fusion.1 = f32[768,256]{1,0:T(8,128)S(1)} fusion(f32[768,256]{1,0:T(8,128)S(1)} %fusion.28, bf16[192,768]{1,0:T(8,128)(2,1)} %collective-permute-done, bf16[1,1,768,768]{3,2,1,0:T(8,128)(2,1)S(1)} %copy-done.1, s32[]{:T(128)S(6)} %select_n.180, f32[192,256]{1,0:T(8,128)S(1)} %fusion.22, f32[192,256]{1,0:T(8,128)S(1)} %collective-permute-done.1), kind=kOutput, calls=%fused_computation.3 | convolution fusion | flops 453672960 | bytes 2555908 | tf_op jit(solution)/shard_map/fd,fr->dr/dot_general | solution.py:137
  59.0 1.5 %fusion.29 = f32[768,256]{1,0:T(8,128)S(1)} fusion(bf16[192,768]{1,0:T(8,128)(2,1)S(1)} %collective-permute-done.6, bf16[1,1,768,768]{3,2,1,0:T(8,128)(2,1)S(1)} %get-tuple-element.13, s32[]{:T(128)S(6)} %select_n.184, f32[192,256]{1,0:T(8,128)S(1)} %fusion.16, f32[192,256]{1,0:T(8,128)S(1)} %collective-permute-done.7), kind=kOutput, calls=%fused_computation.53 | convolution fusion | flops 453476352 | bytes 1769476 | tf_op jit(solution)/shard_map/fd,fr->dr/dot_general | solution.py:137
  60.5 1.5 %convolution_add_fusion = f32[768,256]{1,0:T(8,128)S(1)} fusion(f32[768,256]{1,0:T(8,128)S(1)} %fusion.29, bf16[192,768]{1,0:T(8,128)(2,1)S(1)} %collective-permute-done.4, bf16[1,1,768,768]{3,2,1,0:T(8,128)(2,1)S(1)} %get-tuple-element.13, s32[]{:T(128)S(6)} %select_n.180, f32[192,256]{1,0:T(8,128)S(1)} %fusion.18, f32[192,256]{1,0:T(8,128)S(1)} %collective-permute-done.5), kind=kOutput, calls=%fused_computation.2 | convolution fusion | flops 453672960 | bytes 2555908 | tf_op jit(solution)/shard_map/fd,fr->dr/dot_general | solution.py:137
  63.1 1.1 constant_dynamic-update-slice_fusion.11
  64.2 1.0 collective-permute-start.9
  65.3 1.6 %collective-permute-start.12 = (f32[192,256]{1,0:T(8,128)S(1)}, f32[192,256]{1,0:T(8,128)S(1)}, u32[]{:S(2)}, u32[]{:S(2)}) collective-permute-start(f32[192,256]{1,0:T(8,128)S(1)} %constant_dynamic-slice_fusion.8), channel_id=1, source_target_pairs={{0,4},{2,6},{4,0},{6,2},{1,5},{3,7},{5,1},{7,3},{8,12},{10,14},{12... | collective-permute-start | bytes 589832 | tf_op jit(solution)/shard_map/ppermute | solution.py:81
  67.5 15.3 %collective-permute-done.9 = f32[2,192,256]{2,1,0:T(8,128)S(1)} collective-permute-done((f32[2,192,256]{2,1,0:T(8,128)S(1)}, f32[2,192,256]{2,1,0:T(8,128)S(1)}, u32[]{:S(2)}, u32[]{:S(2)}) %collective-permute-start.9) | collective-permute-done | bytes 393248 | tf_op jit(solution)/shard_map/ppermute | solution.py:73
  82.8 3.1 %collective-permute-start.10 = (f32[2,192,256]{2,1,0:T(8,128)S(1)}, f32[2,192,256]{2,1,0:T(8,128)S(1)}, u32[]{:S(2)}, u32[]{:S(2)}) collective-permute-start(f32[2,192,256]{2,1,0:T(8,128)S(1)} %collective-permute-done.9), channel_id=1, source_target_pairs={{0,8},{8,0},{16,24},{24,16},{1,9},{9,1},{17,25},{25,17},{2,10},{10... | collective-permute-start | bytes 1179656 | tf_op jit(solution)/shard_map/ppermute | solution.py:73
  86.1 1.2 collective-permute-start.13
  87.6 2.9 %collective-permute-start.15 = (f32[48,256]{1,0:T(8,128)S(1)}, f32[48,256]{1,0:T(8,128)S(1)}, u32[]{:S(2)}, u32[]{:S(2)}) collective-permute-start(f32[48,256]{1,0:T(8,128)S(1)} %get-tuple-element.19), channel_id=1, source_target_pairs={{0,8},{8,0},{16,24},{24,16},{1,9},{9,1},{17,25},{25,17},{2,10},{10... | collective-permute-start | bytes 147464 | tf_op jit(solution)/shard_map/ppermute | solution.py:73
  90.6 1.2 collective-permute-start.23
  91.8 6.4 %collective-permute-done.13 = f32[48,256]{1,0:T(8,128)S(1)} collective-permute-done((f32[48,256]{1,0:T(8,128)S(1)}, f32[48,256]{1,0:T(8,128)S(1)}, u32[]{:S(2)}, u32[]{:S(2)}) %collective-permute-start.13) | collective-permute-done | bytes 49184 | tf_op jit(solution)/shard_map/ppermute | solution.py:73
  98.2 3.2 %collective-permute-start.25 = (f32[48,256]{1,0:T(8,128)S(1)}, f32[48,256]{1,0:T(8,128)S(1)}, u32[]{:S(2)}, u32[]{:S(2)}) collective-permute-start(f32[48,256]{1,0:T(8,128)S(1)} %get-tuple-element.22), channel_id=1, source_target_pairs={{0,8},{8,0},{16,24},{24,16},{1,9},{9,1},{17,25},{25,17},{2,10},{10... | collective-permute-start | bytes 147464 | tf_op jit(solution)/shard_map/ppermute | solution.py:73
  101.6 1.7 %collective-permute-start.17 = (f32[48,256]{1,0:T(8,128)S(1)}, f32[48,256]{1,0:T(8,128)S(1)}, u32[]{:S(2)}, u32[]{:S(2)}) collective-permute-start(f32[48,256]{1,0:T(8,128)S(1)} %get-tuple-element.5), channel_id=1, source_target_pairs={{0,16},{8,24},{16,0},{24,8},{1,17},{9,25},{17,1},{25,9},{2,18},{10... | collective-permute-start | bytes 147464 | tf_op jit(solution)/shard_map/ppermute | solution.py:73
  103.3 1.5 %collective-permute-done.24 = f32[48,256]{1,0:T(8,128)S(1)} collective-permute-done((f32[48,256]{1,0:T(8,128)S(1)}, f32[48,256]{1,0:T(8,128)S(1)}, u32[]{:S(2)}, u32[]{:S(2)}) %collective-permute-start.24) | collective-permute-done | bytes 49184 | tf_op jit(solution)/shard_map/ppermute | solution.py:73
  104.8 1.6 %collective-permute-start.18 = (f32[48,256]{1,0:T(8,128)S(1)}, f32[48,256]{1,0:T(8,128)S(1)}, u32[]{:S(2)}, u32[]{:S(2)}) collective-permute-start(f32[48,256]{1,0:T(8,128)S(1)} %get-tuple-element.5), channel_id=1, source_target_pairs={{0,24},{8,16},{16,8},{24,0},{1,25},{9,17},{17,9},{25,1},{2,26},{10... | collective-permute-start | bytes 147464 | tf_op jit(solution)/shard_map/ppermute | solution.py:73
  106.6 2.7 %collective-permute-start.27 = (f32[48,256]{1,0:T(8,128)S(1)}, f32[48,256]{1,0:T(8,128)S(1)}, u32[]{:S(2)}, u32[]{:S(2)}) collective-permute-start(f32[48,256]{1,0:T(8,128)S(1)} %get-tuple-element.7), channel_id=1, source_target_pairs={{0,16},{8,24},{16,0},{24,8},{1,17},{9,25},{17,1},{25,9},{2,18},{10... | collective-permute-start | bytes 147464 | tf_op jit(solution)/shard_map/ppermute | solution.py:73
  109.3 1.6 %collective-permute-start.28 = (f32[48,256]{1,0:T(8,128)S(1)}, f32[48,256]{1,0:T(8,128)S(1)}, u32[]{:S(2)}, u32[]{:S(2)}) collective-permute-start(f32[48,256]{1,0:T(8,128)S(1)} %get-tuple-element.7), channel_id=1, source_target_pairs={{0,24},{8,16},{16,8},{24,0},{1,25},{9,17},{17,9},{25,1},{2,26},{10... | collective-permute-start | bytes 147464 | tf_op jit(solution)/shard_map/ppermute | solution.py:73
  111.0 1.6 %collective-permute-start.19 = (f32[192,256]{1,0:T(8,128)S(1)}, f32[192,256]{1,0:T(8,128)S(1)}, u32[]{:S(2)}, u32[]{:S(2)}) collective-permute-start(f32[192,256]{1,0:T(8,128)S(1)} %constant_dynamic-update-slice_fusion.4), channel_id=1, source_target_pairs={{0,4},{2,6},{4,0},{6,2},{1,5},{3,7},{5,1},{7,3},{8,12},{10,14},{12... | collective-permute-start | bytes 589832 | tf_op jit(solution)/shard_map/ppermute | solution.py:81
  112.6 2.7 %collective-permute-done.28 = f32[48,256]{1,0:T(8,128)S(1)} collective-permute-done((f32[48,256]{1,0:T(8,128)S(1)}, f32[48,256]{1,0:T(8,128)S(1)}, u32[]{:S(2)}, u32[]{:S(2)}) %collective-permute-start.28) | collective-permute-done | bytes 49184 | tf_op jit(solution)/shard_map/ppermute | solution.py:73
  115.3 1.5 %collective-permute-start.29 = (f32[192,256]{1,0:T(8,128)S(1)}, f32[192,256]{1,0:T(8,128)S(1)}, u32[]{:S(2)}, u32[]{:S(2)}) collective-permute-start(f32[192,256]{1,0:T(8,128)S(1)} %constant_dynamic-update-slice_fusion), channel_id=1, source_target_pairs={{0,4},{2,6},{4,0},{6,2},{1,5},{3,7},{5,1},{7,3},{8,12},{10,14},{12... | collective-permute-start | bytes 589832 | tf_op jit(solution)/shard_map/ppermute | solution.py:81
  117.0 5.7 %subtract_convert_fusion = bf16[2,768,768]{2,1,0:T(8,128)(2,1)} fusion(bf16[2,768,768]{2,1,0:T(8,128)(2,1)S(1)} %copy-done.2, f32[2,768,256]{2,1,0:T(8,128)S(1)} %constant_dynamic-update-slice_fusion.8, f32[2,768,256]{2,1,0:T(8,128)S(1)} %copy-done), kind=kOutput, calls=%fused_computation | convolution fusion | flops 3628597248 | bytes 7864320 | tf_op jit(solution)/shard_map/lfr,ldr->lfd/dot_general | solution.py:151
  123.0 0.8 fusion.12
  124.5 1.4 fusion.73
  127.2 1.6 %fusion.30 = f32[256,256]{1,0:T(8,128)S(1)} fusion(f32[768,256]{1,0:T(8,128)S(1)} %fusion.71, f32[384,256]{1,0:T(8,128)S(1)} %collective-permute-done.20, f32[384,256]{1,0:T(8,128)S(1)} %maximum_select_fusion.4, f32[]{:T(128)S(6)} %add.236, pred[]{:T(512)S(6)} %eq.18), kind=kOutput, calls=%fused_computation.62 | convolution fusion | flops 605159424 | bytes 1835013 | tf_op jit(solution)/shard_map/ldr,lds->lrs/dot_general | solution.py:40
  129.1 0.9 convolution_add_fusion.5
  130.1 1.4 fusion.77
  132.7 0.8 fusion.15
  134.2 1.4 fusion.67
  136.0 0.8 fusion.65
  136.8 1.8 %fusion.31 = f32[256,256]{1,0:T(8,128)S(1)} fusion(f32[768,256]{1,0:T(8,128)S(1)} %fusion.65, f32[384,256]{1,0:T(8,128)S(1)} %collective-permute-done.30, f32[384,256]{1,0:T(8,128)S(1)} %maximum_select_fusion.5, f32[]{:T(128)S(6)} %add.249, pred[]{:T(512)S(6)} %eq.18), kind=kOutput, calls=%fused_computation.63 | convolution fusion | flops 605159424 | bytes 1835013 | tf_op jit(solution)/shard_map/ldr,lds->lrs/dot_general | solution.py:40
  139.0 0.9 convolution_add_fusion.3
  139.9 1.4 fusion.78
  142.5 1.2 pad_maximum_fusion
  (86 shorter events, 10.3 us)
Async XLA Ops:
  3.4 13.2 %copy-start = (f32[2,768,256]{2,1,0:T(8,128)S(1)}, f32[2,768,256]{2,1,0:T(8,128)}, u32[]{:S(2)}) copy-start(f32[2,768,256]{2,1,0:T(8,128)} %param.7) | copy-start | bytes 4718596
  5.5 11.2 %collective-permute-start.2 = (bf16[192,768]{1,0:T(8,128)(2,1)}, bf16[192,768]{1,0:T(8,128)(2,1)}, u32[]{:S(2)}, u32[]{:S(2)}) collective-permute-start(bf16[192,768]{1,0:T(8,128)(2,1)} %get-tuple-element.15), channel_id=1, source_target_pairs={{0,8},{8,0},{16,24},{24,16},{1,9},{9,1},{17,25},{25,17},{2,10},{10... | collective-permute-start | bytes 884744 | tf_op jit(solution)/shard_map/ppermute | solution.py:73
  8.5 14.5 %collective-permute-start = (bf16[192,768]{1,0:T(8,128)(2,1)}, bf16[192,768]{1,0:T(8,128)(2,1)}, u32[]{:S(2)}, u32[]{:S(2)}) collective-permute-start(bf16[192,768]{1,0:T(8,128)(2,1)} %get-tuple-element.14), channel_id=1, source_target_pairs={{0,8},{8,0},{16,24},{24,16},{1,9},{9,1},{17,25},{25,17},{2,10},{10... | collective-permute-start | bytes 884744 | tf_op jit(solution)/shard_map/ppermute | solution.py:73
  9.4 19.8 %collective-permute-start.6 = (bf16[192,768]{1,0:T(8,128)(2,1)}, bf16[192,768]{1,0:T(8,128)(2,1)S(1)}, u32[]{:S(2)}, u32[]{:S(2)}) collective-permute-start(bf16[192,768]{1,0:T(8,128)(2,1)} %get-tuple-element.17), channel_id=1, source_target_pairs={{0,8},{8,0},{16,24},{24,16},{1,9},{9,1},{17,25},{25,17},{2,10},{10... | collective-permute-start | bytes 884744 | tf_op jit(solution)/shard_map/ppermute | solution.py:73
  11.4 23.8 %collective-permute-start.4 = (bf16[192,768]{1,0:T(8,128)(2,1)}, bf16[192,768]{1,0:T(8,128)(2,1)S(1)}, u32[]{:S(2)}, u32[]{:S(2)}) collective-permute-start(bf16[192,768]{1,0:T(8,128)(2,1)} %get-tuple-element.16), channel_id=1, source_target_pairs={{0,8},{8,0},{16,24},{24,16},{1,9},{9,1},{17,25},{25,17},{2,10},{10... | collective-permute-start | bytes 884744 | tf_op jit(solution)/shard_map/ppermute | solution.py:73
  11.4 11.5 %copy-start.1 = (bf16[1,1,768,768]{3,2,1,0:T(8,128)(2,1)S(1)}, bf16[1,1,768,768]{3,2,1,0:T(8,128)(2,1)}, u32[]{:S(2)}) copy-start(bf16[1,1,768,768]{3,2,1,0:T(8,128)(2,1)} %get-tuple-element.12) | copy-start | bytes 3538948
  18.4 35.6 %collective-permute-start.3 = (f32[192,256]{1,0:T(8,128)S(1)}, f32[192,256]{1,0:T(8,128)S(1)}, u32[]{:S(2)}, u32[]{:S(2)}) collective-permute-start(f32[192,256]{1,0:T(8,128)S(1)} %fusion.20), channel_id=1, source_target_pairs={{0,24},{8,16},{16,8},{24,0},{1,25},{9,17},{17,9},{25,1},{2,26},{10... | collective-permute-start | bytes 589832 | tf_op jit(solution)/shard_map/ppermute | solution.py:73
  24.6 31.8 %collective-permute-start.1 = (f32[192,256]{1,0:T(8,128)S(1)}, f32[192,256]{1,0:T(8,128)S(1)}, u32[]{:S(2)}, u32[]{:S(2)}) collective-permute-start(f32[192,256]{1,0:T(8,128)S(1)} %fusion.22), channel_id=1, source_target_pairs={{0,24},{8,16},{16,8},{24,0},{1,25},{9,17},{17,9},{25,1},{2,26},{10... | collective-permute-start | bytes 589832 | tf_op jit(solution)/shard_map/ppermute | solution.py:73
  29.9 29.1 %collective-permute-start.7 = (f32[192,256]{1,0:T(8,128)S(1)}, f32[192,256]{1,0:T(8,128)S(1)}, u32[]{:S(2)}, u32[]{:S(2)}) collective-permute-start(f32[192,256]{1,0:T(8,128)S(1)} %fusion.16), channel_id=1, source_target_pairs={{0,24},{8,16},{16,8},{24,0},{1,25},{9,17},{17,9},{25,1},{2,26},{10... | collective-permute-start | bytes 589832 | tf_op jit(solution)/shard_map/ppermute | solution.py:73
  35.9 24.6 %collective-permute-start.5 = (f32[192,256]{1,0:T(8,128)S(1)}, f32[192,256]{1,0:T(8,128)S(1)}, u32[]{:S(2)}, u32[]{:S(2)}) collective-permute-start(f32[192,256]{1,0:T(8,128)S(1)} %fusion.18), channel_id=1, source_target_pairs={{0,24},{8,16},{16,8},{24,0},{1,25},{9,17},{17,9},{25,1},{2,26},{10... | collective-permute-start | bytes 589832 | tf_op jit(solution)/shard_map/ppermute | solution.py:73
  58.9 6.3 %collective-permute-start.11 = (f32[384,256]{1,0:T(8,128)S(1)}, f32[384,256]{1,0:T(8,128)S(1)}, u32[]{:S(2)}, u32[]{:S(2)}) collective-permute-start(f32[384,256]{1,0:T(8,128)S(1)} %constant_dynamic-slice_fusion.9), channel_id=1, source_target_pairs={{0,2},{2,0},{4,6},{6,4},{1,3},{3,1},{5,7},{7,5},{8,10},{10,8},{12,... | collective-permute-start | bytes 1179656 | tf_op jit(solution)/shard_map/ppermute | solution.py:77
  62.0 1.0 copy-start.3
  62.0 1.1 copy-start.4
  62.0 4.8 %collective-permute-start.21 = (f32[384,256]{1,0:T(8,128)S(1)}, f32[384,256]{1,0:T(8,128)S(1)}, u32[]{:S(2)}, u32[]{:S(2)}) collective-permute-start(f32[384,256]{1,0:T(8,128)S(1)} %constant_dynamic-slice_fusion.4), channel_id=1, source_target_pairs={{0,2},{2,0},{4,6},{6,4},{1,3},{3,1},{5,7},{7,5},{8,10},{10,8},{12,... | collective-permute-start | bytes 1179656 | tf_op jit(solution)/shard_map/ppermute | solution.py:77
  64.2 21.7 %collective-permute-start.8 = (f32[2,192,256]{2,1,0:T(8,128)S(1)}, f32[2,192,256]{2,1,0:T(8,128)S(1)}, u32[]{:S(2)}, u32[]{:S(2)}) collective-permute-start(f32[2,192,256]{2,1,0:T(8,128)S(1)} %get-tuple-element.9), channel_id=1, source_target_pairs={{0,8},{8,0},{16,24},{24,16},{1,9},{9,1},{17,25},{25,17},{2,10},{10... | collective-permute-start | bytes 1179656 | tf_op jit(solution)/shard_map/ppermute | solution.py:73
  64.2 18.6 %collective-permute-start.9 = (f32[2,192,256]{2,1,0:T(8,128)S(1)}, f32[2,192,256]{2,1,0:T(8,128)S(1)}, u32[]{:S(2)}, u32[]{:S(2)}) collective-permute-start(f32[2,192,256]{2,1,0:T(8,128)S(1)} %get-tuple-element.9), channel_id=1, source_target_pairs={{0,24},{8,16},{16,8},{24,0},{1,25},{9,17},{17,9},{25,1},{2,26},{10... | collective-permute-start | bytes 1179656 | tf_op jit(solution)/shard_map/ppermute | solution.py:73
  65.3 20.7 %collective-permute-start.12 = (f32[192,256]{1,0:T(8,128)S(1)}, f32[192,256]{1,0:T(8,128)S(1)}, u32[]{:S(2)}, u32[]{:S(2)}) collective-permute-start(f32[192,256]{1,0:T(8,128)S(1)} %constant_dynamic-slice_fusion.8), channel_id=1, source_target_pairs={{0,4},{2,6},{4,0},{6,2},{1,5},{3,7},{5,1},{7,3},{8,12},{10,14},{12... | collective-permute-start | bytes 589832 | tf_op jit(solution)/shard_map/ppermute | solution.py:81
  66.9 23.6 %collective-permute-start.22 = (f32[192,256]{1,0:T(8,128)S(1)}, f32[192,256]{1,0:T(8,128)S(1)}, u32[]{:S(2)}, u32[]{:S(2)}) collective-permute-start(f32[192,256]{1,0:T(8,128)S(1)} %constant_dynamic-slice_fusion.3), channel_id=1, source_target_pairs={{0,4},{2,6},{4,0},{6,2},{1,5},{3,7},{5,1},{7,3},{8,12},{10,14},{12... | collective-permute-start | bytes 589832 | tf_op jit(solution)/shard_map/ppermute | solution.py:81
  82.8 34.0 %collective-permute-start.10 = (f32[2,192,256]{2,1,0:T(8,128)S(1)}, f32[2,192,256]{2,1,0:T(8,128)S(1)}, u32[]{:S(2)}, u32[]{:S(2)}) collective-permute-start(f32[2,192,256]{2,1,0:T(8,128)S(1)} %collective-permute-done.9), channel_id=1, source_target_pairs={{0,8},{8,0},{16,24},{24,16},{1,9},{9,1},{17,25},{25,17},{2,10},{10... | collective-permute-start | bytes 1179656 | tf_op jit(solution)/shard_map/ppermute | solution.py:73
  86.1 12.1 %collective-permute-start.13 = (f32[48,256]{1,0:T(8,128)S(1)}, f32[48,256]{1,0:T(8,128)S(1)}, u32[]{:S(2)}, u32[]{:S(2)}) collective-permute-start(f32[48,256]{1,0:T(8,128)S(1)} %get-tuple-element.18), channel_id=1, source_target_pairs={{0,24},{8,16},{16,8},{24,0},{1,25},{9,17},{17,9},{25,1},{2,26},{10... | collective-permute-start | bytes 147464 | tf_op jit(solution)/shard_map/ppermute | solution.py:73
  87.3 10.9 %collective-permute-start.14 = (f32[48,256]{1,0:T(8,128)S(1)}, f32[48,256]{1,0:T(8,128)S(1)}, u32[]{:S(2)}, u32[]{:S(2)}) collective-permute-start(f32[48,256]{1,0:T(8,128)S(1)} %get-tuple-element.20), channel_id=1, source_target_pairs={{0,16},{8,24},{16,0},{24,8},{1,17},{9,25},{17,1},{25,9},{2,18},{10... | collective-permute-start | bytes 147464 | tf_op jit(solution)/shard_map/ppermute | solution.py:73
  87.6 13.8 %collective-permute-start.15 = (f32[48,256]{1,0:T(8,128)S(1)}, f32[48,256]{1,0:T(8,128)S(1)}, u32[]{:S(2)}, u32[]{:S(2)}) collective-permute-start(f32[48,256]{1,0:T(8,128)S(1)} %get-tuple-element.19), channel_id=1, source_target_pairs={{0,8},{8,0},{16,24},{24,16},{1,9},{9,1},{17,25},{25,17},{2,10},{10... | collective-permute-start | bytes 147464 | tf_op jit(solution)/shard_map/ppermute | solution.py:73
  90.6 11.0 %collective-permute-start.23 = (f32[48,256]{1,0:T(8,128)S(1)}, f32[48,256]{1,0:T(8,128)S(1)}, u32[]{:S(2)}, u32[]{:S(2)}) collective-permute-start(f32[48,256]{1,0:T(8,128)S(1)} %get-tuple-element.21), channel_id=1, source_target_pairs={{0,24},{8,16},{16,8},{24,0},{1,25},{9,17},{17,9},{25,1},{2,26},{10... | collective-permute-start | bytes 147464 | tf_op jit(solution)/shard_map/ppermute | solution.py:73
  98.2 6.6 %collective-permute-start.24 = (f32[48,256]{1,0:T(8,128)S(1)}, f32[48,256]{1,0:T(8,128)S(1)}, u32[]{:S(2)}, u32[]{:S(2)}) collective-permute-start(f32[48,256]{1,0:T(8,128)S(1)} %get-tuple-element.23), channel_id=1, source_target_pairs={{0,16},{8,24},{16,0},{24,8},{1,17},{9,25},{17,1},{25,9},{2,18},{10... | collective-permute-start | bytes 147464 | tf_op jit(solution)/shard_map/ppermute | solution.py:73
  98.2 18.8 %copy-start.2 = (bf16[2,768,768]{2,1,0:T(8,128)(2,1)S(1)}, bf16[2,768,768]{2,1,0:T(8,128)(2,1)}, u32[]{:S(2)}) copy-start(bf16[2,768,768]{2,1,0:T(8,128)(2,1)} %param.6) | copy-start | bytes 7077892
  98.2 8.1 %collective-permute-start.25 = (f32[48,256]{1,0:T(8,128)S(1)}, f32[48,256]{1,0:T(8,128)S(1)}, u32[]{:S(2)}, u32[]{:S(2)}) collective-permute-start(f32[48,256]{1,0:T(8,128)S(1)} %get-tuple-element.22), channel_id=1, source_target_pairs={{0,8},{8,0},{16,24},{24,16},{1,9},{9,1},{17,25},{25,17},{2,10},{10... | collective-permute-start | bytes 147464 | tf_op jit(solution)/shard_map/ppermute | solution.py:73
  101.5 5.2 %collective-permute-start.16 = (f32[48,256]{1,0:T(8,128)S(1)}, f32[48,256]{1,0:T(8,128)S(1)}, u32[]{:S(2)}, u32[]{:S(2)}) collective-permute-start(f32[48,256]{1,0:T(8,128)S(1)} %get-tuple-element.5), channel_id=1, source_target_pairs={{0,8},{8,0},{16,24},{24,16},{1,9},{9,1},{17,25},{25,17},{2,10},{10... | collective-permute-start | bytes 147464 | tf_op jit(solution)/shard_map/ppermute | solution.py:73
  101.6 7.8 %collective-permute-start.17 = (f32[48,256]{1,0:T(8,128)S(1)}, f32[48,256]{1,0:T(8,128)S(1)}, u32[]{:S(2)}, u32[]{:S(2)}) collective-permute-start(f32[48,256]{1,0:T(8,128)S(1)} %get-tuple-element.5), channel_id=1, source_target_pairs={{0,16},{8,24},{16,0},{24,8},{1,17},{9,25},{17,1},{25,9},{2,18},{10... | collective-permute-start | bytes 147464 | tf_op jit(solution)/shard_map/ppermute | solution.py:73
  104.8 6.2 %collective-permute-start.18 = (f32[48,256]{1,0:T(8,128)S(1)}, f32[48,256]{1,0:T(8,128)S(1)}, u32[]{:S(2)}, u32[]{:S(2)}) collective-permute-start(f32[48,256]{1,0:T(8,128)S(1)} %get-tuple-element.5), channel_id=1, source_target_pairs={{0,24},{8,16},{16,8},{24,0},{1,25},{9,17},{17,9},{25,1},{2,26},{10... | collective-permute-start | bytes 147464 | tf_op jit(solution)/shard_map/ppermute | solution.py:73
  106.4 6.2 %collective-permute-start.26 = (f32[48,256]{1,0:T(8,128)S(1)}, f32[48,256]{1,0:T(8,128)S(1)}, u32[]{:S(2)}, u32[]{:S(2)}) collective-permute-start(f32[48,256]{1,0:T(8,128)S(1)} %get-tuple-element.7), channel_id=1, source_target_pairs={{0,8},{8,0},{16,24},{24,16},{1,9},{9,1},{17,25},{25,17},{2,10},{10... | collective-permute-start | bytes 147464 | tf_op jit(solution)/shard_map/ppermute | solution.py:73
  106.6 6.0 %collective-permute-start.27 = (f32[48,256]{1,0:T(8,128)S(1)}, f32[48,256]{1,0:T(8,128)S(1)}, u32[]{:S(2)}, u32[]{:S(2)}) collective-permute-start(f32[48,256]{1,0:T(8,128)S(1)} %get-tuple-element.7), channel_id=1, source_target_pairs={{0,16},{8,24},{16,0},{24,8},{1,17},{9,25},{17,1},{25,9},{2,18},{10... | collective-permute-start | bytes 147464 | tf_op jit(solution)/shard_map/ppermute | solution.py:73
  109.3 6.0 %collective-permute-start.28 = (f32[48,256]{1,0:T(8,128)S(1)}, f32[48,256]{1,0:T(8,128)S(1)}, u32[]{:S(2)}, u32[]{:S(2)}) collective-permute-start(f32[48,256]{1,0:T(8,128)S(1)} %get-tuple-element.7), channel_id=1, source_target_pairs={{0,24},{8,16},{16,8},{24,0},{1,25},{9,17},{17,9},{25,1},{2,26},{10... | collective-permute-start | bytes 147464 | tf_op jit(solution)/shard_map/ppermute | solution.py:73
  111.0 5.9 %collective-permute-start.19 = (f32[192,256]{1,0:T(8,128)S(1)}, f32[192,256]{1,0:T(8,128)S(1)}, u32[]{:S(2)}, u32[]{:S(2)}) collective-permute-start(f32[192,256]{1,0:T(8,128)S(1)} %constant_dynamic-update-slice_fusion.4), channel_id=1, source_target_pairs={{0,4},{2,6},{4,0},{6,2},{1,5},{3,7},{5,1},{7,3},{8,12},{10,14},{12... | collective-permute-start | bytes 589832 | tf_op jit(solution)/shard_map/ppermute | solution.py:81
  115.3 7.4 %collective-permute-start.29 = (f32[192,256]{1,0:T(8,128)S(1)}, f32[192,256]{1,0:T(8,128)S(1)}, u32[]{:S(2)}, u32[]{:S(2)}) collective-permute-start(f32[192,256]{1,0:T(8,128)S(1)} %constant_dynamic-update-slice_fusion), channel_id=1, source_target_pairs={{0,4},{2,6},{4,0},{6,2},{1,5},{3,7},{5,1},{7,3},{8,12},{10,14},{12... | collective-permute-start | bytes 589832 | tf_op jit(solution)/shard_map/ppermute | solution.py:81
  116.9 6.1 %collective-permute-start.20 = (f32[384,256]{1,0:T(8,128)S(1)}, f32[384,256]{1,0:T(8,128)S(1)}, u32[]{:S(2)}, u32[]{:S(2)}) collective-permute-start(f32[384,256]{1,0:T(8,128)S(1)} %maximum_select_fusion.4), channel_id=1, source_target_pairs={{0,2},{2,0},{4,6},{6,4},{1,3},{3,1},{5,7},{7,5},{8,10},{10,8},{12,... | collective-permute-start | bytes 1179656 | tf_op jit(solution)/shard_map/ppermute | solution.py:77
  122.7 10.0 %collective-permute-start.30 = (f32[384,256]{1,0:T(8,128)S(1)}, f32[384,256]{1,0:T(8,128)S(1)}, u32[]{:S(2)}, u32[]{:S(2)}) collective-permute-start(f32[384,256]{1,0:T(8,128)S(1)} %maximum_select_fusion.5), channel_id=1, source_target_pairs={{0,2},{2,0},{4,6},{6,4},{1,3},{3,1},{5,7},{7,5},{8,10},{10,8},{12,... | collective-permute-start | bytes 1179656 | tf_op jit(solution)/shard_map/ppermute | solution.py:77

commit v2 on v0

--- a/solution.py
+++ b/solution.py
@@ -1,6 +1,10 @@
+import functools
+
 import jax
 import jax.numpy as jnp
 from jax import lax
+from jax.experimental import pallas as pl
+from jax.experimental.pallas import tpu as pltpu
 from jax.sharding import PartitionSpec as P
 
 NS_ITERS = 3
@@ -33,7 +37,16 @@
     return (moment_one, moment_two, corrected_one / (jnp.sqrt(corrected_two) + adam_eps))
 
 
-def body(grads, weights, basis, first_moment, second_moment):
+def newton_schulz(power, width):
+    norms = jnp.sqrt(jnp.sum(power * power, axis=(1, 2)))
+    iterate = power / (norms + norm_eps)[:, None, None]
+    for sweep in range(NS_ITERS):
+        gram_matrix = jnp.einsum("ldr,lds->lrs", iterate, iterate, precision=highest)
+        iterate = newton_step(iterate, gram_matrix)
+    return width**0.5 * iterate
+
+
+def general_body(grads, weights, basis, first_moment, second_moment):
     width = basis.shape[1]
     scale_factor = width ** (-0.5)
     local_grads = grads[0]
@@ -52,16 +65,416 @@
     fresh_rows = (current.astype(jnp.float32) - factor * update).astype(jnp.bfloat16)
     weights_next = lax.all_gather(fresh_rows, "shard", axis=1, tiled=True)
     whole = lax.psum(power, ("shard", "tensor"))
-    norms = jnp.sqrt(jnp.sum(whole * whole, axis=(1, 2)))
-    iterate = whole / (norms + norm_eps)[:, None, None]
-    for sweep in range(NS_ITERS):
-        gram_matrix = jnp.einsum("ldr,lds->lrs", iterate, iterate, precision=highest)
-        iterate = newton_step(iterate, gram_matrix)
-    basis_next = width**0.5 * iterate
+    basis_next = newton_schulz(whole, width)
     return (weights_next, basis_next, moment_one, moment_two)
 
 
+PLAIN = ((1,), (0,))
+BOTH_LAST = ((1,), (1,))
+CORE, Z, Y = 2, 3, 4
+
+
+def split(x):
+    high = x.astype(jnp.bfloat16)
+    return high, (x - high.astype(jnp.float32)).astype(jnp.bfloat16)
+
+
+def dot3(a, b, dims=PLAIN):
+    dot = lambda p, q: lax.dot_general(p, q, (dims, ((), ())), preferred_element_type=jnp.float32)
+    return dot(a[0], b[0]) + (dot(a[0], b[1]) + dot(a[1], b[0]))
+
+
+def params(megabytes):
+    return pltpu.CompilerParams(vmem_limit_bytes=megabytes * 2**20)
+
+
+def in_vmem(*arrays):
+    return [pltpu.with_memory_space_constraint(x, pltpu.VMEM) for x in arrays]
+
+
+def local_call(kernel, outs, index, *operands, name, scratch=()):
+    vmem = pl.BlockSpec(memory_space=pltpu.VMEM)
+    return pl.pallas_call(
+        kernel,
+        out_shape=[(jax.ShapeDtypeStruct if name == "moments" and i < 2 else pltpu.VMEM)(*out) for i, out in enumerate(outs)],
+        in_specs=[pl.BlockSpec(memory_space=pltpu.SMEM)] + [vmem] * len(operands),
+        out_specs=[vmem] * len(outs),
+        scratch_shapes=scratch,
+        compiler_params=params(12),
+        name=name,
+    )(index, *in_vmem(*operands))
+
+
+def chunks(rows):
+    half = rows // 2
+    return ((0, 0, 0, rows), (0, 1, 0, rows), (1, 0, 0, rows), (1, 1, 0, half), (1, 1, half, half))
+
+
+def layer_of(index_ref, turn):
+    return index_ref[CORE] if turn else 1 - index_ref[CORE]
+
+
+def give_kernel(rows, grads_ref, *rest):
+    outs, sems = rest[:-1], rest[-1]
+    outer = lax.rem(lax.axis_index("shard") + 1, 4) <= 1
+    core = lax.rem(lax.axis_index("tensor"), 2)
+    copies = []
+    for i, out in enumerate(outs):
+        block = jnp.where(outer, 1 + i % 2, 3 * (i % 2))
+        start = pl.multiple_of(block * rows, rows)
+        layer = 1 - core if i < 2 else core
+        copies.append(pltpu.make_async_copy(grads_ref.at[0, layer, pl.ds(start, rows)], out, sems.at[i]))
+    for copy in copies:
+        copy.start()
+    for copy in copies:
+        copy.wait()
+
+
+def give_blocks(grads, rows):
+    count = 4
+    return pl.pallas_call(
+        functools.partial(give_kernel, rows),
+        out_shape=[pltpu.VMEM((rows, grads.shape[3]), grads.dtype)] * count,
+        in_specs=[pl.BlockSpec(memory_space=pltpu.HBM)],
+        out_specs=[pl.BlockSpec(memory_space=pltpu.VMEM)] * count,
+        scratch_shapes=[pltpu.SemaphoreType.DMA((count,))],
+        compiler_params=params(4),
+        name="give_blocks",
+    )(pltpu.with_memory_space_constraint(grads, pltpu.HBM))
+
+
+def kept_sum(index_ref, grads_ref, other_ref, chunk, rows):
+    turn, j, row, count = chunk
+    start = pl.multiple_of(index_ref[j] * rows + row, count)
+    kept = grads_ref[0, layer_of(index_ref, turn), pl.ds(start, count)]
+    return kept.astype(jnp.float32) + other_ref[pl.ds(row, count)].astype(jnp.float32)
+
+
+def project_kernel(chunk, rows, index_ref, grads_ref, other_ref, basis_ref, *refs):
+    total = kept_sum(index_ref, grads_ref, other_ref, chunk, rows)
+    projected = dot3(split(total), split(basis_ref[layer_of(index_ref, chunk[0])]))
+    if len(refs) == 1:
+        refs[0][...] = projected
+        return
+    *before, out_ref, far0_ref, far1_ref = refs
+    out_ref[...] = projected
+    for (turn, j, row, count), part in zip(chunks(rows), before):
+        (far0_ref, far1_ref)[turn][pl.ds(j * rows + row, count)] = part[...]
+    far1_ref[pl.ds(2 * rows - projected.shape[0], projected.shape[0])] = projected
+
+
+def project(index, grads, other, basis, chunk, rows, before=()):
+    rank = basis.shape[2]
+    kernel = functools.partial(project_kernel, chunk, rows)
+    outs = [((chunk[3], rank), jnp.float32)] + [((2 * rows, rank), jnp.float32)] * (2 if before else 0)
+    return local_call(kernel, outs, index, grads, other, basis, *before, name="project")
+
+
+HALVES = 2
+
+
+def place_of(index_ref, h, k, piece):
+    place = h * 4 + (index_ref[Y] ^ (k // 2)) * 2 + (index_ref[0] ^ (k % 2))
+    return pl.multiple_of(place * piece, piece)
+
+
+def power_kernel(turn, rows, index_ref, grads_ref, *refs):
+    mine_chunks = [chunk for chunk in chunks(rows) if chunk[0] == turn]
+    n = len(mine_chunks)
+    others, partials, inner, (far_ref, *rest) = refs[:n], refs[n : 2 * n], refs[2 * n : 3 * n], refs[3 * n :]
+    sums, summed = [], []
+    for chunk, other, partial, received in zip(mine_chunks, others, partials, inner):
+        _, j, row, count = chunk
+        summed.append(kept_sum(index_ref, grads_ref, other, chunk, rows))
+        sums.append(partial[...] + (received[...] + far_ref[pl.ds(j * rows + row, count)]))
+    projected, summed = jnp.concatenate(sums), jnp.concatenate(summed)
+    total = dot3(split(projected.T), split(summed))
+    *halves, mine_ref, scratch = rest
+    mine_ref[...] = jnp.where(index_ref[Z] < 2, projected[:rows], projected[rows:])
+    scratch[...] = total
+    piece = total.shape[0] // (4 * HALVES)
+    for h in range(HALVES):
+        for k in range(4):
+            halves[h][pl.ds(k * piece, piece)] = scratch[pl.ds(place_of(index_ref, h, k, piece), piece)]
+
+
+def power_product(index, grads, others, partials, inner, far, turn):
+    width, rank, rows = grads.shape[3], far.shape[1], far.shape[0] // 2
+    outs = [((rank // HALVES, width), jnp.float32)] * HALVES + [((rows, rank), jnp.float32)]
+    kernel = functools.partial(power_kernel, turn, rows)
+    scratch = [pltpu.VMEM((rank, width), jnp.float32)]
+    return local_call(kernel, outs, index, grads, *others, *partials, *inner, far, name="power", scratch=scratch)
+
+
+def add_split_kernel(index_ref, own_ref, received_ref, keep_ref, give_ref):
+    half = keep_ref.shape[0]
+    keep_ref[...] = own_ref[0:half] + received_ref[0:half]
+    give_ref[...] = own_ref[half:] + received_ref[half:]
+
+
+def add_split(index, own, received):
+    outs = [((own.shape[0] // 2, own.shape[1]), jnp.float32)] * 2
+    return local_call(add_split_kernel, outs, index, own, received, name="add_split")
+
+
+def newton_schulz_kernel(index_ref, *refs):
+    parts, (out_ref, result_ref, power_ref, sems) = refs[:-4], refs[-4:]
+    piece = parts[0].shape[0] // 2
+    for h in range(HALVES):
+        for k in range(4):
+            part = parts[2 * h + k // 2]
+            power_ref[pl.ds(place_of(index_ref, h, k, piece), piece)] = part[pl.ds(k % 2 * piece, piece)]
+    power = power_ref[...]
+    rank, width = power.shape
+    unscaled = split(power)
+    scale = 1.0 / (jnp.sqrt(jnp.sum(power * power)) + norm_eps)
+    gram = dot3(unscaled, unscaled, BOTH_LAST) * scale * scale
+    ident = lax.broadcasted_iota(jnp.int32, gram.shape, 0) == lax.broadcasted_iota(jnp.int32, gram.shape, 1)
+    diagonal = jnp.where(ident, coeff_a, 0.0)
+    product = None
+    for sweep in range(NS_ITERS - 1):
+        g = split(gram)
+        factor = diagonal + coeff_b * gram + coeff_c * dot3(g, g)
+        f = split(factor)
+        gram = dot3(split(dot3(f, g)), f)
+        product = f if product is None else split(dot3(product, f))
+    iterate = split(dot3(product, unscaled))
+    g = split(gram)
+    last = split((diagonal + coeff_b * gram + coeff_c * dot3(g, g)) * (scale * width**0.5))
+    copies = []
+    for i in range(width // rank):
+        columns = slice(i * rank, (i + 1) * rank)
+        result_ref[columns] = dot3(last, [term[:, columns] for term in iterate]).T
+        copies.append(pltpu.make_async_copy(result_ref.at[columns], out_ref.at[index_ref[CORE], columns], sems.at[i]))
+        copies[-1].start()
+    for copy in copies:
+        copy.wait()
+
+
+def newton_schulz_power(index, layers, *parts):
+    rank, width = 2 * HALVES * parts[0].shape[0], parts[0].shape[1]
+    vmem = pl.BlockSpec(memory_space=pltpu.VMEM)
+    return pl.pallas_call(
+        newton_schulz_kernel,
+        out_shape=[jax.ShapeDtypeStruct((layers, width, rank), jnp.float32), pltpu.VMEM((width, rank), jnp.float32)],
+        in_specs=[pl.BlockSpec(memory_space=pltpu.SMEM)] + [vmem] * len(parts),
+        out_specs=[pl.BlockSpec(memory_space=pl.ANY), vmem],
+        scratch_shapes=[pltpu.VMEM((rank, width), jnp.float32), pltpu.SemaphoreType.DMA((width // rank,))],
+        compiler_params=params(12),
+        name="newton_schulz",
+    )(index, *in_vmem(*parts))
+
+
+def put_layer_kernel(index_ref, layer_ref, whole_ref, out_ref, sem):
+    copy = pltpu.make_async_copy(layer_ref, out_ref.at[1 - index_ref[CORE]], sem)
+    copy.start()
+    copy.wait()
+
+
+def put_layer(index, layer, whole):
+    hbm = pl.BlockSpec(memory_space=pl.ANY)
+    return pl.pallas_call(
+        put_layer_kernel,
+        out_shape=jax.ShapeDtypeStruct(whole.shape, whole.dtype),
+        in_specs=[pl.BlockSpec(memory_space=pltpu.SMEM), pl.BlockSpec(memory_space=pltpu.VMEM), hbm],
+        out_specs=hbm,
+        scratch_shapes=[pltpu.SemaphoreType.DMA],
+        input_output_aliases={2: 0},
+        compiler_params=params(4),
+        name="put_layer",
+    )(index, *in_vmem(layer), whole)
+
+
+SPAN = 250.0
+
+
+def encode(x):
+    bound = jnp.max(jnp.abs(x), axis=0, keepdims=True)
+    bound = (bound * 1.01 + 1e-30).astype(jnp.bfloat16).astype(jnp.float32)
+    size = jnp.exp2(jnp.abs(x) * (SPAN / bound) - SPAN / 2)
+    code = jnp.where(x < 0, -size, size)
+    return code.astype(jnp.bfloat16), jnp.broadcast_to(bound, (16, x.shape[1])).astype(jnp.bfloat16)
+
+
+def decode(code, bound):
+    code, bound = code.astype(jnp.float32), bound[0:1].astype(jnp.float32)
+    size = (jnp.log2(jnp.abs(code)) + SPAN / 2) * (bound / SPAN)
+    return jnp.where(code < 0, -size, size)
+
+
+def moments_kernel(scale, index_ref, mine0_ref, mine1_ref, first_ref, second_ref, one_ref, two_ref, code_ref):
+    rows = first_ref.shape[1]
+    for turn, mine in enumerate((mine0_ref, mine1_ref)):
+        layer = layer_of(index_ref, turn)
+        reduced = scale * mine[...]
+        one_ref[layer], two_ref[layer], direction = adam_direction(reduced, first_ref[layer], second_ref[layer])
+        code_ref[layer, 0:rows], code_ref[layer, rows:] = encode(direction)
+
+
+def moments(index, mine, first_moment, second_moment, scale):
+    layers, rows, rank = first_moment.shape
+    outs = [(first_moment.shape, jnp.float32)] * 2 + [((layers, rows + 16, rank), jnp.bfloat16)]
+    return local_call(functools.partial(moments_kernel, scale), outs, index, *mine, first_moment, second_moment, name="moments")
+
+
+def update_kernel(factor, index_ref, weights_ref, basis_ref, d0_ref, d1_ref, d2_ref, d3_ref, *rest):
+    out_ref, high, low = rest[-3:]
+    k = pl.program_id(0)
+
+    @pl.when(k == 0)
+    def _():
+        high[...], low[...] = split(basis_ref[0].T)
+
+    for step, direction in enumerate((d0_ref, d1_ref, d2_ref, d3_ref)):
+
+        @pl.when(k == step)
+        def _(direction=direction):
+            rows = out_ref.shape[1]
+            exact = decode(direction[0, 0:rows], direction[0, rows:])
+            update = dot3(split(exact), (high[...], low[...]))
+            out_ref[0] = (weights_ref[0].astype(jnp.float32) - factor * update).astype(out_ref.dtype)
+
+
+def update_weights(index, weights, basis, directions, factor, layer, before):
+    layers, height, width = weights.shape
+    rank = basis.shape[2]
+    rows = height // 4
+    row_block = pl.BlockSpec((1, rows, width), lambda k, index: (layer, index[Z] ^ k, 0))
+    layer_block = lambda a, b: pl.BlockSpec((1, a, b), lambda k, index: (layer, 0, 0))
+    extra = [] if before is None else [before]
+    return pl.pallas_call(
+        functools.partial(update_kernel, factor),
+        out_shape=jax.ShapeDtypeStruct(weights.shape, weights.dtype),
+        grid_spec=pltpu.PrefetchScalarGridSpec(
+            num_scalar_prefetch=1,
+            grid=(4,),
+            in_specs=[row_block, layer_block(width, rank)]
+            + [layer_block(rows + 16, rank)] * 4
+            + [pl.BlockSpec(memory_space=pl.ANY)] * len(extra),
+            out_specs=row_block,
+            scratch_shapes=[pltpu.VMEM((rank, width), jnp.bfloat16)] * 2,
+        ),
+        input_output_aliases={7: 0} if extra else {},
+        compiler_params=params(12),
+        name="update_weights",
+    )(index, weights, basis, *directions, *extra)
+
+
+def xor_pairs(k):
+    return [(i, i ^ k) for i in range(4)]
+
+
+OUTER, INNER = (0, 3), (1, 2)
+
+
+def over_z(x, k, members=range(4)):
+    return lax.ppermute(x, "shard", [pair for pair in xor_pairs(k) if pair[0] in members])
+
+
+def over_core(x):
+    return lax.ppermute(x, "tensor", xor_pairs(1))
+
+
+def over_y(x):
+    return lax.ppermute(x, "tensor", xor_pairs(2))
+
+
+class Order:
+    def __init__(self):
+        self.last = None
+
+    def step(self, *operands):
+        if self.last is None:
+            return operands
+        return lax.optimization_barrier(tuple(operands) + (self.last,))[:-1]
+
+    def through(self, result):
+        self.last = result
+        return result
+
+
+def line_body(grads, weights, basis, first_moment, second_moment):
+    width = basis.shape[1]
+    scale_factor = width ** (-0.5)
+    layers = grads.shape[1]
+    rows = first_moment.shape[1]
+    z = lax.axis_index("shard")
+    tensor = lax.axis_index("tensor")
+    y, core = tensor // 2, tensor % 2
+    outer = (z == 0) | (z == 3)
+    order = Order()
+
+    keep = jnp.where(outer, jnp.array([0, 3], jnp.int32), jnp.array([1, 2], jnp.int32))
+    index = jnp.concatenate([keep, jnp.stack([core, z, y]).astype(jnp.int32)])
+    others = [over_z(block, 1) for block in give_blocks(grads, rows)]
+    partials, inner = [], []
+    for i, chunk in enumerate(chunks(rows)):
+        other = others[2 * chunk[0] + chunk[1]]
+        if i < 2:
+            (other,) = order.step(other)
+        else:
+            other, inner[i - 2] = order.step(other, inner[i - 2])
+        partial, *far = project(index, grads, other, basis, chunk, rows, partials if i == 4 else ())
+        partials.append(order.through(partial))
+        inner.append(over_z(partial, 3, INNER))
+    *far, inner[3], inner[4] = order.step(*far, inner[3], inner[4])
+    far = [over_z(part, 3, OUTER) for part in far]
+
+    def product(turn):
+        some = slice(0, 2) if turn == 0 else slice(2, 5)
+        n = some.stop - some.start
+        operands = order.step(*[others[2 * c[0] + c[1]] for c in chunks(rows)[some]], *partials[some], *inner[some], far[turn])
+        *halves, mine = power_product(index, grads, operands[:n], operands[n : 2 * n], operands[2 * n : -1], operands[-1], turn)
+        order.through(halves[0])
+        return halves, mine
+
+    def scatter(over, x, received):
+        keep, give = add_split(index, *order.step(x, received))
+        return order.through(keep), over(give)
+
+    def total(over, x, received):
+        x, received = order.step(x, received)
+        x = order.through(x + received)
+        return x, over(x)
+
+    def gather(over, x, received):
+        x = order.through(jnp.concatenate(order.step(x, received)))
+        return x, over(x)
+
+    next_z = lambda x: over_z(x, 1)
+    opposite_z = lambda x: over_z(x, 3)
+
+    gifts, mine0 = product(0)
+    gifts = [over_core(gift) for gift in gifts]
+    parts, mine1 = product(1)
+    parts = [scatter(over_y, part, gift) for part, gift in zip(parts, gifts)]
+    mine = order.step(mine0, mine1)
+    moment_one, moment_two, code = moments(index, mine, first_moment, second_moment, scale_factor)
+    order.through(code)
+    opposite, near = opposite_z(code), next_z(code)
+    parts = [scatter(next_z, *part) for part in parts]
+    parts = [total(opposite_z, *part) for part in parts]
+    opposite, near = order.step(opposite, near)
+    next_to_opposite = next_z(opposite)
+    parts = [total(next_z, *part) for part in parts]
+    directions = (code, near, next_to_opposite, opposite)
+    factor = learn_rate * galore_scale * scale_factor
+    update = functools.partial(update_weights, index, weights, basis)
+    weights_next = order.through(update(order.step(*directions), factor, 0, None))
+    parts = [gather(over_y, *part) for part in parts]
+    weights_next = order.through(update(order.step(*directions), factor, 1, weights_next))
+    parts = order.step(*[x for part in parts for x in part])
+    basis_next, own = newton_schulz_power(index, layers, *parts)
+    basis_next = put_layer(index, over_core(own), basis_next)
+    return (weights_next, basis_next, moment_one, moment_two)
+
+
 def solution(mesh):
+    line = mesh.shape["shard"] == 4 and mesh.shape["tensor"] == 4
+
+    def body(grads, *others):
+        return (line_body if line and grads.shape[1] == 2 else general_body)(grads, *others)
+
     return jax.shard_map(
         body,
         mesh=mesh,

time: 263 us -> 120 us (0.46)
  waiting for transfers between devices: 215 us -> 46.1 us
  starting transfers between devices: 0.3 us -> 43.9 us
  Pallas kernels: 0 us -> 27.3 us
  matrix products: 21.9 us -> 0 us
  between operations: 13.9 us -> 0.96 us
  other arithmetic: 6.11 us -> 0.13 us
  local copies, waits for them, and re-layouts: 4.91 us -> 1.48 us
    psum x1 -> x0, waiting for transfers between devices: 92.2 us -> none  [body(): whole = lax.psum(power, ('shard', 'tensor'))]
    reduce_scatter x1 -> x0, waiting for transfers between devices: 88.1 us -> none  [body(): lax.psum_scatter(local_grads.astype(jnp.float32), 'shard', scatter_dimens...]
    ppermute x0 -> x27, waiting for transfers between devices: none -> 46.1 us  [the longest x20 41.6 us: over_z(): lax.ppermute(x, 'shard', [pair for pair in xor_pairs(k) if pair[0] in mem...]
    ppermute x0 -> x27, starting transfers between devices: none -> 43.9 us  [the longest x20 39 us: over_z(): lax.ppermute(x, 'shard', [pair for pair in xor_pairs(k) if pair[0] in mem...]
    all_gather x1 -> x0, waiting for transfers between devices: 35.1 us -> none  [body(): weights_next = lax.all_gather(fresh_rows, 'shard', axis=1, tiled=True)]
    pallas_call x0 -> x17, Pallas kernels: none -> 27.3 us  [the longest x12 11.6 us: local_call(): pl.pallas_call(kernel, out_shape=[(jax.ShapeDtypeStruct if name == 'momen...]
    dot_general x12 -> x0, matrix products: 21.9 us -> none  [the longest x3 5.53 us: newton_step(): jnp.einsum('ldr,lrs->lds', iterate, mixing, precision=highest)]
    convert_element_type x1 -> x0, other arithmetic: 4.27 us -> none  [body(): local_grads.astype(jnp.float32)]
  transfers between devices with their start and end apart: 3 -> 27, of which waited for: 3 -> 13; matrix products, arithmetic and copies ran while one was open for 8% -> 0% of each run, Pallas kernels for 0% -> 16%
where the time goes in v2:
time: 120 us
  waiting for transfers between devices  46.1 us (38%)
  starting transfers between devices  43.9 us (37%)
  Pallas kernels  27.3 us (23%)
  local copies, waits for them, and re-layouts  1.48 us (1%)
    ppermute x20, waiting for transfers between devices, over_z(): lax.ppermute(x, 'shard', [pair for pair in xor_pairs(k) if pair[0] in mem...  41.6 us
    ppermute x20, starting transfers between devices, over_z(): lax.ppermute(x, 'shard', [pair for pair in xor_pairs(k) if pair[0] in mem...  39 us
    pallas_call x12, Pallas kernels, local_call(): pl.pallas_call(kernel, out_shape=[(jax.ShapeDtypeStruct if name == 'momen...  11.6 us
    pallas_call x2, Pallas kernels, update_weights(): pl.pallas_call(functools.partial(update_kernel, factor), out_shape=jax.Sh...  7.09 us
    pallas_call x1, Pallas kernels, newton_schulz_power(): pl.pallas_call(newton_schulz_kernel, out_shape=[jax.ShapeDtypeStruct((lay...  4.77 us
    ppermute x4, starting transfers between devices, over_y(): return lax.ppermute(x, 'tensor', xor_pairs(2))  4.25 us
  transfers between devices with their start and end apart: 27, of which 13 were waited for; matrix products, arithmetic and copies ran while one was open for 0% of the time, Pallas kernels for 16%

profile of v2, /device:TPU:0, one launch (start us, length us, event | category | flops | bytes accessed | tf_op | source)
XLA Modules:
  0.0 119.8 jit_solution(1967078112433054701)
XLA Ops:
  0.7 2.3 %give_blocks.1 = (bf16[192,768]{1,0:T(8,128)(2,1)}, bf16[192,768]{1,0:T(8,128)(2,1)}, bf16[192,768]{1,0:T(8,128)(2,1)}, bf16[192,768]{1,0:T(8,128)(2,1)S(1)}) custom-call(bf16[1,2,768,768]{3,2,1,0:T(8,128)(2,1)} %grads_ref.15), custom_call_target="tpu_custom_call" | custom-call | tf_op jit(solution)/shard_map/give_blocks/pallas_call | solution.py:135
  3.0 3.1 %collective-permute-start = (bf16[192,768]{1,0:T(8,128)(2,1)}, bf16[192,768]{1,0:T(8,128)(2,1)S(1)}, u32[]{:S(2)}, u32[]{:S(2)}) collective-permute-start(bf16[192,768]{1,0:T(8,128)(2,1)} %get-tuple-element.94), channel_id=1, source_target_pairs={{0,8},{8,0},{16,24},{24,16},{1,9},{9,1},{17,25},{25,17},{2,10},{10... | collective-permute-start | bytes 884744 | tf_op jit(solution)/shard_map/ppermute | solution.py:371
  6.2 1.9 %collective-permute-start.2 = (bf16[192,768]{1,0:T(8,128)(2,1)}, bf16[192,768]{1,0:T(8,128)(2,1)S(1)}, u32[]{:S(2)}, u32[]{:S(2)}) collective-permute-start(bf16[192,768]{1,0:T(8,128)(2,1)} %get-tuple-element.97), channel_id=1, source_target_pairs={{0,8},{8,0},{16,24},{24,16},{1,9},{9,1},{17,25},{25,17},{2,10},{10... | collective-permute-start | bytes 884744 | tf_op jit(solution)/shard_map/ppermute | solution.py:371
  8.2 5.9 %collective-permute-done.other_ref.refs_0_ = bf16[192,768]{1,0:T(8,128)(2,1)S(1)} collective-permute-done((bf16[192,768]{1,0:T(8,128)(2,1)}, bf16[192,768]{1,0:T(8,128)(2,1)S(1)}, u32[]{:S(2)}, u32[]{:S(2)}) %collective-permute-start) | collective-permute-done | bytes 294944 | tf_op jit(solution)/shard_map/ppermute | solution.py:371
  14.1 1.4 %copy-done.1 = f32[2,768,256]{2,1,0:T(8,128)S(1)} copy-done((f32[2,768,256]{2,1,0:T(8,128)S(1)}, f32[2,768,256]{2,1,0:T(8,128)}, u32[]{:S(2)}) %copy-start.1) | copy-done | bytes 1572888
  15.5 1.0 project.5.refs_0_.refs_2_
  16.5 0.7 collective-permute-start.3
  17.2 4.9 %collective-permute-start.4 = (bf16[192,768]{1,0:T(8,128)(2,1)S(1)}, bf16[192,768]{1,0:T(8,128)(2,1)S(1)}, u32[]{:S(2)}, u32[]{:S(2)}) collective-permute-start(bf16[192,768]{1,0:T(8,128)(2,1)S(1)} %get-tuple-element.99), channel_id=1, source_target_pairs={{0,8},{8,0},{16,24},{24,16},{1,9},{9,1},{17,25},{25,17},{2,10},{10... | collective-permute-start | bytes 884744 | tf_op jit(solution)/shard_map/ppermute | solution.py:371
  22.2 1.0 project.6.refs_1_.refs_3_
  23.1 0.7 collective-permute-start.5
  23.8 2.9 %collective-permute-done.2.other_ref.refs_0_ = bf16[192,768]{1,0:T(8,128)(2,1)S(1)} collective-permute-done((bf16[192,768]{1,0:T(8,128)(2,1)}, bf16[192,768]{1,0:T(8,128)(2,1)S(1)}, u32[]{:S(2)}, u32[]{:S(2)}) %collective-permute-start.2) | collective-permute-done | bytes 294944 | tf_op jit(solution)/shard_map/ppermute | solution.py:371
  26.8 1.0 project.7.refs_2_.refs_3_
  27.8 0.7 collective-permute-start.6
  28.4 3.8 %collective-permute-done.4.other_ref.refs_1_.refs_2_ = bf16[192,768]{1,0:T(8,128)(2,1)S(1)} collective-permute-done((bf16[192,768]{1,0:T(8,128)(2,1)S(1)}, bf16[192,768]{1,0:T(8,128)(2,1)S(1)}, u32[]{:S(2)}, u32[]{:S(2)}) %collective-permute-start.4) | collective-permute-done | bytes 294944 | tf_op jit(solution)/shard_map/ppermute | solution.py:371
  32.3 0.9 project.8.refs_3_.refs_4_
  33.2 0.7 collective-permute-start.7
  33.9 0.9 project.9
  34.8 0.7 collective-permute-start.8
  35.4 5.7 %collective-permute-start.9 = (f32[384,256]{1,0:T(8,128)S(1)}, f32[384,256]{1,0:T(8,128)S(1)}, u32[]{:S(2)}, u32[]{:S(2)}) collective-permute-start(f32[384,256]{1,0:T(8,128)S(1)} %get-tuple-element.107), channel_id=1, source_target_pairs={{0,24},{24,0},{1,25},{25,1},{2,26},{26,2},{3,27},{27,3},{4,28},{28... | collective-permute-start | bytes 1179656 | tf_op jit(solution)/shard_map/ppermute | solution.py:371
  41.1 2.0 %collective-permute-start.10 = (f32[384,256]{1,0:T(8,128)S(1)}, f32[384,256]{1,0:T(8,128)S(1)}, u32[]{:S(2)}, u32[]{:S(2)}) collective-permute-start(f32[384,256]{1,0:T(8,128)S(1)} %get-tuple-element.119), channel_id=1, source_target_pairs={{0,24},{24,0},{1,25},{25,1},{2,26},{26,2},{3,27},{27,3},{4,28},{28... | collective-permute-start | bytes 1179656 | tf_op jit(solution)/shard_map/ppermute | solution.py:371
  43.1 8.2 %collective-permute-done.9.refs_6_ = f32[384,256]{1,0:T(8,128)S(1)} collective-permute-done((f32[384,256]{1,0:T(8,128)S(1)}, f32[384,256]{1,0:T(8,128)S(1)}, u32[]{:S(2)}, u32[]{:S(2)}) %collective-permute-start.9) | collective-permute-done | bytes 393248 | tf_op jit(solution)/shard_map/ppermute | solution.py:371
  51.3 1.5 %power.2 = (f32[128,768]{1,0:T(8,128)S(1)}, f32[128,768]{1,0:T(8,128)S(1)}, f32[192,256]{1,0:T(8,128)S(1)}) custom-call(s32[5]{0:T(128)S(1)} %pad_add_fusion.index_ref, bf16[1,2,768,768]{3,2,1,0:T(8,128)(2,1)S(1)} %copy-done, bf16[192,768]{1,0:T(8,128)(2,1)S(1)} %collective-permute-done.other_ref.refs_0_, ...), custom_call_target="tpu_custom_call" | custom-call | tf_op jit(solution)/shard_map/power/pallas_call | solution.py:97
  53.3 4.6 %collective-permute-done.10.refs_9_ = f32[384,256]{1,0:T(8,128)S(1)} collective-permute-done((f32[384,256]{1,0:T(8,128)S(1)}, f32[384,256]{1,0:T(8,128)S(1)}, u32[]{:S(2)}, u32[]{:S(2)}) %collective-permute-start.10) | collective-permute-done | bytes 393248 | tf_op jit(solution)/shard_map/ppermute | solution.py:371
  58.0 1.5 %power.3 = (f32[128,768]{1,0:T(8,128)S(1)}, f32[128,768]{1,0:T(8,128)S(1)}, f32[192,256]{1,0:T(8,128)S(1)}) custom-call(s32[5]{0:T(128)S(1)} %pad_add_fusion.index_ref, bf16[1,2,768,768]{3,2,1,0:T(8,128)(2,1)S(1)} %copy-done, bf16[192,768]{1,0:T(8,128)(2,1)S(1)} %collective-permute-done.2.other_ref.refs_0_, ...), custom_call_target="tpu_custom_call" | custom-call | tf_op jit(solution)/shard_map/power/pallas_call | solution.py:97
  59.5 0.6 add_split.4
  60.0 1.5 %collective-permute-start.16 = (f32[64,768]{1,0:T(8,128)S(1)}, f32[64,768]{1,0:T(8,128)S(1)}, u32[]{:S(2)}, u32[]{:S(2)}) collective-permute-start(f32[64,768]{1,0:T(8,128)S(1)} %get-tuple-element.145), channel_id=1, source_target_pairs={{0,4},{2,6},{4,0},{6,2},{1,5},{3,7},{5,1},{7,3},{8,12},{10,14},{12... | collective-permute-start | bytes 589832 | tf_op jit(solution)/shard_map/ppermute | solution.py:379
  61.6 0.6 add_split.5
  62.1 0.7 collective-permute-start.15
  62.8 1.7 %moments.1 = (f32[2,192,256]{2,1,0:T(8,128)}, f32[2,192,256]{2,1,0:T(8,128)}, bf16[2,208,256]{2,1,0:T(8,128)(2,1)S(1)}) custom-call(s32[5]{0:T(128)S(1)} %pad_add_fusion.index_ref, f32[192,256]{1,0:T(8,128)S(1)} %get-tuple-element.141.mine0_ref, f32[192,256]{1,0:T(8,128)S(1)} %get-tuple-element.142.mine1_ref, f32[2,192,256]{2,1,0:T(8,128)S(1)} %copy-done.4, ...), custom_call_target="tpu_custom_call" | custom-call | tf_op jit(solution)/shard_map/moments/pallas_call | solution.py:97
  64.5 6.0 %collective-permute-start.14 = (bf16[2,208,256]{2,1,0:T(8,128)(2,1)S(1)}, bf16[2,208,256]{2,1,0:T(8,128)(2,1)S(1)}, u32[]{:S(2)}, u32[]{:S(2)}) collective-permute-start(bf16[2,208,256]{2,1,0:T(8,128)(2,1)S(1)} %get-tuple-element.172.d0_ref), channel_id=1, source_target_pairs={{0,8},{8,0},{16,24},{24,16},{1,9},{9,1},{17,25},{25,17},{2,10},{10... | collective-permute-start | bytes 638984 | tf_op jit(solution)/shard_map/ppermute | solution.py:371
  70.5 2.4 %collective-permute-start.13 = (bf16[2,208,256]{2,1,0:T(8,128)(2,1)S(1)}, bf16[2,208,256]{2,1,0:T(8,128)(2,1)S(1)}, u32[]{:S(2)}, u32[]{:S(2)}) collective-permute-start(bf16[2,208,256]{2,1,0:T(8,128)(2,1)S(1)} %get-tuple-element.172.d0_ref), channel_id=1, source_target_pairs={{0,24},{8,16},{16,8},{24,0},{1,25},{9,17},{17,9},{25,1},{2,26},{10... | collective-permute-start | bytes 638984 | tf_op jit(solution)/shard_map/ppermute | solution.py:371
  73.5 1.0 collective-permute-start.18
  75.1 2.8 %collective-permute-start.17 = (f32[32,768]{1,0:T(8,128)S(1)}, f32[32,768]{1,0:T(8,128)S(1)}, u32[]{:S(2)}, u32[]{:S(2)}) collective-permute-start(f32[32,768]{1,0:T(8,128)S(1)} %get-tuple-element.152), channel_id=1, source_target_pairs={{0,8},{8,0},{16,24},{24,16},{1,9},{9,1},{17,25},{25,17},{2,10},{10... | collective-permute-start | bytes 294920 | tf_op jit(solution)/shard_map/ppermute | solution.py:371
  77.9 4.6 %collective-permute-done.18 = f32[32,768]{1,0:T(8,128)S(1)} collective-permute-done((f32[32,768]{1,0:T(8,128)S(1)}, f32[32,768]{1,0:T(8,128)S(1)}, u32[]{:S(2)}, u32[]{:S(2)}) %collective-permute-start.18) | collective-permute-done | bytes 98336 | tf_op jit(solution)/shard_map/ppermute | solution.py:371
  82.5 1.9 %collective-permute-done.17 = f32[32,768]{1,0:T(8,128)S(1)} collective-permute-done((f32[32,768]{1,0:T(8,128)S(1)}, f32[32,768]{1,0:T(8,128)S(1)}, u32[]{:S(2)}, u32[]{:S(2)}) %collective-permute-start.17) | collective-permute-done | bytes 98336 | tf_op jit(solution)/shard_map/ppermute | solution.py:371
  84.4 1.7 %collective-permute-start.19 = (bf16[2,208,256]{2,1,0:T(8,128)(2,1)S(1)}, bf16[2,208,256]{2,1,0:T(8,128)(2,1)S(1)}, u32[]{:S(2)}, u32[]{:S(2)}) collective-permute-start(bf16[2,208,256]{2,1,0:T(8,128)(2,1)S(1)} %collective-permute-done.13.d3_ref), channel_id=1, source_target_pairs={{0,8},{8,0},{16,24},{24,16},{1,9},{9,1},{17,25},{25,17},{2,10},{10... | collective-permute-start | bytes 638984 | tf_op jit(solution)/shard_map/ppermute | solution.py:371
  86.1 2.4 %collective-permute-start.21 = (f32[32,768]{1,0:T(8,128)S(1)}, f32[32,768]{1,0:T(8,128)S(1)}, u32[]{:S(2)}, u32[]{:S(2)}) collective-permute-start(f32[32,768]{1,0:T(8,128)S(1)} %add.18), channel_id=1, source_target_pairs={{0,24},{8,16},{16,8},{24,0},{1,25},{9,17},{17,9},{25,1},{2,26},{10... | collective-permute-start | bytes 294920 | tf_op jit(solution)/shard_map/ppermute | solution.py:371
  88.5 1.4 %collective-permute-start.20 = (f32[32,768]{1,0:T(8,128)S(1)}, f32[32,768]{1,0:T(8,128)S(1)}, u32[]{:S(2)}, u32[]{:S(2)}) collective-permute-start(f32[32,768]{1,0:T(8,128)S(1)} %add.19), channel_id=1, source_target_pairs={{0,24},{8,16},{16,8},{24,0},{1,25},{9,17},{17,9},{25,1},{2,26},{10... | collective-permute-start | bytes 294920 | tf_op jit(solution)/shard_map/ppermute | solution.py:371
  89.9 6.7 %collective-permute-done.21 = f32[32,768]{1,0:T(8,128)S(1)} collective-permute-done((f32[32,768]{1,0:T(8,128)S(1)}, f32[32,768]{1,0:T(8,128)S(1)}, u32[]{:S(2)}, u32[]{:S(2)}) %collective-permute-start.21) | collective-permute-done | bytes 98336 | tf_op jit(solution)/shard_map/ppermute | solution.py:371
  96.7 2.0 %collective-permute-done.20 = f32[32,768]{1,0:T(8,128)S(1)} collective-permute-done((f32[32,768]{1,0:T(8,128)S(1)}, f32[32,768]{1,0:T(8,128)S(1)}, u32[]{:S(2)}, u32[]{:S(2)}) %collective-permute-start.20) | collective-permute-done | bytes 98336 | tf_op jit(solution)/shard_map/ppermute | solution.py:371
  98.8 3.5 %update_weights.2.rest_0_ = bf16[2,768,768]{2,1,0:T(8,128)(2,1)} custom-call(s32[5]{0:T(128)S(1)} %pad_add_fusion.index_ref, bf16[2,768,768]{2,1,0:T(8,128)(2,1)S(1)} %copy-done.3, f32[2,768,256]{2,1,0:T(8,128)S(1)} %copy-done.2, bf16[2,208,256]{2,1,0:T(8,128)(2,1)S(1)} %get-tuple-element.172.d0_ref, ...), custom_call_target="tpu_custom_call" | custom-call | tf_op jit(solution)/shard_map/update_weights/pallas_call | solution.py:345
  102.4 1.0 collective-permute-done.22
  103.4 1.6 %collective-permute-start.25 = (f32[64,768]{1,0:T(8,128)S(1)}, f32[64,768]{1,0:T(8,128)S(1)}, u32[]{:S(2)}, u32[]{:S(2)}) collective-permute-start(f32[64,768]{1,0:T(8,128)S(1)} %constant_dynamic-update-slice_fusion.2.refs_2_), channel_id=1, source_target_pairs={{0,4},{2,6},{4,0},{6,2},{1,5},{3,7},{5,1},{7,3},{8,12},{10,14},{12... | collective-permute-start | bytes 589832 | tf_op jit(solution)/shard_map/ppermute | solution.py:379
  105.5 3.5 %update_weights.3 = bf16[2,768,768]{2,1,0:T(8,128)(2,1)} custom-call(s32[5]{0:T(128)S(1)} %pad_add_fusion.index_ref, bf16[2,768,768]{2,1,0:T(8,128)(2,1)S(1)} %copy-done.3, f32[2,768,256]{2,1,0:T(8,128)S(1)} %copy-done.2, bf16[2,208,256]{2,1,0:T(8,128)(2,1)S(1)} %get-tuple-element.172.d0_ref, ...), custom_call_target="tpu_custom_call", output_to_operand_aliasing={{}: (7, {})} | custom-call | tf_op jit(solution)/shard_map/update_weights/pallas_call | solution.py:345
  109.1 2.1 %collective-permute-done.24.refs_1_ = f32[64,768]{1,0:T(8,128)S(1)} collective-permute-done((f32[64,768]{1,0:T(8,128)S(1)}, f32[64,768]{1,0:T(8,128)S(1)}, u32[]{:S(2)}, u32[]{:S(2)}) %collective-permute-start.24) | collective-permute-done | bytes 196640 | tf_op jit(solution)/shard_map/ppermute | solution.py:379
  111.3 4.8 %newton_schulz.1 = (f32[2,768,256]{2,1,0:T(8,128)}, f32[768,256]{1,0:T(8,128)S(1)}) custom-call(s32[5]{0:T(128)S(1)} %pad_add_fusion.index_ref, f32[64,768]{1,0:T(8,128)S(1)} %constant_dynamic-update-slice_fusion.refs_0_, f32[64,768]{1,0:T(8,128)S(1)} %collective-permute-done.24.refs_1_, f32[64,768]{1,0:T(8,128)S(1)} %constant_dynamic-update-slice_fusion.2.refs_2_, ...), custom_call_target="tpu_custom_call" | custom-call | tf_op jit(solution)/shard_map/newton_schulz/pallas_call | solution.py:257
  116.1 2.3 %collective-permute-done.26.layer_ref = f32[768,256]{1,0:T(8,128)S(1)} collective-permute-done((f32[768,256]{1,0:T(8,128)S(1)}, f32[768,256]{1,0:T(8,128)S(1)}, u32[]{:S(2)}, u32[]{:S(2)}) %collective-permute-start.26) | collective-permute-done | bytes 786464 | tf_op jit(solution)/shard_map/ppermute | solution.py:375
  118.4 1.4 %put_layer.1 = f32[2,768,256]{2,1,0:T(8,128)} custom-call(s32[5]{0:T(128)S(1)} %pad_add_fusion.index_ref, f32[768,256]{1,0:T(8,128)S(1)} %collective-permute-done.26.layer_ref, f32[2,768,256]{2,1,0:T(8,128)} %get-tuple-element.181.whole_ref), custom_call_target="tpu_custom_call", output_to_operand_aliasing={{}: (2, {})} | custom-call | tf_op jit(solution)/shard_map/put_layer/pallas_call | solution.py:276
  (47 shorter events, 2.9 us)
Async XLA Ops:
  0.6 7.5 %copy-start.6 = (s32[2]{0:T(128)S(1)}, s32[2]{0:T(128)}, u32[]{:S(2)}) copy-start(s32[2]{0:T(128)} %constant.42.clone) | copy-start | bytes 28
  0.6 13.5 %copy-start = (bf16[1,2,768,768]{3,2,1,0:T(8,128)(2,1)S(1)}, bf16[1,2,768,768]{3,2,1,0:T(8,128)(2,1)}, u32[]{:S(2)}) copy-start(bf16[1,2,768,768]{3,2,1,0:T(8,128)(2,1)} %grads_ref.15) | copy-start | bytes 7077892
  3.0 11.1 %collective-permute-start = (bf16[192,768]{1,0:T(8,128)(2,1)}, bf16[192,768]{1,0:T(8,128)(2,1)S(1)}, u32[]{:S(2)}, u32[]{:S(2)}) collective-permute-start(bf16[192,768]{1,0:T(8,128)(2,1)} %get-tuple-element.94), channel_id=1, source_target_pairs={{0,8},{8,0},{16,24},{24,16},{1,9},{9,1},{17,25},{25,17},{2,10},{10... | collective-permute-start | bytes 884744 | tf_op jit(solution)/shard_map/ppermute | solution.py:371
  6.1 16.1 %collective-permute-start.1 = (bf16[192,768]{1,0:T(8,128)(2,1)}, bf16[192,768]{1,0:T(8,128)(2,1)S(1)}, u32[]{:S(2)}, u32[]{:S(2)}) collective-permute-start(bf16[192,768]{1,0:T(8,128)(2,1)} %get-tuple-element.95), channel_id=1, source_target_pairs={{0,8},{8,0},{16,24},{24,16},{1,9},{9,1},{17,25},{25,17},{2,10},{10... | collective-permute-start | bytes 884744 | tf_op jit(solution)/shard_map/ppermute | solution.py:371
  6.2 20.6 %collective-permute-start.2 = (bf16[192,768]{1,0:T(8,128)(2,1)}, bf16[192,768]{1,0:T(8,128)(2,1)S(1)}, u32[]{:S(2)}, u32[]{:S(2)}) collective-permute-start(bf16[192,768]{1,0:T(8,128)(2,1)} %get-tuple-element.97), channel_id=1, source_target_pairs={{0,8},{8,0},{16,24},{24,16},{1,9},{9,1},{17,25},{25,17},{2,10},{10... | collective-permute-start | bytes 884744 | tf_op jit(solution)/shard_map/ppermute | solution.py:371
  14.1 1.4 %copy-start.1 = (f32[2,768,256]{2,1,0:T(8,128)S(1)}, f32[2,768,256]{2,1,0:T(8,128)}, u32[]{:S(2)}) copy-start(f32[2,768,256]{2,1,0:T(8,128)} %basis_ref.13) | copy-start | bytes 4718596
  15.5 6.6 %copy-start.2 = (f32[2,768,256]{2,1,0:T(8,128)S(1)}, f32[2,768,256]{2,1,0:T(8,128)}, u32[]{:S(2)}) copy-start(f32[2,768,256]{2,1,0:T(8,128)} %basis_ref.13) | copy-start | bytes 4718596
  16.5 10.2 %collective-permute-start.3 = (f32[192,256]{1,0:T(8,128)S(1)}, f32[192,256]{1,0:T(8,128)S(1)}, u32[]{:S(2)}, u32[]{:S(2)}) collective-permute-start(f32[192,256]{1,0:T(8,128)S(1)} %project.5.refs_0_.refs_2_), channel_id=1, source_target_pairs={{8,16},{16,8},{9,17},{17,9},{10,18},{18,10},{11,19},{19,11},{12,20... | collective-permute-start | bytes 589832 | tf_op jit(solution)/shard_map/ppermute | solution.py:371
  17.2 15.0 %collective-permute-start.4 = (bf16[192,768]{1,0:T(8,128)(2,1)S(1)}, bf16[192,768]{1,0:T(8,128)(2,1)S(1)}, u32[]{:S(2)}, u32[]{:S(2)}) collective-permute-start(bf16[192,768]{1,0:T(8,128)(2,1)S(1)} %get-tuple-element.99), channel_id=1, source_target_pairs={{0,8},{8,0},{16,24},{24,16},{1,9},{9,1},{17,25},{25,17},{2,10},{10... | collective-permute-start | bytes 884744 | tf_op jit(solution)/shard_map/ppermute | solution.py:371
  23.1 9.1 %collective-permute-start.5 = (f32[192,256]{1,0:T(8,128)S(1)}, f32[192,256]{1,0:T(8,128)S(1)}, u32[]{:S(2)}, u32[]{:S(2)}) collective-permute-start(f32[192,256]{1,0:T(8,128)S(1)} %project.6.refs_1_.refs_3_), channel_id=1, source_target_pairs={{8,16},{16,8},{9,17},{17,9},{10,18},{18,10},{11,19},{19,11},{12,20... | collective-permute-start | bytes 589832 | tf_op jit(solution)/shard_map/ppermute | solution.py:371
  27.8 6.1 %collective-permute-start.6 = (f32[192,256]{1,0:T(8,128)S(1)}, f32[192,256]{1,0:T(8,128)S(1)}, u32[]{:S(2)}, u32[]{:S(2)}) collective-permute-start(f32[192,256]{1,0:T(8,128)S(1)} %project.7.refs_2_.refs_3_), channel_id=1, source_target_pairs={{8,16},{16,8},{9,17},{17,9},{10,18},{18,10},{11,19},{19,11},{12,20... | collective-permute-start | bytes 589832 | tf_op jit(solution)/shard_map/ppermute | solution.py:371
  33.2 2.3 %collective-permute-start.7 = (f32[96,256]{1,0:T(8,128)S(1)}, f32[96,256]{1,0:T(8,128)S(1)}, u32[]{:S(2)}, u32[]{:S(2)}) collective-permute-start(f32[96,256]{1,0:T(8,128)S(1)} %project.8.refs_3_.refs_4_), channel_id=1, source_target_pairs={{8,16},{16,8},{9,17},{17,9},{10,18},{18,10},{11,19},{19,11},{12,20... | collective-permute-start | bytes 294920 | tf_op jit(solution)/shard_map/ppermute | solution.py:371
  34.8 0.7 collective-permute-start.8
  35.4 15.8 %collective-permute-start.9 = (f32[384,256]{1,0:T(8,128)S(1)}, f32[384,256]{1,0:T(8,128)S(1)}, u32[]{:S(2)}, u32[]{:S(2)}) collective-permute-start(f32[384,256]{1,0:T(8,128)S(1)} %get-tuple-element.107), channel_id=1, source_target_pairs={{0,24},{24,0},{1,25},{25,1},{2,26},{26,2},{3,27},{27,3},{4,28},{28... | collective-permute-start | bytes 1179656 | tf_op jit(solution)/shard_map/ppermute | solution.py:371
  41.1 16.8 %collective-permute-start.10 = (f32[384,256]{1,0:T(8,128)S(1)}, f32[384,256]{1,0:T(8,128)S(1)}, u32[]{:S(2)}, u32[]{:S(2)}) collective-permute-start(f32[384,256]{1,0:T(8,128)S(1)} %get-tuple-element.119), channel_id=1, source_target_pairs={{0,24},{24,0},{1,25},{25,1},{2,26},{26,2},{3,27},{27,3},{4,28},{28... | collective-permute-start | bytes 1179656 | tf_op jit(solution)/shard_map/ppermute | solution.py:371
  52.8 6.7 %collective-permute-start.12 = (f32[128,768]{1,0:T(8,128)S(1)}, f32[128,768]{1,0:T(8,128)S(1)}, u32[]{:S(2)}, u32[]{:S(2)}) collective-permute-start(f32[128,768]{1,0:T(8,128)S(1)} %get-tuple-element.120), channel_id=1, source_target_pairs={{0,2},{2,0},{4,6},{6,4},{1,3},{3,1},{5,7},{7,5},{8,10},{10,8},{12,... | collective-permute-start | bytes 1179656 | tf_op jit(solution)/shard_map/ppermute | solution.py:375
  52.8 10.0 %copy-start.4 = (f32[2,192,256]{2,1,0:T(8,128)S(1)}, f32[2,192,256]{2,1,0:T(8,128)}, u32[]{:S(2)}) copy-start(f32[2,192,256]{2,1,0:T(8,128)} %first_ref.1) | copy-start | bytes 1179652
  52.8 10.0 %copy-start.5 = (f32[2,192,256]{2,1,0:T(8,128)S(1)}, f32[2,192,256]{2,1,0:T(8,128)}, u32[]{:S(2)}) copy-start(f32[2,192,256]{2,1,0:T(8,128)} %second_ref.1) | copy-start | bytes 1179652
  52.9 8.7 %collective-permute-start.11 = (f32[128,768]{1,0:T(8,128)S(1)}, f32[128,768]{1,0:T(8,128)S(1)}, u32[]{:S(2)}, u32[]{:S(2)}) collective-permute-start(f32[128,768]{1,0:T(8,128)S(1)} %get-tuple-element.133), channel_id=1, source_target_pairs={{0,2},{2,0},{4,6},{6,4},{1,3},{3,1},{5,7},{7,5},{8,10},{10,8},{12,... | collective-permute-start | bytes 1179656 | tf_op jit(solution)/shard_map/ppermute | solution.py:375
  59.4 39.4 %copy-start.3 = (bf16[2,768,768]{2,1,0:T(8,128)(2,1)S(1)}, bf16[2,768,768]{2,1,0:T(8,128)(2,1)}, u32[]{:S(2)}) copy-start(bf16[2,768,768]{2,1,0:T(8,128)(2,1)} %weights_ref.3) | copy-start | bytes 7077892
  60.0 12.9 %collective-permute-start.16 = (f32[64,768]{1,0:T(8,128)S(1)}, f32[64,768]{1,0:T(8,128)S(1)}, u32[]{:S(2)}, u32[]{:S(2)}) collective-permute-start(f32[64,768]{1,0:T(8,128)S(1)} %get-tuple-element.145), channel_id=1, source_target_pairs={{0,4},{2,6},{4,0},{6,2},{1,5},{3,7},{5,1},{7,3},{8,12},{10,14},{12... | collective-permute-start | bytes 589832 | tf_op jit(solution)/shard_map/ppermute | solution.py:379
  62.1 12.4 %collective-permute-start.15 = (f32[64,768]{1,0:T(8,128)S(1)}, f32[64,768]{1,0:T(8,128)S(1)}, u32[]{:S(2)}, u32[]{:S(2)}) collective-permute-start(f32[64,768]{1,0:T(8,128)S(1)} %get-tuple-element.144), channel_id=1, source_target_pairs={{0,4},{2,6},{4,0},{6,2},{1,5},{3,7},{5,1},{7,3},{8,12},{10,14},{12... | collective-permute-start | bytes 589832 | tf_op jit(solution)/shard_map/ppermute | solution.py:379
  64.5 19.8 %collective-permute-start.14 = (bf16[2,208,256]{2,1,0:T(8,128)(2,1)S(1)}, bf16[2,208,256]{2,1,0:T(8,128)(2,1)S(1)}, u32[]{:S(2)}, u32[]{:S(2)}) collective-permute-start(bf16[2,208,256]{2,1,0:T(8,128)(2,1)S(1)} %get-tuple-element.172.d0_ref), channel_id=1, source_target_pairs={{0,8},{8,0},{16,24},{24,16},{1,9},{9,1},{17,25},{25,17},{2,10},{10... | collective-permute-start | bytes 638984 | tf_op jit(solution)/shard_map/ppermute | solution.py:371
  70.5 13.8 %collective-permute-start.13 = (bf16[2,208,256]{2,1,0:T(8,128)(2,1)S(1)}, bf16[2,208,256]{2,1,0:T(8,128)(2,1)S(1)}, u32[]{:S(2)}, u32[]{:S(2)}) collective-permute-start(bf16[2,208,256]{2,1,0:T(8,128)(2,1)S(1)} %get-tuple-element.172.d0_ref), channel_id=1, source_target_pairs={{0,24},{8,16},{16,8},{24,0},{1,25},{9,17},{17,9},{25,1},{2,26},{10... | collective-permute-start | bytes 638984 | tf_op jit(solution)/shard_map/ppermute | solution.py:371
  73.5 9.0 %collective-permute-start.18 = (f32[32,768]{1,0:T(8,128)S(1)}, f32[32,768]{1,0:T(8,128)S(1)}, u32[]{:S(2)}, u32[]{:S(2)}) collective-permute-start(f32[32,768]{1,0:T(8,128)S(1)} %get-tuple-element.153), channel_id=1, source_target_pairs={{0,8},{8,0},{16,24},{24,16},{1,9},{9,1},{17,25},{25,17},{2,10},{10... | collective-permute-start | bytes 294920 | tf_op jit(solution)/shard_map/ppermute | solution.py:371
  75.1 9.3 %collective-permute-start.17 = (f32[32,768]{1,0:T(8,128)S(1)}, f32[32,768]{1,0:T(8,128)S(1)}, u32[]{:S(2)}, u32[]{:S(2)}) collective-permute-start(f32[32,768]{1,0:T(8,128)S(1)} %get-tuple-element.152), channel_id=1, source_target_pairs={{0,8},{8,0},{16,24},{24,16},{1,9},{9,1},{17,25},{25,17},{2,10},{10... | collective-permute-start | bytes 294920 | tf_op jit(solution)/shard_map/ppermute | solution.py:371
  84.4 14.5 %collective-permute-start.19 = (bf16[2,208,256]{2,1,0:T(8,128)(2,1)S(1)}, bf16[2,208,256]{2,1,0:T(8,128)(2,1)S(1)}, u32[]{:S(2)}, u32[]{:S(2)}) collective-permute-start(bf16[2,208,256]{2,1,0:T(8,128)(2,1)S(1)} %collective-permute-done.13.d3_ref), channel_id=1, source_target_pairs={{0,8},{8,0},{16,24},{24,16},{1,9},{9,1},{17,25},{25,17},{2,10},{10... | collective-permute-start | bytes 638984 | tf_op jit(solution)/shard_map/ppermute | solution.py:371
  86.1 10.5 %collective-permute-start.21 = (f32[32,768]{1,0:T(8,128)S(1)}, f32[32,768]{1,0:T(8,128)S(1)}, u32[]{:S(2)}, u32[]{:S(2)}) collective-permute-start(f32[32,768]{1,0:T(8,128)S(1)} %add.18), channel_id=1, source_target_pairs={{0,24},{8,16},{16,8},{24,0},{1,25},{9,17},{17,9},{25,1},{2,26},{10... | collective-permute-start | bytes 294920 | tf_op jit(solution)/shard_map/ppermute | solution.py:371
  88.5 10.2 %collective-permute-start.20 = (f32[32,768]{1,0:T(8,128)S(1)}, f32[32,768]{1,0:T(8,128)S(1)}, u32[]{:S(2)}, u32[]{:S(2)}) collective-permute-start(f32[32,768]{1,0:T(8,128)S(1)} %add.19), channel_id=1, source_target_pairs={{0,24},{8,16},{16,8},{24,0},{1,25},{9,17},{17,9},{25,1},{2,26},{10... | collective-permute-start | bytes 294920 | tf_op jit(solution)/shard_map/ppermute | solution.py:371
  96.7 5.7 %collective-permute-start.23 = (f32[32,768]{1,0:T(8,128)S(1)}, f32[32,768]{1,0:T(8,128)S(1)}, u32[]{:S(2)}, u32[]{:S(2)}) collective-permute-start(f32[32,768]{1,0:T(8,128)S(1)} %add.20), channel_id=1, source_target_pairs={{0,8},{8,0},{16,24},{24,16},{1,9},{9,1},{17,25},{25,17},{2,10},{10... | collective-permute-start | bytes 294920 | tf_op jit(solution)/shard_map/ppermute | solution.py:371
  98.7 4.7 %collective-permute-start.22 = (f32[32,768]{1,0:T(8,128)S(1)}, f32[32,768]{1,0:T(8,128)S(1)}, u32[]{:S(2)}, u32[]{:S(2)}) collective-permute-start(f32[32,768]{1,0:T(8,128)S(1)} %add.21), channel_id=1, source_target_pairs={{0,8},{8,0},{16,24},{24,16},{1,9},{9,1},{17,25},{25,17},{2,10},{10... | collective-permute-start | bytes 294920 | tf_op jit(solution)/shard_map/ppermute | solution.py:371
  103.4 5.7 %collective-permute-start.25 = (f32[64,768]{1,0:T(8,128)S(1)}, f32[64,768]{1,0:T(8,128)S(1)}, u32[]{:S(2)}, u32[]{:S(2)}) collective-permute-start(f32[64,768]{1,0:T(8,128)S(1)} %constant_dynamic-update-slice_fusion.2.refs_2_), channel_id=1, source_target_pairs={{0,4},{2,6},{4,0},{6,2},{1,5},{3,7},{5,1},{7,3},{8,12},{10,14},{12... | collective-permute-start | bytes 589832 | tf_op jit(solution)/shard_map/ppermute | solution.py:379
  105.0 6.3 %collective-permute-start.24 = (f32[64,768]{1,0:T(8,128)S(1)}, f32[64,768]{1,0:T(8,128)S(1)}, u32[]{:S(2)}, u32[]{:S(2)}) collective-permute-start(f32[64,768]{1,0:T(8,128)S(1)} %constant_dynamic-update-slice_fusion.refs_0_), channel_id=1, source_target_pairs={{0,4},{2,6},{4,0},{6,2},{1,5},{3,7},{5,1},{7,3},{8,12},{10,14},{12... | collective-permute-start | bytes 589832 | tf_op jit(solution)/shard_map/ppermute | solution.py:379
  116.0 2.4 %collective-permute-start.26 = (f32[768,256]{1,0:T(8,128)S(1)}, f32[768,256]{1,0:T(8,128)S(1)}, u32[]{:S(2)}, u32[]{:S(2)}) collective-permute-start(f32[768,256]{1,0:T(8,128)S(1)} %get-tuple-element.180), channel_id=1, source_target_pairs={{0,2},{2,0},{4,6},{6,4},{1,3},{3,1},{5,7},{7,5},{8,10},{10,8},{12,... | collective-permute-start | bytes 2359304 | tf_op jit(solution)/shard_map/ppermute | solution.py:375

commit v3 on v0

--- a/solution.py
+++ b/solution.py
@@ -1,6 +1,10 @@
+import functools
+
 import jax
 import jax.numpy as jnp
 from jax import lax
+from jax.experimental import pallas as pl
+from jax.experimental.pallas import tpu as pltpu
 from jax.sharding import PartitionSpec as P
 
 NS_ITERS = 3
@@ -33,7 +37,16 @@
     return (moment_one, moment_two, corrected_one / (jnp.sqrt(corrected_two) + adam_eps))
 
 
-def body(grads, weights, basis, first_moment, second_moment):
+def newton_schulz(power, width):
+    norms = jnp.sqrt(jnp.sum(power * power, axis=(1, 2)))
+    iterate = power / (norms + norm_eps)[:, None, None]
+    for sweep in range(NS_ITERS):
+        gram_matrix = jnp.einsum("ldr,lds->lrs", iterate, iterate, precision=highest)
+        iterate = newton_step(iterate, gram_matrix)
+    return width**0.5 * iterate
+
+
+def general_body(grads, weights, basis, first_moment, second_moment):
     width = basis.shape[1]
     scale_factor = width ** (-0.5)
     local_grads = grads[0]
@@ -52,16 +65,478 @@
     fresh_rows = (current.astype(jnp.float32) - factor * update).astype(jnp.bfloat16)
     weights_next = lax.all_gather(fresh_rows, "shard", axis=1, tiled=True)
     whole = lax.psum(power, ("shard", "tensor"))
-    norms = jnp.sqrt(jnp.sum(whole * whole, axis=(1, 2)))
-    iterate = whole / (norms + norm_eps)[:, None, None]
-    for sweep in range(NS_ITERS):
-        gram_matrix = jnp.einsum("ldr,lds->lrs", iterate, iterate, precision=highest)
-        iterate = newton_step(iterate, gram_matrix)
-    basis_next = width**0.5 * iterate
+    basis_next = newton_schulz(whole, width)
     return (weights_next, basis_next, moment_one, moment_two)
 
 
+PLAIN = ((1,), (0,))
+BOTH_LAST = ((1,), (1,))
+
+
+class Place:
+    def __init__(self):
+        tensor, self.z = lax.axis_index("tensor"), lax.axis_index("shard")
+        self.core, self.y = lax.rem(tensor, 2), lax.div(tensor, 2)
+        self.inner = lax.div(lax.rem(self.z + 1, 4), 2)
+
+    def keeps(self, j):
+        return jnp.where(self.inner == 1, 1 + j, 3 * j)
+
+    def gives(self, j):
+        return jnp.where(self.inner == 1, 3 * j, 1 + j)
+
+    def layer(self, turn):
+        return self.core if turn else 1 - self.core
+
+    def piece(self, h, k, piece):
+        return pl.multiple_of((h * 4 + (self.y ^ (k // 2)) * 2 + (self.inner ^ (k % 2))) * piece, piece)
+
+
+def split(x):
+    high = x.astype(jnp.bfloat16)
+    return high, (x - high.astype(jnp.float32)).astype(jnp.bfloat16)
+
+
+def dot3(a, b, dims=PLAIN):
+    dot = lambda p, q: lax.dot_general(p, q, (dims, ((), ())), preferred_element_type=jnp.float32)
+    return dot(a[0], b[0]) + (dot(a[0], b[1]) + dot(a[1], b[0]))
+
+
+def params(megabytes):
+    return pltpu.CompilerParams(vmem_limit_bytes=megabytes * 2**20)
+
+
+def in_vmem(*arrays):
+    return [pltpu.with_memory_space_constraint(x, pltpu.VMEM) for x in arrays]
+
+
+def local_call(kernel, outs, *operands, name, scratch=(), flops=0):
+    vmem = pl.BlockSpec(memory_space=pltpu.VMEM)
+    return pl.pallas_call(
+        kernel,
+        out_shape=[pltpu.VMEM(shape, dtype) for shape, dtype in outs],
+        in_specs=[vmem] * len(operands),
+        out_specs=[vmem] * len(outs),
+        scratch_shapes=scratch,
+        compiler_params=params(12),
+        cost_estimate=cost(flops),
+        name=name,
+    )(*in_vmem(*operands))
+
+
+def cost(flops):
+    return pl.CostEstimate(flops=int(flops), bytes_accessed=0, transcendentals=0) if flops else None
+
+
+SPAN = 250.0
+
+
+def encode(x):
+    bound = jnp.max(jnp.abs(x), axis=0, keepdims=True)
+    bound = (bound * 1.01 + 1e-30).astype(jnp.bfloat16).astype(jnp.float32)
+    size = jnp.exp2(jnp.abs(x) * (SPAN / bound) - SPAN / 2)
+    code = jnp.where(x < 0, -size, size)
+    return code.astype(jnp.bfloat16), jnp.broadcast_to(bound, (16, x.shape[1])).astype(jnp.bfloat16)
+
+
+def decode(code, bound):
+    code, bound = code.astype(jnp.float32), bound[0:1].astype(jnp.float32)
+    size = (jnp.log2(jnp.abs(code)) + SPAN / 2) * (bound / SPAN)
+    return jnp.where(code < 0, -size, size)
+
+
+def give_kernel(rows, grads_ref, *rest):
+    outs, sems = rest[:-1], rest[-1]
+    place = Place()
+    copies = []
+    for i in range(4):
+        start = pl.multiple_of(place.gives(i % 2) * rows, rows)
+        out = outs[0].at[pl.ds(i * rows, rows)] if i < 2 else outs[i - 1]
+        copies.append(pltpu.make_async_copy(grads_ref.at[0, place.layer(i // 2), pl.ds(start, rows)], out, sems.at[i]))
+    for copy in copies:
+        copy.start()
+    for copy in copies:
+        copy.wait()
+
+
+def give_blocks(grads, rows):
+    heights = (2 * rows, rows, rows)
+    return pl.pallas_call(
+        functools.partial(give_kernel, rows),
+        out_shape=[pltpu.VMEM((height, grads.shape[3]), grads.dtype) for height in heights],
+        in_specs=[pl.BlockSpec(memory_space=pltpu.HBM)],
+        out_specs=[pl.BlockSpec(memory_space=pltpu.VMEM)] * len(heights),
+        scratch_shapes=[pltpu.SemaphoreType.DMA((4,))],
+        compiler_params=params(4),
+        name="give_blocks",
+    )(pltpu.with_memory_space_constraint(grads, pltpu.HBM))
+
+
+def prepare_kernel(basis_hbm, high_ref, low_ref, buffer, sems):
+    layers = buffer.shape[0]
+    copies = [pltpu.make_async_copy(basis_hbm.at[layer], buffer.at[layer], sems.at[layer]) for layer in range(layers)]
+    for copy in copies:
+        copy.start()
+    for layer, copy in enumerate(copies):
+        copy.wait()
+        high_ref[layer], low_ref[layer] = split(buffer[layer])
+
+
+def prepare_basis(basis):
+    layers = basis.shape[0]
+    vmem = pl.BlockSpec(memory_space=pltpu.VMEM)
+    return pl.pallas_call(
+        prepare_kernel,
+        out_shape=[pltpu.VMEM(basis.shape, jnp.bfloat16)] * 2,
+        in_specs=[pl.BlockSpec(memory_space=pltpu.HBM)],
+        out_specs=[vmem] * 2,
+        scratch_shapes=[pltpu.VMEM(basis.shape, jnp.float32), pltpu.SemaphoreType.DMA((layers,))],
+        compiler_params=params(12),
+        cost_estimate=cost(3e9),
+        name="prepare_basis",
+    )(pltpu.with_memory_space_constraint(basis, pltpu.HBM))
+
+
+def kept_sum(place, grads_ref, other, turn, j, rows):
+    start = pl.multiple_of(place.keeps(j) * rows, rows)
+    kept = grads_ref[0, place.layer(turn), pl.ds(start, rows)]
+    return kept.astype(jnp.float32) + other.astype(jnp.float32)
+
+
+def project_kernel(turn, blocks, rows, grads_ref, other_ref, high_ref, low_ref, out_ref, code_ref):
+    place = Place()
+    basis = high_ref[place.layer(turn)], low_ref[place.layer(turn)]
+    for i, j in enumerate(blocks):
+        total = kept_sum(place, grads_ref, other_ref[i * rows : (i + 1) * rows], turn, j, rows)
+        projected = dot3(split(total), basis)
+        out_ref[i * rows : (i + 1) * rows] = projected
+        row = i * (rows + 16)
+        code_ref[row : row + rows], code_ref[row + rows : row + rows + 16] = encode(projected)
+
+
+def project(grads, other, basis, turn, blocks):
+    rank, rows = basis[0].shape[2], other.shape[0] // len(blocks)
+    kernel = functools.partial(project_kernel, turn, blocks, rows)
+    outs = [((len(blocks) * rows, rank), jnp.float32), ((len(blocks) * (rows + 16), rank), jnp.bfloat16)]
+    return local_call(kernel, outs, grads, other, *basis, name="project")
+
+
+HALVES = 2
+
+
+def power_kernel(turn, scale, grads_ref, first_ref, second_ref, *refs):
+    place = Place()
+    parts = 1 + turn
+    others, partials, received, rest = refs[:parts], refs[parts : 2 * parts], refs[2 * parts : 3 * parts], refs[3 * parts :]
+    rest = rest[3 * turn :]
+    half0_ref, half1_ref, one_ref, two_ref, code_ref, product, one, two, sems = rest
+    layers, rows = first_ref.shape[0], first_ref.shape[1]
+    sums, summed = [], []
+    for j in range(2):
+        part, row = (0, j) if turn == 0 else (j, 0)
+        block, coded = pl.ds(row * rows, rows), row * (rows + 16)
+        summed.append(kept_sum(place, grads_ref, others[part][block], turn, j, rows))
+        code, bound = received[part][coded : coded + rows], received[part][coded + rows : coded + rows + 16]
+        sums.append(partials[part][block] + decode(code, bound))
+    layer = place.layer(turn)
+    reduced = scale * jnp.where(place.z < 2, sums[0], sums[1])
+    one[...], two[...], direction = adam_direction(reduced, first_ref[layer], second_ref[layer])
+    copies = [pltpu.make_async_copy(x, out.at[layer], sems.at[i]) for i, (x, out) in enumerate(((one, one_ref), (two, two_ref)))]
+    for copy in copies:
+        copy.start()
+    if turn == 0:
+        code_ref[0:rows], code_ref[rows:] = encode(direction)
+    else:
+        code_ref[1 - layer] = refs[3 * parts + 2][...]
+        code_ref[layer, 0:rows], code_ref[layer, rows:] = encode(direction)
+    product[...] = dot3(split(jnp.concatenate(sums).T), split(jnp.concatenate(summed)))
+    piece = product.shape[0] // (4 * HALVES)
+    for h in range(HALVES):
+        for k in range(4):
+            (half0_ref, half1_ref)[h][pl.ds(k * piece, piece)] = product[pl.ds(place.piece(h, k, piece), piece)]
+    for copy in copies:
+        copy.wait()
+
+
+def power_product(grads, first_moment, second_moment, others, partials, received, turn, scale, before=()):
+    width = grads.shape[3]
+    layers, rows, rank = first_moment.shape
+    vmem, anywhere = pl.BlockSpec(memory_space=pltpu.VMEM), pl.BlockSpec(memory_space=pl.ANY)
+    operands = in_vmem(grads, first_moment, second_moment, *others, *partials, *received)
+    count = len(operands)
+    return pl.pallas_call(
+        functools.partial(power_kernel, turn, scale),
+        out_shape=[pltpu.VMEM((rank // HALVES, width), jnp.float32)] * HALVES
+        + [jax.ShapeDtypeStruct(first_moment.shape, jnp.float32)] * 2
+        + [pltpu.VMEM((layers, rows + 16, rank) if turn else (rows + 16, rank), jnp.bfloat16)],
+        in_specs=[vmem] * count + [anywhere, anywhere, vmem][: len(before)],
+        out_specs=[vmem] * HALVES + [anywhere] * 2 + [vmem],
+        scratch_shapes=[pltpu.VMEM((rank, width), jnp.float32)]
+        + [pltpu.VMEM((rows, rank), jnp.float32)] * 2
+        + [pltpu.SemaphoreType.DMA((2,))],
+        input_output_aliases={count: HALVES, count + 1: HALVES + 1} if before else {},
+        compiler_params=params(12),
+        cost_estimate=cost(5e9 * turn),
+        name="power",
+    )(*operands, *before[:2], *in_vmem(*before[2:]))
+
+
+def add_split_kernel(own_ref, received_ref, keep_ref, give_ref):
+    half = keep_ref.shape[0]
+    keep_ref[...] = own_ref[0:half] + received_ref[0:half]
+    give_ref[...] = own_ref[half:] + received_ref[half:]
+
+
+def add_split(own, received):
+    outs = [((own.shape[0] // 2, own.shape[1]), jnp.float32)] * 2
+    return local_call(add_split_kernel, outs, own, received, name="add_split", flops=1e9)
+
+
+def add_kernel(own_ref, received_ref, out_ref):
+    out_ref[...] = own_ref[...] + received_ref[...]
+
+
+def join_kernel(own_ref, received_ref, out_ref):
+    half = own_ref.shape[0]
+    out_ref[0:half] = own_ref[...]
+    out_ref[half:] = received_ref[...]
+
+
+def add(own, received):
+    return local_call(add_kernel, [(own.shape, jnp.float32)], own, received, name="add")[0]
+
+
+def join(own, received):
+    outs = [((2 * own.shape[0], own.shape[1]), jnp.float32)]
+    return local_call(join_kernel, outs, own, received, name="join")[0]
+
+
+def newton_schulz_kernel(*refs):
+    place = Place()
+    parts, (out_ref, result_ref, power_ref, sems) = refs[:-4], refs[-4:]
+    piece = parts[0].shape[0] // 2
+    for h in range(HALVES):
+        for k in range(4):
+            part = parts[2 * h + k // 2]
+            power_ref[pl.ds(place.piece(h, k, piece), piece)] = part[pl.ds(k % 2 * piece, piece)]
+    power = power_ref[...]
+    rank, width = power.shape
+    unscaled = split(power)
+    scale = 1.0 / (jnp.sqrt(jnp.sum(power * power)) + norm_eps)
+    gram = dot3(unscaled, unscaled, BOTH_LAST) * scale * scale
+    ident = lax.broadcasted_iota(jnp.int32, gram.shape, 0) == lax.broadcasted_iota(jnp.int32, gram.shape, 1)
+    diagonal = jnp.where(ident, coeff_a, 0.0)
+    product = None
+    for sweep in range(NS_ITERS - 1):
+        g = split(gram)
+        factor = diagonal + coeff_b * gram + coeff_c * dot3(g, g)
+        f = split(factor)
+        gram = dot3(split(dot3(f, g)), f)
+        product = f if product is None else split(dot3(product, f))
+    iterate = split(dot3(product, unscaled))
+    g = split(gram)
+    last = split((diagonal + coeff_b * gram + coeff_c * dot3(g, g)) * (scale * width**0.5))
+    copies = []
+    for i in range(width // rank):
+        columns = slice(i * rank, (i + 1) * rank)
+        result_ref[columns] = dot3(last, [term[:, columns] for term in iterate]).T
+        copies.append(pltpu.make_async_copy(result_ref.at[columns], out_ref.at[place.core, columns], sems.at[i]))
+        copies[-1].start()
+    for copy in copies:
+        copy.wait()
+
+
+def newton_schulz_power(layers, *parts):
+    rank, width = 2 * HALVES * parts[0].shape[0], parts[0].shape[1]
+    vmem = pl.BlockSpec(memory_space=pltpu.VMEM)
+    return pl.pallas_call(
+        newton_schulz_kernel,
+        out_shape=[jax.ShapeDtypeStruct((layers, width, rank), jnp.float32), pltpu.VMEM((width, rank), jnp.float32)],
+        in_specs=[vmem] * len(parts),
+        out_specs=[pl.BlockSpec(memory_space=pl.ANY), vmem],
+        scratch_shapes=[pltpu.VMEM((rank, width), jnp.float32), pltpu.SemaphoreType.DMA((width // rank,))],
+        compiler_params=params(12),
+        cost_estimate=cost(4e9),
+        name="newton_schulz",
+    )(*in_vmem(*parts))
+
+
+def put_layer_kernel(layer_ref, whole_ref, out_ref, sems):
+    count = sems.shape[0]
+    rows = layer_ref.shape[0] // count
+    copies = []
+    for i in range(count):
+        part = pl.ds(i * rows, rows)
+        copies.append(pltpu.make_async_copy(layer_ref.at[part], out_ref.at[1 - Place().core, part], sems.at[i]))
+    for copy in copies:
+        copy.start()
+    for copy in copies:
+        copy.wait()
+
+
+def put_layer(layer, whole):
+    hbm = pl.BlockSpec(memory_space=pl.ANY)
+    return pl.pallas_call(
+        put_layer_kernel,
+        out_shape=jax.ShapeDtypeStruct(whole.shape, whole.dtype),
+        in_specs=[pl.BlockSpec(memory_space=pltpu.VMEM), hbm],
+        out_specs=hbm,
+        scratch_shapes=[pltpu.SemaphoreType.DMA((4,))],
+        input_output_aliases={1: 0},
+        compiler_params=params(4),
+        name="put_layer",
+    )(*in_vmem(layer), whole)
+
+
+def update_kernel(factor, index_ref, weights_ref, basis_ref, *refs):
+    directions, (out_ref, high, low) = refs[:2], refs[-3:]
+    k = pl.program_id(1)
+
+    @pl.when(k == 0)
+    def _():
+        high[...], low[...] = split(basis_ref[0].T)
+
+    for step, direction in enumerate(directions):
+
+        @pl.when(k == step)
+        def _(direction=direction):
+            rows = out_ref.shape[1]
+            exact = decode(direction[0, 0:rows], direction[0, rows:])
+            update = dot3(split(exact), (high[...], low[...]))
+            out_ref[0] = (weights_ref[0].astype(jnp.float32) - factor * update).astype(out_ref.dtype)
+
+
+def update_weights(index, weights, basis, blocks, directions, factor, before=()):
+    layers, height, width = weights.shape
+    rank, rows = basis.shape[2], height // 4
+    row_block = pl.BlockSpec((1, rows, width), lambda l, k, index: (l, index[0] ^ (blocks[0] + k * (blocks[1] - blocks[0])), 0))
+    layer_block = lambda a, b: pl.BlockSpec((1, a, b), lambda l, k, index: (l, 0, 0))
+    return pl.pallas_call(
+        functools.partial(update_kernel, factor),
+        out_shape=jax.ShapeDtypeStruct(weights.shape, weights.dtype),
+        grid_spec=pltpu.PrefetchScalarGridSpec(
+            num_scalar_prefetch=1,
+            grid=(layers, 2),
+            in_specs=[row_block, layer_block(width, rank)]
+            + [layer_block(rows + 16, rank)] * 2
+            + [pl.BlockSpec(memory_space=pl.ANY)] * len(before),
+            out_specs=row_block,
+            scratch_shapes=[pltpu.VMEM((rank, width), jnp.bfloat16)] * 2,
+        ),
+        input_output_aliases={5: 0} if before else {},
+        compiler_params=params(12),
+        cost_estimate=cost(3e9),
+        name="update_weights",
+    )(index, pltpu.with_memory_space_constraint(weights, pltpu.HBM), basis, *directions, *before)
+
+
+def xor_pairs(k):
+    return [(i, i ^ k) for i in range(4)]
+
+
+def over_z(x, k):
+    return lax.ppermute(x, "shard", xor_pairs(k))
+
+
+def over_core(x):
+    return lax.ppermute(x, "tensor", xor_pairs(1))
+
+
+def over_y(x):
+    return lax.ppermute(x, "tensor", xor_pairs(2))
+
+
+class Order:
+    def __init__(self):
+        self.last = None
+
+    def step(self, *operands):
+        if self.last is None:
+            return operands
+        return lax.optimization_barrier(tuple(operands) + (self.last,))[:-1]
+
+    def through(self, result):
+        self.last = result
+        return result
+
+
+def line_body(grads, weights, basis, first_moment, second_moment):
+    width = basis.shape[1]
+    scale_factor = width ** (-0.5)
+    layers, rows = grads.shape[1], first_moment.shape[1]
+    order = Order()
+
+    others = [over_z(block, 1) for block in give_blocks(grads, rows)]
+    high, low = prepare_basis(basis)
+    partials, received = [], []
+
+    def exchange(i, turn, blocks, *awaited):
+        other, *awaited = order.step(others[i], *awaited)
+        partial, code = project(grads, other, (high, low), turn, blocks)
+        partials.append(order.through(partial))
+        received.append(over_z(code, 3))
+        return awaited
+
+    def product(turn, *before):
+        some = slice(1, 3) if turn else slice(0, 1)
+        operands = order.step(*others[some], *partials[some], *received[some])
+        n = 1 + turn
+        *halves, one, two, code = power_product(
+            grads, first_moment, second_moment, operands[:n], operands[n : 2 * n], operands[2 * n :], turn, scale_factor, before
+        )
+        order.through(halves[0])
+        return halves, (one, two, code)
+
+    def scatter(over, x, received):
+        keep, give = add_split(*order.step(x, received))
+        return order.through(keep), over(give)
+
+    def total(over, x, received):
+        x = order.through(add(*order.step(x, received)))
+        return x, over(x)
+
+    def gather(over, x, received):
+        x = order.through(join(*order.step(x, received)))
+        return x, over(x)
+
+    next_z = lambda x: over_z(x, 1)
+    opposite_z = lambda x: over_z(x, 3)
+
+    exchange(0, 0, (0, 1))
+    exchange(1, 1, (0,))
+    gifts, before = product(0)
+    gifts = [over_core(gift) for gift in gifts]
+    (received[1],) = exchange(2, 1, (1,), received[1])
+    parts, (moment_one, moment_two, code) = product(1, *before)
+    parts = [scatter(over_y, part, gift) for part, gift in zip(parts, gifts)]
+    (code,) = order.step(code)
+    near, opposite = next_z(code), opposite_z(code)
+    first = scatter(next_z, *parts[0])
+    near, opposite, *second = order.step(near, opposite, *parts[1])
+    parts = [first, scatter(next_z, *second)]
+    parts = [total(opposite_z, *part) for part in parts]
+    parts = [total(next_z, *part) for part in parts]
+    last = next_z(order.step(opposite)[0])
+    parts = [gather(over_y, *part) for part in parts]
+    index = lax.axis_index("shard").astype(jnp.int32)[None]
+    factor = learn_rate * galore_scale * scale_factor
+    update = functools.partial(update_weights, index, weights, basis)
+    weights_next = order.through(update((0, 1), order.step(code, near), factor))
+    last, *parts = order.step(last, *[x for part in parts for x in part])
+    basis_next, own = newton_schulz_power(layers, *parts)
+    order.through(own)
+    other = over_core(own)
+    weights_next = order.through(update((2, 3), order.step(last, opposite), factor, (weights_next,)))
+    basis_next = put_layer(*order.step(other, basis_next))
+    return (weights_next, basis_next, moment_one, moment_two)
+
+
 def solution(mesh):
+    line = mesh.shape["shard"] == 4 and mesh.shape["tensor"] == 4
+
+    def body(grads, *others):
+        return (line_body if line and grads.shape[1] == 2 else general_body)(grads, *others)
+
     return jax.shard_map(
         body,
         mesh=mesh,

time: 263 us -> 95.7 us (0.36)
  waiting for transfers between devices: 215 us -> 45.6 us
  starting transfers between devices: 0.3 us -> 27.2 us
  matrix products: 21.9 us -> 0 us
  Pallas kernels: 0 us -> 21.7 us
  between operations: 13.9 us -> 0.84 us
  other arithmetic: 6.11 us -> 0 us
  local copies, waits for them, and re-layouts: 4.91 us -> 0.02 us
    psum x1 -> x0, waiting for transfers between devices: 92.2 us -> none  [body(): whole = lax.psum(power, ('shard', 'tensor'))]
    reduce_scatter x1 -> x0, waiting for transfers between devices: 88.1 us -> none  [body(): lax.psum_scatter(local_grads.astype(jnp.float32), 'shard', scatter_dimens...]
    ppermute x0 -> x22, waiting for transfers between devices: none -> 45.6 us  [the longest x15 39.7 us: over_z(): return lax.ppermute(x, 'shard', xor_pairs(k))]
    all_gather x1 -> x0, waiting for transfers between devices: 35.1 us -> none  [body(): weights_next = lax.all_gather(fresh_rows, 'shard', axis=1, tiled=True)]
    ppermute x0 -> x22, starting transfers between devices: none -> 27.2 us  [the longest x15 23.5 us: over_z(): return lax.ppermute(x, 'shard', xor_pairs(k))]
    dot_general x12 -> x0, matrix products: 21.9 us -> none  [the longest x3 5.53 us: newton_step(): jnp.einsum('ldr,lrs->lds', iterate, mixing, precision=highest)]
    pallas_call x0 -> x21, Pallas kernels: none -> 21.7 us  [the longest x2 8.99 us: update_weights(): pl.pallas_call(functools.partial(update_kernel, factor), out_shape=jax.Sh...]
    unnamed x16 -> x8, local copies, waits for them, and re-layouts: 4.91 us -> 0.02 us
  transfers between devices with their start and end apart: 3 -> 22, of which waited for: 3 -> 14; matrix products, arithmetic and copies ran while one was open for 8% -> 0% of each run, Pallas kernels for 0% -> 16%
where the time goes in v3:
time: 95.7 us; the launch traced here: 95.4 us
  waiting for transfers between devices  45.6 us (48%)
  starting transfers between devices  27.2 us (28%)
  Pallas kernels  21.7 us (23%)
    ppermute x15, waiting for transfers between devices, over_z(): return lax.ppermute(x, 'shard', xor_pairs(k))  39.7 us
    ppermute x15, starting transfers between devices, over_z(): return lax.ppermute(x, 'shard', xor_pairs(k))  23.5 us
    pallas_call x2, Pallas kernels, update_weights(): pl.pallas_call(functools.partial(update_kernel, factor), out_shape=jax.Sh...  8.99 us
    ppermute x4, waiting for transfers between devices, over_y(): return lax.ppermute(x, 'tensor', xor_pairs(2))  5.91 us
    pallas_call x1, Pallas kernels, newton_schulz_power(): pl.pallas_call(newton_schulz_kernel, out_shape=[jax.ShapeDtypeStruct((lay...  4.24 us
    ppermute x4, starting transfers between devices, over_y(): return lax.ppermute(x, 'tensor', xor_pairs(2))  3.12 us
    pallas_call x2, Pallas kernels, power_product(): pl.pallas_call(functools.partial(power_kernel, turn, scale), out_shape=[p...  2.77 us
    pallas_call x13, Pallas kernels, local_call(): pl.pallas_call(kernel, out_shape=[pltpu.VMEM(shape, dtype) for shape, dty...  2.02 us
  transfers between devices with their start and end apart: 22, of which 14 were waited for; matrix products, arithmetic and copies ran while one was open for 0% of the time, Pallas kernels for 16%

profile of v3, /device:TPU:0, one launch (start us, length us, event | category | flops | bytes accessed | tf_op | source)
XLA Modules:
  0.0 95.4 jit_solution(936869810724792899)
XLA Ops:
  0.6 1.3 %give_blocks.1 = (bf16[384,768]{1,0:T(8,128)(2,1)S(1)}, bf16[192,768]{1,0:T(8,128)(2,1)S(1)}, bf16[192,768]{1,0:T(8,128)(2,1)S(1)}) custom-call(bf16[1,2,768,768]{3,2,1,0:T(8,128)(2,1)} %grads_ref.11), custom_call_target="tpu_custom_call" | custom-call | tf_op jit(solution)/shard_map/give_blocks/pallas_call | solution.py:164
  1.9 3.1 %collective-permute-start.2 = (bf16[384,768]{1,0:T(8,128)(2,1)S(1)}, bf16[384,768]{1,0:T(8,128)(2,1)S(1)}, u32[]{:S(2)}, u32[]{:S(2)}) collective-permute-start(bf16[384,768]{1,0:T(8,128)(2,1)S(1)} %get-tuple-element.86), channel_id=1, source_target_pairs={{0,8},{8,0},{16,24},{24,16},{1,9},{9,1},{17,25},{25,17},{2,10},{10... | collective-permute-start | bytes 1769480 | tf_op jit(solution)/shard_map/ppermute | solution.py:438
  5.0 0.1 collective-permute-start
  5.1 1.9 %collective-permute-start.1 = (bf16[192,768]{1,0:T(8,128)(2,1)S(1)}, bf16[192,768]{1,0:T(8,128)(2,1)S(1)}, u32[]{:S(2)}, u32[]{:S(2)}) collective-permute-start(bf16[192,768]{1,0:T(8,128)(2,1)S(1)} %get-tuple-element.85), channel_id=1, source_target_pairs={{0,8},{8,0},{16,24},{24,16},{1,9},{9,1},{17,25},{25,17},{2,10},{10... | collective-permute-start | bytes 884744 | tf_op jit(solution)/shard_map/ppermute | solution.py:438
  7.0 1.5 %prepare_basis.1 = (bf16[2,768,256]{2,1,0:T(8,128)(2,1)S(1)}, bf16[2,768,256]{2,1,0:T(8,128)(2,1)S(1)}) custom-call(f32[2,768,256]{2,1,0:T(8,128)} %basis_ref.3), custom_call_target="tpu_custom_call" | custom-call | flops 3000000000 | tf_op jit(solution)/shard_map/prepare_basis/pallas_call | solution.py:188
  8.6 10.6 %collective-permute-done.2.other_ref.refs_0_ = bf16[384,768]{1,0:T(8,128)(2,1)S(1)} collective-permute-done((bf16[384,768]{1,0:T(8,128)(2,1)S(1)}, bf16[384,768]{1,0:T(8,128)(2,1)S(1)}, u32[]{:S(2)}, u32[]{:S(2)}) %collective-permute-start.2) | collective-permute-done | bytes 589856 | tf_op jit(solution)/shard_map/ppermute | solution.py:438
  19.2 0.8 project.3
  20.0 0.0 copy-start.1
  20.0 0.0 copy-start.2
  20.0 4.2 %collective-permute-start.4 = (bf16[416,256]{1,0:T(8,128)(2,1)S(1)}, bf16[416,256]{1,0:T(8,128)(2,1)S(1)}, u32[]{:S(2)}, u32[]{:S(2)}) collective-permute-start(bf16[416,256]{1,0:T(8,128)(2,1)S(1)} %get-tuple-element.93), channel_id=1, source_target_pairs={{0,24},{8,16},{16,8},{24,0},{1,25},{9,17},{17,9},{25,1},{2,26},{10... | collective-permute-start | bytes 638984 | tf_op jit(solution)/shard_map/ppermute | solution.py:438
  24.2 1.3 %collective-permute-done.other_ref.refs_0_ = bf16[192,768]{1,0:T(8,128)(2,1)S(1)} collective-permute-done((bf16[192,768]{1,0:T(8,128)(2,1)S(1)}, bf16[192,768]{1,0:T(8,128)(2,1)S(1)}, u32[]{:S(2)}, u32[]{:S(2)}) %collective-permute-start) | collective-permute-done | bytes 294944 | tf_op jit(solution)/shard_map/ppermute | solution.py:438
  25.5 0.5 project.4
  26.0 4.1 %collective-permute-start.3 = (bf16[208,256]{1,0:T(8,128)(2,1)S(1)}, bf16[208,256]{1,0:T(8,128)(2,1)S(1)}, u32[]{:S(2)}, u32[]{:S(2)}) collective-permute-start(bf16[208,256]{1,0:T(8,128)(2,1)S(1)} %get-tuple-element.92), channel_id=1, source_target_pairs={{0,24},{8,16},{16,8},{24,0},{1,25},{9,17},{17,9},{25,1},{2,26},{10... | collective-permute-start | bytes 319496 | tf_op jit(solution)/shard_map/ppermute | solution.py:438
  30.1 8.8 %collective-permute-done.4.refs_2_ = bf16[416,256]{1,0:T(8,128)(2,1)S(1)} collective-permute-done((bf16[416,256]{1,0:T(8,128)(2,1)S(1)}, bf16[416,256]{1,0:T(8,128)(2,1)S(1)}, u32[]{:S(2)}, u32[]{:S(2)}) %collective-permute-start.4) | collective-permute-done | bytes 213024 | tf_op jit(solution)/shard_map/ppermute | solution.py:438
  39.0 1.4 %power.2 = (f32[128,768]{1,0:T(8,128)S(1)}, f32[128,768]{1,0:T(8,128)S(1)}, f32[2,192,256]{2,1,0:T(8,128)}, f32[2,192,256]{2,1,0:T(8,128)}, bf16[208,256]{1,0:T(8,128)(2,1)S(1)}) custom-call(bf16[1,2,768,768]{3,2,1,0:T(8,128)(2,1)S(1)} %copy-done, f32[2,192,256]{2,1,0:T(8,128)S(1)} %copy-done.1, f32[2,192,256]{2,1,0:T(8,128)S(1)} %copy-done.2, ...), custom_call_target="tpu_custom_call" | custom-call | tf_op jit(solution)/shard_map/power/pallas_call | solution.py:267
  40.4 0.5 project.5
  40.9 1.5 %collective-permute-start.5 = (bf16[208,256]{1,0:T(8,128)(2,1)S(1)}, bf16[208,256]{1,0:T(8,128)(2,1)S(1)}, u32[]{:S(2)}, u32[]{:S(2)}) collective-permute-start(bf16[208,256]{1,0:T(8,128)(2,1)S(1)} %get-tuple-element.101), channel_id=1, source_target_pairs={{0,24},{8,16},{16,8},{24,0},{1,25},{9,17},{17,9},{25,1},{2,26},{10... | collective-permute-start | bytes 319496 | tf_op jit(solution)/shard_map/ppermute | solution.py:438
  42.4 0.5 collective-permute-start.6
  42.9 4.6 %collective-permute-done.5.refs_5_ = bf16[208,256]{1,0:T(8,128)(2,1)S(1)} collective-permute-done((bf16[208,256]{1,0:T(8,128)(2,1)S(1)}, bf16[208,256]{1,0:T(8,128)(2,1)S(1)}, u32[]{:S(2)}, u32[]{:S(2)}) %collective-permute-start.5) | collective-permute-done | bytes 106528 | tf_op jit(solution)/shard_map/ppermute | solution.py:438
  47.5 1.4 %power.3 = (f32[128,768]{1,0:T(8,128)S(1)}, f32[128,768]{1,0:T(8,128)S(1)}, f32[2,192,256]{2,1,0:T(8,128)}, f32[2,192,256]{2,1,0:T(8,128)}, bf16[2,208,256]{2,1,0:T(8,128)(2,1)S(1)}) custom-call(bf16[1,2,768,768]{3,2,1,0:T(8,128)(2,1)S(1)} %copy-done, f32[2,192,256]{2,1,0:T(8,128)S(1)} %copy-done.1, ...), custom_call_target="tpu_custom_call", output_to_operand_aliasing={{2}: (9, {}), {3}: (10, {})} | custom-call | flops 5000000000 | tf_op jit(solution)/shard_map/power/pallas_call | solution.py:267
  48.9 1.7 %collective-permute-start.11 = (f32[64,768]{1,0:T(8,128)S(1)}, f32[64,768]{1,0:T(8,128)S(1)}, u32[]{:S(2)}, u32[]{:S(2)}) collective-permute-start(f32[64,768]{1,0:T(8,128)S(1)} %get-tuple-element.123), channel_id=1, source_target_pairs={{0,4},{2,6},{4,0},{6,2},{1,5},{3,7},{5,1},{7,3},{8,12},{10,14},{12... | collective-permute-start | bytes 589832 | tf_op jit(solution)/shard_map/ppermute | solution.py:446
  50.6 0.1 add_split.5
  50.6 1.4 %collective-permute-start.9 = (bf16[2,208,256]{2,1,0:T(8,128)(2,1)S(1)}, bf16[2,208,256]{2,1,0:T(8,128)(2,1)S(1)}, u32[]{:S(2)}, u32[]{:S(2)}) collective-permute-start(bf16[2,208,256]{2,1,0:T(8,128)(2,1)S(1)} %get-tuple-element.149.refs_0_), channel_id=1, source_target_pairs={{0,24},{8,16},{16,8},{24,0},{1,25},{9,17},{17,9},{25,1},{2,26},{10... | collective-permute-start | bytes 638984 | tf_op jit(solution)/shard_map/ppermute | solution.py:438
  52.1 0.5 collective-permute-start.10
  52.5 3.2 %collective-permute-done.11.received_ref = f32[64,768]{1,0:T(8,128)S(1)} collective-permute-done((f32[64,768]{1,0:T(8,128)S(1)}, f32[64,768]{1,0:T(8,128)S(1)}, u32[]{:S(2)}, u32[]{:S(2)}) %collective-permute-start.11) | collective-permute-done | bytes 196640 | tf_op jit(solution)/shard_map/ppermute | solution.py:446
  55.7 0.1 collective-permute-start.13
  55.8 2.0 %collective-permute-done.10.received_ref = f32[64,768]{1,0:T(8,128)S(1)} collective-permute-done((f32[64,768]{1,0:T(8,128)S(1)}, f32[64,768]{1,0:T(8,128)S(1)}, u32[]{:S(2)}, u32[]{:S(2)}) %collective-permute-start.10) | collective-permute-done | bytes 196640 | tf_op jit(solution)/shard_map/ppermute | solution.py:446
  57.8 2.5 %collective-permute-done.9.refs_1_ = bf16[2,208,256]{2,1,0:T(8,128)(2,1)S(1)} collective-permute-done((bf16[2,208,256]{2,1,0:T(8,128)(2,1)S(1)}, bf16[2,208,256]{2,1,0:T(8,128)(2,1)S(1)}, u32[]{:S(2)}, u32[]{:S(2)}) %collective-permute-start.9) | collective-permute-done | bytes 213024 | tf_op jit(solution)/shard_map/ppermute | solution.py:438
  60.3 2.3 %collective-permute-done.8.refs_1_ = bf16[2,208,256]{2,1,0:T(8,128)(2,1)S(1)} collective-permute-done((bf16[2,208,256]{2,1,0:T(8,128)(2,1)S(1)}, bf16[2,208,256]{2,1,0:T(8,128)(2,1)S(1)}, u32[]{:S(2)}, u32[]{:S(2)}) %collective-permute-start.8) | collective-permute-done | bytes 213024 | tf_op jit(solution)/shard_map/ppermute | solution.py:438
  62.6 0.6 collective-permute-start.12
  63.1 0.6 collective-permute-done.13.received_ref
  63.8 2.2 %collective-permute-start.15 = (f32[32,768]{1,0:T(8,128)S(1)}, f32[32,768]{1,0:T(8,128)S(1)}, u32[]{:S(2)}, u32[]{:S(2)}) collective-permute-start(f32[32,768]{1,0:T(8,128)S(1)} %add.4.own_ref), channel_id=1, source_target_pairs={{0,24},{8,16},{16,8},{24,0},{1,25},{9,17},{17,9},{25,1},{2,26},{10... | collective-permute-start | bytes 294920 | tf_op jit(solution)/shard_map/ppermute | solution.py:438
  66.0 1.6 %collective-permute-done.12.received_ref = f32[32,768]{1,0:T(8,128)S(1)} collective-permute-done((f32[32,768]{1,0:T(8,128)S(1)}, f32[32,768]{1,0:T(8,128)S(1)}, u32[]{:S(2)}, u32[]{:S(2)}) %collective-permute-start.12) | collective-permute-done | bytes 98336 | tf_op jit(solution)/shard_map/ppermute | solution.py:438
  67.7 2.2 %collective-permute-start.14 = (f32[32,768]{1,0:T(8,128)S(1)}, f32[32,768]{1,0:T(8,128)S(1)}, u32[]{:S(2)}, u32[]{:S(2)}) collective-permute-start(f32[32,768]{1,0:T(8,128)S(1)} %add.5.own_ref), channel_id=1, source_target_pairs={{0,24},{8,16},{16,8},{24,0},{1,25},{9,17},{17,9},{25,1},{2,26},{10... | collective-permute-start | bytes 294920 | tf_op jit(solution)/shard_map/ppermute | solution.py:438
  69.9 1.2 %collective-permute-done.15.received_ref = f32[32,768]{1,0:T(8,128)S(1)} collective-permute-done((f32[32,768]{1,0:T(8,128)S(1)}, f32[32,768]{1,0:T(8,128)S(1)}, u32[]{:S(2)}, u32[]{:S(2)}) %collective-permute-start.15) | collective-permute-done | bytes 98336 | tf_op jit(solution)/shard_map/ppermute | solution.py:438
  71.1 0.1 collective-permute-start.17
  71.2 4.0 %collective-permute-done.14.received_ref = f32[32,768]{1,0:T(8,128)S(1)} collective-permute-done((f32[32,768]{1,0:T(8,128)S(1)}, f32[32,768]{1,0:T(8,128)S(1)}, u32[]{:S(2)}, u32[]{:S(2)}) %collective-permute-start.14) | collective-permute-done | bytes 98336 | tf_op jit(solution)/shard_map/ppermute | solution.py:438
  75.2 0.1 collective-permute-start.19
  75.3 2.0 %collective-permute-start.16 = (bf16[2,208,256]{2,1,0:T(8,128)(2,1)S(1)}, bf16[2,208,256]{2,1,0:T(8,128)(2,1)S(1)}, u32[]{:S(2)}, u32[]{:S(2)}) collective-permute-start(bf16[2,208,256]{2,1,0:T(8,128)(2,1)S(1)} %collective-permute-done.9.refs_1_), channel_id=1, source_target_pairs={{0,8},{8,0},{16,24},{24,16},{1,9},{9,1},{17,25},{25,17},{2,10},{10... | collective-permute-start | bytes 638984 | tf_op jit(solution)/shard_map/ppermute | solution.py:438
  77.3 0.5 collective-permute-start.18
  77.8 2.1 %collective-permute-done.19.received_ref = f32[32,768]{1,0:T(8,128)S(1)} collective-permute-done((f32[32,768]{1,0:T(8,128)S(1)}, f32[32,768]{1,0:T(8,128)S(1)}, u32[]{:S(2)}, u32[]{:S(2)}) %collective-permute-start.19) | collective-permute-done | bytes 98336 | tf_op jit(solution)/shard_map/ppermute | solution.py:438
  79.9 0.5 collective-permute-start.20
  80.4 4.5 %update_weights.2.refs_2_ = bf16[2,768,768]{2,1,0:T(8,128)(2,1)} custom-call(s32[1]{0:T(128)} %bitcast.index_ref, bf16[2,768,768]{2,1,0:T(8,128)(2,1)} %weights_ref.3, f32[2,768,256]{2,1,0:T(8,128)S(1)} %copy-done.3, bf16[2,208,256]{2,1,0:T(8,128)(2,1)S(1)} %get-tuple-element.149.refs_0_, bf16[2,208,256]{2,1,0:T(8,128)(2,1)S(1)} %collective-permute-done.8.refs_1_), custom_call_target="tpu_custom_call" | custom-call | flops 3000000000 | tf_op jit(solution)/shard_map/update_weights/pallas_call | solution.py:414
  84.9 0.7 collective-permute-done.20.refs_3_
  85.7 4.2 %newton_schulz.1 = (f32[2,768,256]{2,1,0:T(8,128)}, f32[768,256]{1,0:T(8,128)S(1)}) custom-call(f32[64,768]{1,0:T(8,128)S(1)} %join.2.refs_0_, f32[64,768]{1,0:T(8,128)S(1)} %collective-permute-done.18.refs_1_, f32[64,768]{1,0:T(8,128)S(1)} %join.3.refs_2_, f32[64,768]{1,0:T(8,128)S(1)} %collective-permute-done.20.refs_3_), custom_call_target="tpu_custom_call" | custom-call | flops 4000000000 | tf_op jit(solution)/shard_map/newton_schulz/pallas_call | solution.py:352
  89.9 0.1 collective-permute-start.21
  90.0 4.5 %update_weights.3 = bf16[2,768,768]{2,1,0:T(8,128)(2,1)} custom-call(s32[1]{0:T(128)} %bitcast.index_ref, bf16[2,768,768]{2,1,0:T(8,128)(2,1)} %weights_ref.3, f32[2,768,256]{2,1,0:T(8,128)S(1)} %copy-done.3, bf16[2,208,256]{2,1,0:T(8,128)(2,1)S(1)} %collective-permute-done.16.refs_0_, ...), custom_call_target="tpu_custom_call", output_to_operand_aliasing={{}: (5, {})} | custom-call | flops 3000000000 | tf_op jit(solution)/shard_map/update_weights/pallas_call | solution.py:414
  94.5 0.9 put_layer.1
  (25 shorter events, 0.2 us)
Async XLA Ops:
  1.9 17.2 %collective-permute-start.2 = (bf16[384,768]{1,0:T(8,128)(2,1)S(1)}, bf16[384,768]{1,0:T(8,128)(2,1)S(1)}, u32[]{:S(2)}, u32[]{:S(2)}) collective-permute-start(bf16[384,768]{1,0:T(8,128)(2,1)S(1)} %get-tuple-element.86), channel_id=1, source_target_pairs={{0,8},{8,0},{16,24},{24,16},{1,9},{9,1},{17,25},{25,17},{2,10},{10... | collective-permute-start | bytes 1769480 | tf_op jit(solution)/shard_map/ppermute | solution.py:438
  5.0 20.5 %collective-permute-start = (bf16[192,768]{1,0:T(8,128)(2,1)S(1)}, bf16[192,768]{1,0:T(8,128)(2,1)S(1)}, u32[]{:S(2)}, u32[]{:S(2)}) collective-permute-start(bf16[192,768]{1,0:T(8,128)(2,1)S(1)} %get-tuple-element.84), channel_id=1, source_target_pairs={{0,8},{8,0},{16,24},{24,16},{1,9},{9,1},{17,25},{25,17},{2,10},{10... | collective-permute-start | bytes 884744 | tf_op jit(solution)/shard_map/ppermute | solution.py:438
  5.1 14.1 %copy-start = (bf16[1,2,768,768]{3,2,1,0:T(8,128)(2,1)S(1)}, bf16[1,2,768,768]{3,2,1,0:T(8,128)(2,1)}, u32[]{:S(2)}) copy-start(bf16[1,2,768,768]{3,2,1,0:T(8,128)(2,1)} %grads_ref.11) | copy-start | bytes 7077892
  5.1 35.3 %collective-permute-start.1 = (bf16[192,768]{1,0:T(8,128)(2,1)S(1)}, bf16[192,768]{1,0:T(8,128)(2,1)S(1)}, u32[]{:S(2)}, u32[]{:S(2)}) collective-permute-start(bf16[192,768]{1,0:T(8,128)(2,1)S(1)} %get-tuple-element.85), channel_id=1, source_target_pairs={{0,8},{8,0},{16,24},{24,16},{1,9},{9,1},{17,25},{25,17},{2,10},{10... | collective-permute-start | bytes 884744 | tf_op jit(solution)/shard_map/ppermute | solution.py:438
  20.0 19.0 %copy-start.1 = (f32[2,192,256]{2,1,0:T(8,128)S(1)}, f32[2,192,256]{2,1,0:T(8,128)}, u32[]{:S(2)}) copy-start(f32[2,192,256]{2,1,0:T(8,128)} %first_ref.3) | copy-start | bytes 1179652
  20.0 19.0 %copy-start.2 = (f32[2,192,256]{2,1,0:T(8,128)S(1)}, f32[2,192,256]{2,1,0:T(8,128)}, u32[]{:S(2)}) copy-start(f32[2,192,256]{2,1,0:T(8,128)} %second_ref.3) | copy-start | bytes 1179652
  20.0 19.0 %collective-permute-start.4 = (bf16[416,256]{1,0:T(8,128)(2,1)S(1)}, bf16[416,256]{1,0:T(8,128)(2,1)S(1)}, u32[]{:S(2)}, u32[]{:S(2)}) collective-permute-start(bf16[416,256]{1,0:T(8,128)(2,1)S(1)} %get-tuple-element.93), channel_id=1, source_target_pairs={{0,24},{8,16},{16,8},{24,0},{1,25},{9,17},{17,9},{25,1},{2,26},{10... | collective-permute-start | bytes 638984 | tf_op jit(solution)/shard_map/ppermute | solution.py:438
  26.0 14.4 %collective-permute-start.3 = (bf16[208,256]{1,0:T(8,128)(2,1)S(1)}, bf16[208,256]{1,0:T(8,128)(2,1)S(1)}, u32[]{:S(2)}, u32[]{:S(2)}) collective-permute-start(bf16[208,256]{1,0:T(8,128)(2,1)S(1)} %get-tuple-element.92), channel_id=1, source_target_pairs={{0,24},{8,16},{16,8},{24,0},{1,25},{9,17},{17,9},{25,1},{2,26},{10... | collective-permute-start | bytes 319496 | tf_op jit(solution)/shard_map/ppermute | solution.py:438
  40.9 6.6 %collective-permute-start.5 = (bf16[208,256]{1,0:T(8,128)(2,1)S(1)}, bf16[208,256]{1,0:T(8,128)(2,1)S(1)}, u32[]{:S(2)}, u32[]{:S(2)}) collective-permute-start(bf16[208,256]{1,0:T(8,128)(2,1)S(1)} %get-tuple-element.101), channel_id=1, source_target_pairs={{0,24},{8,16},{16,8},{24,0},{1,25},{9,17},{17,9},{25,1},{2,26},{10... | collective-permute-start | bytes 319496 | tf_op jit(solution)/shard_map/ppermute | solution.py:438
  42.4 6.5 %collective-permute-start.7 = (f32[128,768]{1,0:T(8,128)S(1)}, f32[128,768]{1,0:T(8,128)S(1)}, u32[]{:S(2)}, u32[]{:S(2)}) collective-permute-start(f32[128,768]{1,0:T(8,128)S(1)} %get-tuple-element.97), channel_id=1, source_target_pairs={{0,2},{2,0},{4,6},{6,4},{1,3},{3,1},{5,7},{7,5},{8,10},{10,8},{12,... | collective-permute-start | bytes 1179656 | tf_op jit(solution)/shard_map/ppermute | solution.py:442
  42.4 6.6 %collective-permute-start.6 = (f32[128,768]{1,0:T(8,128)S(1)}, f32[128,768]{1,0:T(8,128)S(1)}, u32[]{:S(2)}, u32[]{:S(2)}) collective-permute-start(f32[128,768]{1,0:T(8,128)S(1)} %get-tuple-element.113), channel_id=1, source_target_pairs={{0,2},{2,0},{4,6},{6,4},{1,3},{3,1},{5,7},{7,5},{8,10},{10,8},{12,... | collective-permute-start | bytes 1179656 | tf_op jit(solution)/shard_map/ppermute | solution.py:442
  48.9 6.8 %collective-permute-start.11 = (f32[64,768]{1,0:T(8,128)S(1)}, f32[64,768]{1,0:T(8,128)S(1)}, u32[]{:S(2)}, u32[]{:S(2)}) collective-permute-start(f32[64,768]{1,0:T(8,128)S(1)} %get-tuple-element.123), channel_id=1, source_target_pairs={{0,4},{2,6},{4,0},{6,2},{1,5},{3,7},{5,1},{7,3},{8,12},{10,14},{12... | collective-permute-start | bytes 589832 | tf_op jit(solution)/shard_map/ppermute | solution.py:446
  50.6 9.6 %collective-permute-start.9 = (bf16[2,208,256]{2,1,0:T(8,128)(2,1)S(1)}, bf16[2,208,256]{2,1,0:T(8,128)(2,1)S(1)}, u32[]{:S(2)}, u32[]{:S(2)}) collective-permute-start(bf16[2,208,256]{2,1,0:T(8,128)(2,1)S(1)} %get-tuple-element.149.refs_0_), channel_id=1, source_target_pairs={{0,24},{8,16},{16,8},{24,0},{1,25},{9,17},{17,9},{25,1},{2,26},{10... | collective-permute-start | bytes 638984 | tf_op jit(solution)/shard_map/ppermute | solution.py:438
  52.1 10.5 %collective-permute-start.8 = (bf16[2,208,256]{2,1,0:T(8,128)(2,1)S(1)}, bf16[2,208,256]{2,1,0:T(8,128)(2,1)S(1)}, u32[]{:S(2)}, u32[]{:S(2)}) collective-permute-start(bf16[2,208,256]{2,1,0:T(8,128)(2,1)S(1)} %get-tuple-element.149.refs_0_), channel_id=1, source_target_pairs={{0,8},{8,0},{16,24},{24,16},{1,9},{9,1},{17,25},{25,17},{2,10},{10... | collective-permute-start | bytes 638984 | tf_op jit(solution)/shard_map/ppermute | solution.py:438
  52.1 5.7 %collective-permute-start.10 = (f32[64,768]{1,0:T(8,128)S(1)}, f32[64,768]{1,0:T(8,128)S(1)}, u32[]{:S(2)}, u32[]{:S(2)}) collective-permute-start(f32[64,768]{1,0:T(8,128)S(1)} %get-tuple-element.122), channel_id=1, source_target_pairs={{0,4},{2,6},{4,0},{6,2},{1,5},{3,7},{5,1},{7,3},{8,12},{10,14},{12... | collective-permute-start | bytes 589832 | tf_op jit(solution)/shard_map/ppermute | solution.py:446
  55.7 8.0 %collective-permute-start.13 = (f32[32,768]{1,0:T(8,128)S(1)}, f32[32,768]{1,0:T(8,128)S(1)}, u32[]{:S(2)}, u32[]{:S(2)}) collective-permute-start(f32[32,768]{1,0:T(8,128)S(1)} %get-tuple-element.134), channel_id=1, source_target_pairs={{0,8},{8,0},{16,24},{24,16},{1,9},{9,1},{17,25},{25,17},{2,10},{10... | collective-permute-start | bytes 294920 | tf_op jit(solution)/shard_map/ppermute | solution.py:438
  62.6 17.9 %copy-start.3 = (f32[2,768,256]{2,1,0:T(8,128)S(1)}, f32[2,768,256]{2,1,0:T(8,128)}, u32[]{:S(2)}) copy-start(f32[2,768,256]{2,1,0:T(8,128)} %basis_ref.3) | copy-start | bytes 4718596
  62.6 5.1 %collective-permute-start.12 = (f32[32,768]{1,0:T(8,128)S(1)}, f32[32,768]{1,0:T(8,128)S(1)}, u32[]{:S(2)}, u32[]{:S(2)}) collective-permute-start(f32[32,768]{1,0:T(8,128)S(1)} %get-tuple-element.133), channel_id=1, source_target_pairs={{0,8},{8,0},{16,24},{24,16},{1,9},{9,1},{17,25},{25,17},{2,10},{10... | collective-permute-start | bytes 294920 | tf_op jit(solution)/shard_map/ppermute | solution.py:438
  63.8 7.3 %collective-permute-start.15 = (f32[32,768]{1,0:T(8,128)S(1)}, f32[32,768]{1,0:T(8,128)S(1)}, u32[]{:S(2)}, u32[]{:S(2)}) collective-permute-start(f32[32,768]{1,0:T(8,128)S(1)} %add.4.own_ref), channel_id=1, source_target_pairs={{0,24},{8,16},{16,8},{24,0},{1,25},{9,17},{17,9},{25,1},{2,26},{10... | collective-permute-start | bytes 294920 | tf_op jit(solution)/shard_map/ppermute | solution.py:438
  67.7 7.5 %collective-permute-start.14 = (f32[32,768]{1,0:T(8,128)S(1)}, f32[32,768]{1,0:T(8,128)S(1)}, u32[]{:S(2)}, u32[]{:S(2)}) collective-permute-start(f32[32,768]{1,0:T(8,128)S(1)} %add.5.own_ref), channel_id=1, source_target_pairs={{0,24},{8,16},{16,8},{24,0},{1,25},{9,17},{17,9},{25,1},{2,26},{10... | collective-permute-start | bytes 294920 | tf_op jit(solution)/shard_map/ppermute | solution.py:438
  71.1 6.2 %collective-permute-start.17 = (f32[32,768]{1,0:T(8,128)S(1)}, f32[32,768]{1,0:T(8,128)S(1)}, u32[]{:S(2)}, u32[]{:S(2)}) collective-permute-start(f32[32,768]{1,0:T(8,128)S(1)} %add.6.own_ref), channel_id=1, source_target_pairs={{0,8},{8,0},{16,24},{24,16},{1,9},{9,1},{17,25},{25,17},{2,10},{10... | collective-permute-start | bytes 294920 | tf_op jit(solution)/shard_map/ppermute | solution.py:438
  75.2 4.7 %collective-permute-start.19 = (f32[32,768]{1,0:T(8,128)S(1)}, f32[32,768]{1,0:T(8,128)S(1)}, u32[]{:S(2)}, u32[]{:S(2)}) collective-permute-start(f32[32,768]{1,0:T(8,128)S(1)} %add.7.own_ref), channel_id=1, source_target_pairs={{0,8},{8,0},{16,24},{24,16},{1,9},{9,1},{17,25},{25,17},{2,10},{10... | collective-permute-start | bytes 294920 | tf_op jit(solution)/shard_map/ppermute | solution.py:438
  75.3 9.6 %collective-permute-start.16 = (bf16[2,208,256]{2,1,0:T(8,128)(2,1)S(1)}, bf16[2,208,256]{2,1,0:T(8,128)(2,1)S(1)}, u32[]{:S(2)}, u32[]{:S(2)}) collective-permute-start(bf16[2,208,256]{2,1,0:T(8,128)(2,1)S(1)} %collective-permute-done.9.refs_1_), channel_id=1, source_target_pairs={{0,8},{8,0},{16,24},{24,16},{1,9},{9,1},{17,25},{25,17},{2,10},{10... | collective-permute-start | bytes 638984 | tf_op jit(solution)/shard_map/ppermute | solution.py:438
  77.3 7.6 %collective-permute-start.18 = (f32[64,768]{1,0:T(8,128)S(1)}, f32[64,768]{1,0:T(8,128)S(1)}, u32[]{:S(2)}, u32[]{:S(2)}) collective-permute-start(f32[64,768]{1,0:T(8,128)S(1)} %join.2.refs_0_), channel_id=1, source_target_pairs={{0,4},{2,6},{4,0},{6,2},{1,5},{3,7},{5,1},{7,3},{8,12},{10,14},{12... | collective-permute-start | bytes 589832 | tf_op jit(solution)/shard_map/ppermute | solution.py:446
  79.9 5.7 %collective-permute-start.20 = (f32[64,768]{1,0:T(8,128)S(1)}, f32[64,768]{1,0:T(8,128)S(1)}, u32[]{:S(2)}, u32[]{:S(2)}) collective-permute-start(f32[64,768]{1,0:T(8,128)S(1)} %join.3.refs_2_), channel_id=1, source_target_pairs={{0,4},{2,6},{4,0},{6,2},{1,5},{3,7},{5,1},{7,3},{8,12},{10,14},{12... | collective-permute-start | bytes 589832 | tf_op jit(solution)/shard_map/ppermute | solution.py:446
  89.9 4.6 %collective-permute-start.21 = (f32[768,256]{1,0:T(8,128)S(1)}, f32[768,256]{1,0:T(8,128)S(1)}, u32[]{:S(2)}, u32[]{:S(2)}) collective-permute-start(f32[768,256]{1,0:T(8,128)S(1)} %get-tuple-element.156), channel_id=1, source_target_pairs={{0,2},{2,0},{4,6},{6,4},{1,3},{3,1},{5,7},{7,5},{8,10},{10,8},{12,... | collective-permute-start | bytes 2359304 | tf_op jit(solution)/shard_map/ppermute | solution.py:442

commit v4 on v3

--- a/solution.py
+++ b/solution.py
@@ -145,33 +145,6 @@
     return jnp.where(code < 0, -size, size)
 
 
-def give_kernel(rows, grads_ref, *rest):
-    outs, sems = rest[:-1], rest[-1]
-    place = Place()
-    copies = []
-    for i in range(4):
-        start = pl.multiple_of(place.gives(i % 2) * rows, rows)
-        out = outs[0].at[pl.ds(i * rows, rows)] if i < 2 else outs[i - 1]
-        copies.append(pltpu.make_async_copy(grads_ref.at[0, place.layer(i // 2), pl.ds(start, rows)], out, sems.at[i]))
-    for copy in copies:
-        copy.start()
-    for copy in copies:
-        copy.wait()
-
-
-def give_blocks(grads, rows):
-    heights = (2 * rows, rows, rows)
-    return pl.pallas_call(
-        functools.partial(give_kernel, rows),
-        out_shape=[pltpu.VMEM((height, grads.shape[3]), grads.dtype) for height in heights],
-        in_specs=[pl.BlockSpec(memory_space=pltpu.HBM)],
-        out_specs=[pl.BlockSpec(memory_space=pltpu.VMEM)] * len(heights),
-        scratch_shapes=[pltpu.SemaphoreType.DMA((4,))],
-        compiler_params=params(4),
-        name="give_blocks",
-    )(pltpu.with_memory_space_constraint(grads, pltpu.HBM))
-
-
 def prepare_kernel(basis_hbm, high_ref, low_ref, buffer, sems):
     layers = buffer.shape[0]
     copies = [pltpu.make_async_copy(basis_hbm.at[layer], buffer.at[layer], sems.at[layer]) for layer in range(layers)]
@@ -197,47 +170,90 @@
     )(pltpu.with_memory_space_constraint(basis, pltpu.HBM))
 
 
-def kept_sum(place, grads_ref, other, turn, j, rows):
-    start = pl.multiple_of(place.keeps(j) * rows, rows)
-    kept = grads_ref[0, place.layer(turn), pl.ds(start, rows)]
-    return kept.astype(jnp.float32) + other.astype(jnp.float32)
-
-
-def project_kernel(turn, blocks, rows, grads_ref, other_ref, high_ref, low_ref, out_ref, code_ref):
+def fetch_kernel(weights_hbm, high_ref, low_ref, weights_ref, high_t_ref, low_t_ref, sems):
+    layers = weights_ref.shape[0]
+    copies = [pltpu.make_async_copy(weights_hbm.at[layer], weights_ref.at[layer], sems.at[layer]) for layer in range(layers)]
+    for copy in copies:
+        copy.start()
+    for layer in range(layers):
+        for source, out in ((high_ref, high_t_ref), (low_ref, low_t_ref)):
+            out[layer] = source[layer].astype(jnp.float32).T.astype(jnp.bfloat16)
+    for copy in copies:
+        copy.wait()
+
+
+def fetch(weights, high, low):
+    layers, width, rank = high.shape
+    vmem = pl.BlockSpec(memory_space=pltpu.VMEM)
+    return pl.pallas_call(
+        fetch_kernel,
+        out_shape=[pltpu.VMEM(weights.shape, weights.dtype)] + [pltpu.VMEM((layers, rank, width), jnp.bfloat16)] * 2,
+        in_specs=[pl.BlockSpec(memory_space=pltpu.HBM), vmem, vmem],
+        out_specs=[vmem] * 3,
+        scratch_shapes=[pltpu.SemaphoreType.DMA((layers,))],
+        compiler_params=params(12),
+        name="fetch",
+    )(pltpu.with_memory_space_constraint(weights, pltpu.HBM), *in_vmem(high, low))
+
+
+def code_blocks(code_ref, parts):
+    for j, part in enumerate(parts):
+        rows = part.shape[0]
+        row = j * (rows + 16)
+        code_ref[row : row + rows], code_ref[row + rows : row + rows + 16] = encode(part)
+
+
+def blocks_of(code_ref):
+    rows = code_ref.shape[0] // 2 - 16
+    return [decode(code_ref[j * (rows + 16) : j * (rows + 16) + rows], code_ref[j * (rows + 16) + rows : (j + 1) * (rows + 16)]) for j in range(2)]
+
+
+def rows_of(grads_ref, layer, block, rows):
+    return grads_ref[0, layer, pl.ds(pl.multiple_of(block * rows, rows), rows)]
+
+
+def exact_dot(a, b, dims=PLAIN):
+    dot = lambda p, q: lax.dot_general(p, q, (dims, ((), ())), preferred_element_type=jnp.float32)
+    return dot(a[0], b) + dot(a[1], b) if isinstance(a, tuple) else dot(a, b[0]) + dot(a, b[1])
+
+
+def project_kernel(turn, grads_ref, high_ref, low_ref, out_ref, code_ref):
     place = Place()
-    basis = high_ref[place.layer(turn)], low_ref[place.layer(turn)]
-    for i, j in enumerate(blocks):
-        total = kept_sum(place, grads_ref, other_ref[i * rows : (i + 1) * rows], turn, j, rows)
-        projected = dot3(split(total), basis)
-        out_ref[i * rows : (i + 1) * rows] = projected
-        row = i * (rows + 16)
-        code_ref[row : row + rows], code_ref[row + rows : row + rows + 16] = encode(projected)
-
-
-def project(grads, other, basis, turn, blocks):
-    rank, rows = basis[0].shape[2], other.shape[0] // len(blocks)
-    kernel = functools.partial(project_kernel, turn, blocks, rows)
-    outs = [((len(blocks) * rows, rank), jnp.float32), ((len(blocks) * (rows + 16), rank), jnp.bfloat16)]
-    return local_call(kernel, outs, grads, other, *basis, name="project")
+    layer, rows = place.layer(turn), out_ref.shape[0] // 2
+    basis = high_ref[layer], low_ref[layer]
+    code_blocks(code_ref, [exact_dot(rows_of(grads_ref, layer, place.gives(j), rows), basis) for j in range(2)])
+    for j in range(2):
+        out_ref[j * rows : (j + 1) * rows] = exact_dot(rows_of(grads_ref, layer, place.keeps(j), rows), basis)
+
+
+def project(grads, basis, turn):
+    rows, rank = grads.shape[2] // 4, basis[0].shape[2]
+    outs = [((2 * rows, rank), jnp.float32), ((2 * (rows + 16), rank), jnp.bfloat16)]
+    return local_call(functools.partial(project_kernel, turn), outs, grads, *basis, name="project")
+
+
+def add_coded_kernel(own_ref, received_ref, out_ref, code_ref):
+    rows = own_ref.shape[0] // 2
+    parts = [own_ref[j * rows : (j + 1) * rows] + block for j, block in enumerate(blocks_of(received_ref))]
+    code_blocks(code_ref, parts)
+    for j, part in enumerate(parts):
+        out_ref[j * rows : (j + 1) * rows] = part
+
+
+def add_coded(own, received):
+    outs = [(own.shape, jnp.float32), (received.shape, jnp.bfloat16)]
+    return local_call(add_coded_kernel, outs, own, received, name="add_coded")
 
 
 HALVES = 2
 
 
-def power_kernel(turn, scale, grads_ref, first_ref, second_ref, *refs):
+def power_kernel(turn, scale, grads_ref, first_ref, second_ref, kept_ref, given_ref, *rest):
     place = Place()
-    parts = 1 + turn
-    others, partials, received, rest = refs[:parts], refs[parts : 2 * parts], refs[2 * parts : 3 * parts], refs[3 * parts :]
-    rest = rest[3 * turn :]
-    half0_ref, half1_ref, one_ref, two_ref, code_ref, product, one, two, sems = rest
-    layers, rows = first_ref.shape[0], first_ref.shape[1]
-    sums, summed = [], []
-    for j in range(2):
-        part, row = (0, j) if turn == 0 else (j, 0)
-        block, coded = pl.ds(row * rows, rows), row * (rows + 16)
-        summed.append(kept_sum(place, grads_ref, others[part][block], turn, j, rows))
-        code, bound = received[part][coded : coded + rows], received[part][coded + rows : coded + rows + 16]
-        sums.append(partials[part][block] + decode(code, bound))
+    code_before = rest[2] if turn else None
+    half0_ref, half1_ref, one_ref, two_ref, code_ref, product, one, two, sems = rest[3 * turn :]
+    rows = first_ref.shape[1]
+    sums = [kept_ref[0:rows], kept_ref[rows:]]
     layer = place.layer(turn)
     reduced = scale * jnp.where(place.z < 2, sums[0], sums[1])
     one[...], two[...], direction = adam_direction(reduced, first_ref[layer], second_ref[layer])
@@ -247,9 +263,11 @@
     if turn == 0:
         code_ref[0:rows], code_ref[rows:] = encode(direction)
     else:
-        code_ref[1 - layer] = refs[3 * parts + 2][...]
+        code_ref[1 - layer] = code_before[...]
         code_ref[layer, 0:rows], code_ref[layer, rows:] = encode(direction)
-    product[...] = dot3(split(jnp.concatenate(sums).T), split(jnp.concatenate(summed)))
+    blocks = [place.keeps(0), place.keeps(1), place.gives(0), place.gives(1)]
+    rows_in_order = jnp.concatenate([rows_of(grads_ref, layer, block, rows) for block in blocks])
+    product[...] = exact_dot(split(jnp.concatenate(sums + blocks_of(given_ref)).T), rows_in_order)
     piece = product.shape[0] // (4 * HALVES)
     for h in range(HALVES):
         for k in range(4):
@@ -258,11 +276,11 @@
         copy.wait()
 
 
-def power_product(grads, first_moment, second_moment, others, partials, received, turn, scale, before=()):
+def power_product(grads, first_moment, second_moment, kept, given, turn, scale, before=()):
     width = grads.shape[3]
     layers, rows, rank = first_moment.shape
     vmem, anywhere = pl.BlockSpec(memory_space=pltpu.VMEM), pl.BlockSpec(memory_space=pl.ANY)
-    operands = in_vmem(grads, first_moment, second_moment, *others, *partials, *received)
+    operands = in_vmem(grads, first_moment, second_moment, kept, given)
     count = len(operands)
     return pl.pallas_call(
         functools.partial(power_kernel, turn, scale),
@@ -276,7 +294,7 @@
         + [pltpu.SemaphoreType.DMA((2,))],
         input_output_aliases={count: HALVES, count + 1: HALVES + 1} if before else {},
         compiler_params=params(12),
-        cost_estimate=cost(5e9 * turn),
+        cost_estimate=cost(5e9),
         name="power",
     )(*operands, *before[:2], *in_vmem(*before[2:]))
 
@@ -287,9 +305,9 @@
     give_ref[...] = own_ref[half:] + received_ref[half:]
 
 
-def add_split(own, received):
+def add_split(own, received, flops):
     outs = [((own.shape[0] // 2, own.shape[1]), jnp.float32)] * 2
-    return local_call(add_split_kernel, outs, own, received, name="add_split", flops=1e9)
+    return local_call(add_split_kernel, outs, own, received, name="add_split", flops=flops)
 
 
 def add_kernel(own_ref, received_ref, out_ref):
@@ -302,8 +320,8 @@
     out_ref[half:] = received_ref[...]
 
 
-def add(own, received):
-    return local_call(add_kernel, [(own.shape, jnp.float32)], own, received, name="add")[0]
+def add(own, received, flops):
+    return local_call(add_kernel, [(own.shape, jnp.float32)], own, received, name="add", flops=flops)[0]
 
 
 def join(own, received):
@@ -356,7 +374,6 @@
         out_specs=[pl.BlockSpec(memory_space=pl.ANY), vmem],
         scratch_shapes=[pltpu.VMEM((rank, width), jnp.float32), pltpu.SemaphoreType.DMA((width // rank,))],
         compiler_params=params(12),
-        cost_estimate=cost(4e9),
         name="newton_schulz",
     )(*in_vmem(*parts))
 
@@ -388,46 +405,48 @@
     )(*in_vmem(layer), whole)
 
 
-def update_kernel(factor, index_ref, weights_ref, basis_ref, *refs):
-    directions, (out_ref, high, low) = refs[:2], refs[-3:]
-    k = pl.program_id(1)
-
-    @pl.when(k == 0)
-    def _():
-        high[...], low[...] = split(basis_ref[0].T)
-
-    for step, direction in enumerate(directions):
-
-        @pl.when(k == step)
-        def _(direction=direction):
-            rows = out_ref.shape[1]
-            exact = decode(direction[0, 0:rows], direction[0, rows:])
-            update = dot3(split(exact), (high[...], low[...]))
-            out_ref[0] = (weights_ref[0].astype(jnp.float32) - factor * update).astype(out_ref.dtype)
-
-
-def update_weights(index, weights, basis, blocks, directions, factor, before=()):
+def stack_kernel(a_ref, b_ref, out_ref):
+    out_ref[0] = a_ref[...]
+    out_ref[1] = b_ref[...]
+
+
+def stack(a, b):
+    return local_call(stack_kernel, [((2,) + a.shape, a.dtype)], a, b, name="stack")[0]
+
+
+def update_kernel(factor, blocks, weights_ref, high_ref, low_ref, *refs):
+    directions, (out_ref, buffer, sems) = refs[:2], refs[-3:]
+    place = Place()
+    layers, rows = weights_ref.shape[0], buffer.shape[2]
+    copies = []
+    for layer in range(layers):
+        basis = high_ref[layer], low_ref[layer]
+        for i, (direction, (k, source)) in enumerate(zip(directions, blocks)):
+            where = pl.ds(pl.multiple_of((place.z ^ k) * rows, rows), rows)
+            exact = decode(direction[source, layer, 0:rows], direction[source, layer, rows:])
+            update = dot3(split(exact), basis)
+            buffer[layer, i] = (weights_ref[layer, where].astype(jnp.float32) - factor * update).astype(buffer.dtype)
+            copies.append(pltpu.make_async_copy(buffer.at[layer, i], out_ref.at[layer, where], sems.at[layer, i]))
+            copies[-1].start()
+    for copy in copies:
+        copy.wait()
+
+
+def update_weights(weights, basis, directions, blocks, factor, flops, before=()):
     layers, height, width = weights.shape
-    rank, rows = basis.shape[2], height // 4
-    row_block = pl.BlockSpec((1, rows, width), lambda l, k, index: (l, index[0] ^ (blocks[0] + k * (blocks[1] - blocks[0])), 0))
-    layer_block = lambda a, b: pl.BlockSpec((1, a, b), lambda l, k, index: (l, 0, 0))
-    return pl.pallas_call(
-        functools.partial(update_kernel, factor),
+    vmem, anywhere = pl.BlockSpec(memory_space=pltpu.VMEM), pl.BlockSpec(memory_space=pl.ANY)
+    operands = in_vmem(weights, *basis, *directions)
+    return pl.pallas_call(
+        functools.partial(update_kernel, factor, blocks),
         out_shape=jax.ShapeDtypeStruct(weights.shape, weights.dtype),
-        grid_spec=pltpu.PrefetchScalarGridSpec(
-            num_scalar_prefetch=1,
-            grid=(layers, 2),
-            in_specs=[row_block, layer_block(width, rank)]
-            + [layer_block(rows + 16, rank)] * 2
-            + [pl.BlockSpec(memory_space=pl.ANY)] * len(before),
-            out_specs=row_block,
-            scratch_shapes=[pltpu.VMEM((rank, width), jnp.bfloat16)] * 2,
-        ),
+        in_specs=[vmem] * len(operands) + [anywhere] * len(before),
+        out_specs=anywhere,
+        scratch_shapes=[pltpu.VMEM((layers, 2, height // 4, width), weights.dtype), pltpu.SemaphoreType.DMA((layers, 2))],
         input_output_aliases={5: 0} if before else {},
         compiler_params=params(12),
-        cost_estimate=cost(3e9),
+        cost_estimate=cost(flops),
         name="update_weights",
-    )(index, pltpu.with_memory_space_constraint(weights, pltpu.HBM), basis, *directions, *before)
+    )(*operands, *before)
 
 
 def xor_pairs(k):
@@ -466,33 +485,25 @@
     layers, rows = grads.shape[1], first_moment.shape[1]
     order = Order()
 
-    others = [over_z(block, 1) for block in give_blocks(grads, rows)]
     high, low = prepare_basis(basis)
-    partials, received = [], []
-
-    def exchange(i, turn, blocks, *awaited):
-        other, *awaited = order.step(others[i], *awaited)
-        partial, code = project(grads, other, (high, low), turn, blocks)
-        partials.append(order.through(partial))
-        received.append(over_z(code, 3))
-        return awaited
-
-    def product(turn, *before):
-        some = slice(1, 3) if turn else slice(0, 1)
-        operands = order.step(*others[some], *partials[some], *received[some])
-        n = 1 + turn
+
+    def product(turn, kept, given, *before):
         *halves, one, two, code = power_product(
-            grads, first_moment, second_moment, operands[:n], operands[n : 2 * n], operands[2 * n :], turn, scale_factor, before
+            grads, first_moment, second_moment, *order.step(kept, given), turn, scale_factor, before
         )
         order.through(halves[0])
         return halves, (one, two, code)
 
-    def scatter(over, x, received):
-        keep, give = add_split(*order.step(x, received))
+    def add_code(x, received):
+        x, code = add_coded(*order.step(x, received))
+        return order.through(x), code
+
+    def scatter(over, x, received, flops=0):
+        keep, give = add_split(*order.step(x, received), flops)
         return order.through(keep), over(give)
 
-    def total(over, x, received):
-        x = order.through(add(*order.step(x, received)))
+    def total(over, x, received, flops=0):
+        x = order.through(add(*order.step(x, received), flops))
         return x, over(x)
 
     def gather(over, x, received):
@@ -502,31 +513,45 @@
     next_z = lambda x: over_z(x, 1)
     opposite_z = lambda x: over_z(x, 3)
 
-    exchange(0, 0, (0, 1))
-    exchange(1, 1, (0,))
-    gifts, before = product(0)
+    codes = []
+    kept = []
+    for turn in range(2):
+        x, code = project(order.step(grads)[0], (high, low), turn)
+        kept.append(order.through(x))
+        codes.append(code)
+    first, code = add_code(kept[0], next_z(codes[0]))
+    first = first, opposite_z(code)
+    second, code = add_code(kept[1], next_z(order.step(codes[1])[0]))
+    second = second, opposite_z(code)
+    weights, *turned = fetch(*order.step(weights, high, low))
+    order.through(weights)
+    sums = []
+    for pair in (first, second):
+        x, code = add_code(*pair)
+        sums.append((x, next_z(code)))
+    gifts, before = product(0, *sums[0])
     gifts = [over_core(gift) for gift in gifts]
-    (received[1],) = exchange(2, 1, (1,), received[1])
-    parts, (moment_one, moment_two, code) = product(1, *before)
-    parts = [scatter(over_y, part, gift) for part, gift in zip(parts, gifts)]
-    (code,) = order.step(code)
-    near, opposite = next_z(code), opposite_z(code)
-    first = scatter(next_z, *parts[0])
-    near, opposite, *second = order.step(near, opposite, *parts[1])
-    parts = [first, scatter(next_z, *second)]
-    parts = [total(opposite_z, *part) for part in parts]
+    parts, (moment_one, moment_two, code) = product(1, *sums[1], *before)
+    parts = [scatter(over_y, part, gift, 1e9) for part, gift in zip(parts, gifts)]
+    opposite = opposite_z(order.step(code)[0])
+    parts = [scatter(next_z, *part) for part in parts]
+    opposite, *parts[0] = order.step(opposite, *parts[0])
+    first = total(opposite_z, *parts[0], 1e9)
+    parts = [first, total(opposite_z, *parts[1])]
     parts = [total(next_z, *part) for part in parts]
-    last = next_z(order.step(opposite)[0])
     parts = [gather(over_y, *part) for part in parts]
-    index = lax.axis_index("shard").astype(jnp.int32)[None]
+    pair = next_z(order.through(stack(*order.step(code, opposite))))
     factor = learn_rate * galore_scale * scale_factor
-    update = functools.partial(update_weights, index, weights, basis)
-    weights_next = order.through(update((0, 1), order.step(code, near), factor))
-    last, *parts = order.step(last, *[x for part in parts for x in part])
+    code, opposite, weights, *parts[0] = order.step(code[None], opposite[None], weights, *parts[0])
+    weights_next = order.through(update_weights(weights, turned, (code, opposite), ((0, 0), (3, 0)), factor, 3e9))
+    parts = order.step(*[x for part in parts for x in part])
     basis_next, own = newton_schulz_power(layers, *parts)
     order.through(own)
     other = over_core(own)
-    weights_next = order.through(update((2, 3), order.step(last, opposite), factor, (weights_next,)))
+    (pair,) = order.step(pair)
+    weights_next = order.through(
+        update_weights(weights, turned, (pair, pair), ((1, 0), (2, 1)), factor, 8e9, (weights_next,))
+    )
     basis_next = put_layer(*order.step(other, basis_next))
     return (weights_next, basis_next, moment_one, moment_two)
 

time: 95.7 us -> 87.4 us (0.913)
  waiting for transfers between devices: 45.6 us -> 22.8 us
  starting transfers between devices: 27.2 us -> 44.1 us
  Pallas kernels: 21.7 us -> 19 us
    ppermute x15 -> x14, waiting for transfers between devices: 39.7 us -> 15.8 us  [over_z(): return lax.ppermute(x, 'shard', xor_pairs(k))]
    ppermute x15 -> x14, starting transfers between devices: 23.5 us -> 40.3 us  [over_z(): return lax.ppermute(x, 'shard', xor_pairs(k))]
    pallas_call x3, Pallas kernels: 10.3 us -> 5.99 us  [the longest x2 4.34 us: update_weights(): pl.pallas_call(functools.partial(update_kernel, factor, blocks), out_shap...]
    pallas_call x13 -> x17, Pallas kernels: 2.02 us -> 3.19 us  [local_call(): pl.pallas_call(kernel, out_shape=[pltpu.VMEM(shape, dtype) for shape, dty...]
    ppermute x4, waiting for transfers between devices: 5.91 us -> 6.91 us  [over_y(): return lax.ppermute(x, 'tensor', xor_pairs(2))]
  transfers between devices with their start and end apart: 22 -> 21, of which waited for: 14 -> 14; matrix products, arithmetic and copies ran while one was open for 0% -> 0% of each run, Pallas kernels for 16% -> 17%
where the time goes in v4:
time: 87.4 us; the launch traced here: 87.3 us
  starting transfers between devices  44.1 us (50%)
  waiting for transfers between devices  22.8 us (26%)
  Pallas kernels  19 us (22%)
    ppermute x14, starting transfers between devices, over_z(): return lax.ppermute(x, 'shard', xor_pairs(k))  40.3 us
    ppermute x14, waiting for transfers between devices, over_z(): return lax.ppermute(x, 'shard', xor_pairs(k))  15.8 us
    ppermute x4, waiting for transfers between devices, over_y(): return lax.ppermute(x, 'tensor', xor_pairs(2))  6.91 us
    pallas_call x2, Pallas kernels, update_weights(): pl.pallas_call(functools.partial(update_kernel, factor, blocks), out_shap...  4.34 us
    pallas_call x1, Pallas kernels, newton_schulz_power(): pl.pallas_call(newton_schulz_kernel, out_shape=[jax.ShapeDtypeStruct((lay...  4.24 us
    ppermute x4, starting transfers between devices, over_y(): return lax.ppermute(x, 'tensor', xor_pairs(2))  3.22 us
    pallas_call x17, Pallas kernels, local_call(): pl.pallas_call(kernel, out_shape=[pltpu.VMEM(shape, dtype) for shape, dty...  3.19 us
    pallas_call x2, Pallas kernels, power_product(): pl.pallas_call(functools.partial(power_kernel, turn, scale), out_shape=[p...  2.99 us
  transfers between devices with their start and end apart: 21, of which 14 were waited for; matrix products, arithmetic and copies ran while one was open for 0% of the time, Pallas kernels for 17%

profile of v4, /device:TPU:0, one launch (start us, length us, event | category | flops | bytes accessed | tf_op | source)
XLA Modules:
  0.0 87.3 jit_solution(13287034881864104973)
XLA Ops:
  0.6 1.7 %prepare_basis.1 = (bf16[2,768,256]{2,1,0:T(8,128)(2,1)S(1)}, bf16[2,768,256]{2,1,0:T(8,128)(2,1)S(1)}) custom-call(f32[2,768,256]{2,1,0:T(8,128)} %basis_hbm.1), custom_call_target="tpu_custom_call" | custom-call | flops 3000000000 | tf_op jit(solution)/shard_map/prepare_basis/pallas_call | solution.py:161
  2.3 0.4 copy-done
  2.8 0.8 project.2
  3.6 3.1 %collective-permute-start = (bf16[416,256]{1,0:T(8,128)(2,1)S(1)}, bf16[416,256]{1,0:T(8,128)(2,1)S(1)}, u32[]{:S(2)}, u32[]{:S(2)}) collective-permute-start(bf16[416,256]{1,0:T(8,128)(2,1)S(1)} %get-tuple-element.102), channel_id=1, source_target_pairs={{0,8},{8,0},{16,24},{24,16},{1,9},{9,1},{17,25},{25,17},{2,10},{10... | collective-permute-start | bytes 638984 | tf_op jit(solution)/shard_map/ppermute | solution.py:457
  6.7 0.8 project.3
  7.5 4.4 %collective-permute-done.received_ref = bf16[416,256]{1,0:T(8,128)(2,1)S(1)} collective-permute-done((bf16[416,256]{1,0:T(8,128)(2,1)S(1)}, bf16[416,256]{1,0:T(8,128)(2,1)S(1)}, u32[]{:S(2)}, u32[]{:S(2)}) %collective-permute-start) | collective-permute-done | bytes 213024 | tf_op jit(solution)/shard_map/ppermute | solution.py:457
  11.9 0.3 add_coded.4
  12.3 1.8 %collective-permute-start.1 = (bf16[416,256]{1,0:T(8,128)(2,1)S(1)}, bf16[416,256]{1,0:T(8,128)(2,1)S(1)}, u32[]{:S(2)}, u32[]{:S(2)}) collective-permute-start(bf16[416,256]{1,0:T(8,128)(2,1)S(1)} %get-tuple-element.106), channel_id=1, source_target_pairs={{0,8},{8,0},{16,24},{24,16},{1,9},{9,1},{17,25},{25,17},{2,10},{10... | collective-permute-start | bytes 638984 | tf_op jit(solution)/shard_map/ppermute | solution.py:457
  14.1 2.5 %collective-permute-start.3 = (bf16[416,256]{1,0:T(8,128)(2,1)S(1)}, bf16[416,256]{1,0:T(8,128)(2,1)S(1)}, u32[]{:S(2)}, u32[]{:S(2)}) collective-permute-start(bf16[416,256]{1,0:T(8,128)(2,1)S(1)} %get-tuple-element.111), channel_id=1, source_target_pairs={{0,24},{8,16},{16,8},{24,0},{1,25},{9,17},{17,9},{25,1},{2,26},{10... | collective-permute-start | bytes 638984 | tf_op jit(solution)/shard_map/ppermute | solution.py:457
  16.5 3.2 %collective-permute-done.1.received_ref = bf16[416,256]{1,0:T(8,128)(2,1)S(1)} collective-permute-done((bf16[416,256]{1,0:T(8,128)(2,1)S(1)}, bf16[416,256]{1,0:T(8,128)(2,1)S(1)}, u32[]{:S(2)}, u32[]{:S(2)}) %collective-permute-start.1) | collective-permute-done | bytes 213024 | tf_op jit(solution)/shard_map/ppermute | solution.py:457
  19.8 0.3 add_coded.5
  20.1 9.3 %collective-permute-start.2 = (bf16[416,256]{1,0:T(8,128)(2,1)S(1)}, bf16[416,256]{1,0:T(8,128)(2,1)S(1)}, u32[]{:S(2)}, u32[]{:S(2)}) collective-permute-start(bf16[416,256]{1,0:T(8,128)(2,1)S(1)} %get-tuple-element.110), channel_id=1, source_target_pairs={{0,24},{8,16},{16,8},{24,0},{1,25},{9,17},{17,9},{25,1},{2,26},{10... | collective-permute-start | bytes 638984 | tf_op jit(solution)/shard_map/ppermute | solution.py:457
  29.5 1.6 %fetch.1 = (bf16[2,768,768]{2,1,0:T(8,128)(2,1)S(1)}, bf16[2,256,768]{2,1,0:T(8,128)(2,1)S(1)}, bf16[2,256,768]{2,1,0:T(8,128)(2,1)S(1)}) custom-call(bf16[2,768,768]{2,1,0:T(8,128)(2,1)} %weights_hbm, bf16[2,768,256]{2,1,0:T(8,128)(2,1)S(1)} %get-tuple-element.113.high_ref, bf16[2,768,256]{2,1,0:T(8,128)(2,1)S(1)} %get-tuple-element.114.low_ref), custom_call_target="tpu_custom_call" | custom-call | tf_op jit(solution)/shard_map/fetch/pallas_call | solution.py:188
  31.1 0.3 add_coded.6
  31.5 0.1 collective-permute-start.5
  31.6 1.9 %collective-permute-done.2.received_ref = bf16[416,256]{1,0:T(8,128)(2,1)S(1)} collective-permute-done((bf16[416,256]{1,0:T(8,128)(2,1)S(1)}, bf16[416,256]{1,0:T(8,128)(2,1)S(1)}, u32[]{:S(2)}, u32[]{:S(2)}) %collective-permute-start.2) | collective-permute-done | bytes 213024 | tf_op jit(solution)/shard_map/ppermute | solution.py:457
  33.5 0.3 add_coded.7
  33.8 1.6 %collective-permute-start.4 = (bf16[416,256]{1,0:T(8,128)(2,1)S(1)}, bf16[416,256]{1,0:T(8,128)(2,1)S(1)}, u32[]{:S(2)}, u32[]{:S(2)}) collective-permute-start(bf16[416,256]{1,0:T(8,128)(2,1)S(1)} %get-tuple-element.122), channel_id=1, source_target_pairs={{0,8},{8,0},{16,24},{24,16},{1,9},{9,1},{17,25},{25,17},{2,10},{10... | collective-permute-start | bytes 638984 | tf_op jit(solution)/shard_map/ppermute | solution.py:457
  35.4 2.6 %collective-permute-done.5.given_ref = bf16[416,256]{1,0:T(8,128)(2,1)S(1)} collective-permute-done((bf16[416,256]{1,0:T(8,128)(2,1)S(1)}, bf16[416,256]{1,0:T(8,128)(2,1)S(1)}, u32[]{:S(2)}, u32[]{:S(2)}) %collective-permute-start.5) | collective-permute-done | bytes 213024 | tf_op jit(solution)/shard_map/ppermute | solution.py:457
  38.0 1.5 %power.2 = (f32[128,768]{1,0:T(8,128)S(1)}, f32[128,768]{1,0:T(8,128)S(1)}, f32[2,192,256]{2,1,0:T(8,128)}, f32[2,192,256]{2,1,0:T(8,128)}, bf16[208,256]{1,0:T(8,128)(2,1)S(1)}) custom-call(bf16[1,2,768,768]{3,2,1,0:T(8,128)(2,1)S(1)} %copy-done, f32[2,192,256]{2,1,0:T(8,128)S(1)} %copy-done.1, f32[2,192,256]{2,1,0:T(8,128)S(1)} %copy-done.2, ...), custom_call_target="tpu_custom_call" | custom-call | flops 5000000000 | tf_op jit(solution)/shard_map/power/pallas_call | solution.py:285
  39.5 0.1 collective-permute-start.6
  39.6 0.5 collective-permute-start.7
  40.1 0.2 collective-permute-done.4.given_ref
  40.3 1.5 %power.3 = (f32[128,768]{1,0:T(8,128)S(1)}, f32[128,768]{1,0:T(8,128)S(1)}, f32[2,192,256]{2,1,0:T(8,128)}, f32[2,192,256]{2,1,0:T(8,128)}, bf16[2,208,256]{2,1,0:T(8,128)(2,1)S(1)}) custom-call(bf16[1,2,768,768]{3,2,1,0:T(8,128)(2,1)S(1)} %copy-done, f32[2,192,256]{2,1,0:T(8,128)S(1)} %copy-done.1, ...), custom_call_target="tpu_custom_call", output_to_operand_aliasing={{2}: (5, {}), {3}: (6, {})} | custom-call | flops 5000000000 | tf_op jit(solution)/shard_map/power/pallas_call | solution.py:285
  41.9 1.6 %collective-permute-start.9 = (f32[64,768]{1,0:T(8,128)S(1)}, f32[64,768]{1,0:T(8,128)S(1)}, u32[]{:S(2)}, u32[]{:S(2)}) collective-permute-start(f32[64,768]{1,0:T(8,128)S(1)} %get-tuple-element.143), channel_id=1, source_target_pairs={{0,4},{2,6},{4,0},{6,2},{1,5},{3,7},{5,1},{7,3},{8,12},{10,14},{12... | collective-permute-start | bytes 589832 | tf_op jit(solution)/shard_map/ppermute | solution.py:465
  43.5 3.8 %collective-permute-start.8 = (bf16[2,208,256]{2,1,0:T(8,128)(2,1)S(1)}, bf16[2,208,256]{2,1,0:T(8,128)(2,1)S(1)}, u32[]{:S(2)}, u32[]{:S(2)}) collective-permute-start(bf16[2,208,256]{2,1,0:T(8,128)(2,1)S(1)} %get-tuple-element.168.a_ref), channel_id=1, source_target_pairs={{0,24},{8,16},{16,8},{24,0},{1,25},{9,17},{17,9},{25,1},{2,26},{10... | collective-permute-start | bytes 638984 | tf_op jit(solution)/shard_map/ppermute | solution.py:457
  47.3 0.5 collective-permute-start.11
  47.8 1.1 %collective-permute-done.9.received_ref = f32[64,768]{1,0:T(8,128)S(1)} collective-permute-done((f32[64,768]{1,0:T(8,128)S(1)}, f32[64,768]{1,0:T(8,128)S(1)}, u32[]{:S(2)}, u32[]{:S(2)}) %collective-permute-start.9) | collective-permute-done | bytes 196640 | tf_op jit(solution)/shard_map/ppermute | solution.py:465
  48.9 2.8 %collective-permute-start.10 = (f32[32,768]{1,0:T(8,128)S(1)}, f32[32,768]{1,0:T(8,128)S(1)}, u32[]{:S(2)}, u32[]{:S(2)}) collective-permute-start(f32[32,768]{1,0:T(8,128)S(1)} %get-tuple-element.147), channel_id=1, source_target_pairs={{0,8},{8,0},{16,24},{24,16},{1,9},{9,1},{17,25},{25,17},{2,10},{10... | collective-permute-start | bytes 294920 | tf_op jit(solution)/shard_map/ppermute | solution.py:457
  51.7 2.0 %collective-permute-done.11.received_ref = f32[64,768]{1,0:T(8,128)S(1)} collective-permute-done((f32[64,768]{1,0:T(8,128)S(1)}, f32[64,768]{1,0:T(8,128)S(1)}, u32[]{:S(2)}, u32[]{:S(2)}) %collective-permute-start.11) | collective-permute-done | bytes 196640 | tf_op jit(solution)/shard_map/ppermute | solution.py:465
  53.7 1.4 %collective-permute-start.13 = (f32[32,768]{1,0:T(8,128)S(1)}, f32[32,768]{1,0:T(8,128)S(1)}, u32[]{:S(2)}, u32[]{:S(2)}) collective-permute-start(f32[32,768]{1,0:T(8,128)S(1)} %get-tuple-element.157), channel_id=1, source_target_pairs={{0,8},{8,0},{16,24},{24,16},{1,9},{9,1},{17,25},{25,17},{2,10},{10... | collective-permute-start | bytes 294920 | tf_op jit(solution)/shard_map/ppermute | solution.py:457
  55.1 3.3 %collective-permute-start.12 = (f32[32,768]{1,0:T(8,128)S(1)}, f32[32,768]{1,0:T(8,128)S(1)}, u32[]{:S(2)}, u32[]{:S(2)}) collective-permute-start(f32[32,768]{1,0:T(8,128)S(1)} %add.4.own_ref), channel_id=1, source_target_pairs={{0,24},{8,16},{16,8},{24,0},{1,25},{9,17},{17,9},{25,1},{2,26},{10... | collective-permute-start | bytes 294920 | tf_op jit(solution)/shard_map/ppermute | solution.py:457
  58.4 3.2 %collective-permute-start.15 = (f32[32,768]{1,0:T(8,128)S(1)}, f32[32,768]{1,0:T(8,128)S(1)}, u32[]{:S(2)}, u32[]{:S(2)}) collective-permute-start(f32[32,768]{1,0:T(8,128)S(1)} %add.5.own_ref), channel_id=1, source_target_pairs={{0,24},{8,16},{16,8},{24,0},{1,25},{9,17},{17,9},{25,1},{2,26},{10... | collective-permute-start | bytes 294920 | tf_op jit(solution)/shard_map/ppermute | solution.py:457
  61.6 0.1 collective-permute-done.12.received_ref
  61.8 4.6 %collective-permute-start.14 = (f32[32,768]{1,0:T(8,128)S(1)}, f32[32,768]{1,0:T(8,128)S(1)}, u32[]{:S(2)}, u32[]{:S(2)}) collective-permute-start(f32[32,768]{1,0:T(8,128)S(1)} %add.6.own_ref), channel_id=1, source_target_pairs={{0,8},{8,0},{16,24},{24,16},{1,9},{9,1},{17,25},{25,17},{2,10},{10... | collective-permute-start | bytes 294920 | tf_op jit(solution)/shard_map/ppermute | solution.py:457
  66.4 1.3 %collective-permute-start.17 = (f32[32,768]{1,0:T(8,128)S(1)}, f32[32,768]{1,0:T(8,128)S(1)}, u32[]{:S(2)}, u32[]{:S(2)}) collective-permute-start(f32[32,768]{1,0:T(8,128)S(1)} %add.7.own_ref), channel_id=1, source_target_pairs={{0,8},{8,0},{16,24},{24,16},{1,9},{9,1},{17,25},{25,17},{2,10},{10... | collective-permute-start | bytes 294920 | tf_op jit(solution)/shard_map/ppermute | solution.py:457
  67.7 2.1 %collective-permute-done.14.received_ref = f32[32,768]{1,0:T(8,128)S(1)} collective-permute-done((f32[32,768]{1,0:T(8,128)S(1)}, f32[32,768]{1,0:T(8,128)S(1)}, u32[]{:S(2)}, u32[]{:S(2)}) %collective-permute-start.14) | collective-permute-done | bytes 98336 | tf_op jit(solution)/shard_map/ppermute | solution.py:457
  69.8 0.1 collective-permute-start.16
  69.9 1.2 %collective-permute-done.17.received_ref = f32[32,768]{1,0:T(8,128)S(1)} collective-permute-done((f32[32,768]{1,0:T(8,128)S(1)}, f32[32,768]{1,0:T(8,128)S(1)}, u32[]{:S(2)}, u32[]{:S(2)}) %collective-permute-start.17) | collective-permute-done | bytes 98336 | tf_op jit(solution)/shard_map/ppermute | solution.py:457
  71.2 1.6 %collective-permute-start.18 = (bf16[2,2,208,256]{3,2,1,0:T(8,128)(2,1)S(1)}, bf16[2,2,208,256]{3,2,1,0:T(8,128)(2,1)S(1)}, u32[]{:S(2)}, u32[]{:S(2)}) collective-permute-start(bf16[2,2,208,256]{3,2,1,0:T(8,128)(2,1)S(1)} %stack.1), channel_id=1, source_target_pairs={{0,8},{8,0},{16,24},{24,16},{1,9},{9,1},{17,25},{25,17},{2,10},{10... | collective-permute-start | bytes 1277960 | tf_op jit(solution)/shard_map/ppermute | solution.py:457
  72.7 1.1 %collective-permute-start.19 = (f32[64,768]{1,0:T(8,128)S(1)}, f32[64,768]{1,0:T(8,128)S(1)}, u32[]{:S(2)}, u32[]{:S(2)}) collective-permute-start(f32[64,768]{1,0:T(8,128)S(1)} %join.3.refs_2_), channel_id=1, source_target_pairs={{0,4},{2,6},{4,0},{6,2},{1,5},{3,7},{5,1},{7,3},{8,12},{10,14},{12... | collective-permute-start | bytes 589832 | tf_op jit(solution)/shard_map/ppermute | solution.py:465
  73.8 3.7 %collective-permute-done.16.refs_1_ = f32[64,768]{1,0:T(8,128)S(1)} collective-permute-done((f32[64,768]{1,0:T(8,128)S(1)}, f32[64,768]{1,0:T(8,128)S(1)}, u32[]{:S(2)}, u32[]{:S(2)}) %collective-permute-start.16) | collective-permute-done | bytes 196640 | tf_op jit(solution)/shard_map/ppermute | solution.py:465
  77.5 2.2 %update_weights.2.refs_2_ = bf16[2,768,768]{2,1,0:T(8,128)(2,1)} custom-call(bf16[2,768,768]{2,1,0:T(8,128)(2,1)S(1)} %get-tuple-element.170.weights_ref, bf16[2,256,768]{2,1,0:T(8,128)(2,1)S(1)} %get-tuple-element.171.high_ref, bf16[2,256,768]{2,1,0:T(8,128)(2,1)S(1)} %get-tuple-element.172.low_ref, bf16[1,2,208,256]{3,2,1,0:T(8,128)(2,1)S(1)} %bitcast.2, ...), custom_call_target="tpu_custom_call" | custom-call | flops 3000000000 | tf_op jit(solution)/shard_map/update_weights/pallas_call | solution.py:439
  79.6 0.1 collective-permute-done.19.refs_3_
  79.8 4.2 %newton_schulz.1 = (f32[2,768,256]{2,1,0:T(8,128)}, f32[768,256]{1,0:T(8,128)S(1)}) custom-call(f32[64,768]{1,0:T(8,128)S(1)} %join.2.refs_0_, f32[64,768]{1,0:T(8,128)S(1)} %collective-permute-done.16.refs_1_, f32[64,768]{1,0:T(8,128)S(1)} %join.3.refs_2_, f32[64,768]{1,0:T(8,128)S(1)} %collective-permute-done.19.refs_3_), custom_call_target="tpu_custom_call" | custom-call | tf_op jit(solution)/shard_map/newton_schulz/pallas_call | solution.py:370
  84.1 2.2 %update_weights.3 = bf16[2,768,768]{2,1,0:T(8,128)(2,1)} custom-call(bf16[2,768,768]{2,1,0:T(8,128)(2,1)S(1)} %get-tuple-element.170.weights_ref, bf16[2,256,768]{2,1,0:T(8,128)(2,1)S(1)} %get-tuple-element.171.high_ref, bf16[2,256,768]{2,1,0:T(8,128)(2,1)S(1)} %get-tuple-element.172.low_ref, ...), custom_call_target="tpu_custom_call", output_to_operand_aliasing={{}: (5, {})} | custom-call | flops 8000000000 | tf_op jit(solution)/shard_map/update_weights/pallas_call | solution.py:439
  86.3 0.1 collective-permute-done.20.layer_ref
  86.4 0.9 %put_layer.1 = f32[2,768,256]{2,1,0:T(8,128)} custom-call(f32[768,256]{1,0:T(8,128)S(1)} %collective-permute-done.20.layer_ref, f32[2,768,256]{2,1,0:T(8,128)} %get-tuple-element.185.whole_ref), custom_call_target="tpu_custom_call", output_to_operand_aliasing={{}: (1, {})} | custom-call | tf_op jit(solution)/shard_map/put_layer/pallas_call | solution.py:396
  (25 shorter events, 0.4 us)
Async XLA Ops:
  0.6 2.1 %copy-start = (bf16[1,2,768,768]{3,2,1,0:T(8,128)(2,1)S(1)}, bf16[1,2,768,768]{3,2,1,0:T(8,128)(2,1)}, u32[]{:S(2)}) copy-start(bf16[1,2,768,768]{3,2,1,0:T(8,128)(2,1)} %grads_ref.6) | copy-start | bytes 7077892
  3.6 8.3 %collective-permute-start = (bf16[416,256]{1,0:T(8,128)(2,1)S(1)}, bf16[416,256]{1,0:T(8,128)(2,1)S(1)}, u32[]{:S(2)}, u32[]{:S(2)}) collective-permute-start(bf16[416,256]{1,0:T(8,128)(2,1)S(1)} %get-tuple-element.102), channel_id=1, source_target_pairs={{0,8},{8,0},{16,24},{24,16},{1,9},{9,1},{17,25},{25,17},{2,10},{10... | collective-permute-start | bytes 638984 | tf_op jit(solution)/shard_map/ppermute | solution.py:457
  12.3 7.5 %collective-permute-start.1 = (bf16[416,256]{1,0:T(8,128)(2,1)S(1)}, bf16[416,256]{1,0:T(8,128)(2,1)S(1)}, u32[]{:S(2)}, u32[]{:S(2)}) collective-permute-start(bf16[416,256]{1,0:T(8,128)(2,1)S(1)} %get-tuple-element.106), channel_id=1, source_target_pairs={{0,8},{8,0},{16,24},{24,16},{1,9},{9,1},{17,25},{25,17},{2,10},{10... | collective-permute-start | bytes 638984 | tf_op jit(solution)/shard_map/ppermute | solution.py:457
  14.1 17.1 %collective-permute-start.3 = (bf16[416,256]{1,0:T(8,128)(2,1)S(1)}, bf16[416,256]{1,0:T(8,128)(2,1)S(1)}, u32[]{:S(2)}, u32[]{:S(2)}) collective-permute-start(bf16[416,256]{1,0:T(8,128)(2,1)S(1)} %get-tuple-element.111), channel_id=1, source_target_pairs={{0,24},{8,16},{16,8},{24,0},{1,25},{9,17},{17,9},{25,1},{2,26},{10... | collective-permute-start | bytes 638984 | tf_op jit(solution)/shard_map/ppermute | solution.py:457
  20.1 17.9 %copy-start.1 = (f32[2,192,256]{2,1,0:T(8,128)S(1)}, f32[2,192,256]{2,1,0:T(8,128)}, u32[]{:S(2)}) copy-start(f32[2,192,256]{2,1,0:T(8,128)} %first_ref.3) | copy-start | bytes 1179652
  20.1 17.9 %copy-start.2 = (f32[2,192,256]{2,1,0:T(8,128)S(1)}, f32[2,192,256]{2,1,0:T(8,128)}, u32[]{:S(2)}) copy-start(f32[2,192,256]{2,1,0:T(8,128)} %second_ref.3) | copy-start | bytes 1179652
  20.1 13.3 %collective-permute-start.2 = (bf16[416,256]{1,0:T(8,128)(2,1)S(1)}, bf16[416,256]{1,0:T(8,128)(2,1)S(1)}, u32[]{:S(2)}, u32[]{:S(2)}) collective-permute-start(bf16[416,256]{1,0:T(8,128)(2,1)S(1)} %get-tuple-element.110), channel_id=1, source_target_pairs={{0,24},{8,16},{16,8},{24,0},{1,25},{9,17},{17,9},{25,1},{2,26},{10... | collective-permute-start | bytes 638984 | tf_op jit(solution)/shard_map/ppermute | solution.py:457
  31.5 6.5 %collective-permute-start.5 = (bf16[416,256]{1,0:T(8,128)(2,1)S(1)}, bf16[416,256]{1,0:T(8,128)(2,1)S(1)}, u32[]{:S(2)}, u32[]{:S(2)}) collective-permute-start(bf16[416,256]{1,0:T(8,128)(2,1)S(1)} %get-tuple-element.123), channel_id=1, source_target_pairs={{0,8},{8,0},{16,24},{24,16},{1,9},{9,1},{17,25},{25,17},{2,10},{10... | collective-permute-start | bytes 638984 | tf_op jit(solution)/shard_map/ppermute | solution.py:457
  33.8 6.5 %collective-permute-start.4 = (bf16[416,256]{1,0:T(8,128)(2,1)S(1)}, bf16[416,256]{1,0:T(8,128)(2,1)S(1)}, u32[]{:S(2)}, u32[]{:S(2)}) collective-permute-start(bf16[416,256]{1,0:T(8,128)(2,1)S(1)} %get-tuple-element.122), channel_id=1, source_target_pairs={{0,8},{8,0},{16,24},{24,16},{1,9},{9,1},{17,25},{25,17},{2,10},{10... | collective-permute-start | bytes 638984 | tf_op jit(solution)/shard_map/ppermute | solution.py:457
  39.5 2.4 %collective-permute-start.6 = (f32[128,768]{1,0:T(8,128)S(1)}, f32[128,768]{1,0:T(8,128)S(1)}, u32[]{:S(2)}, u32[]{:S(2)}) collective-permute-start(f32[128,768]{1,0:T(8,128)S(1)} %get-tuple-element.134), channel_id=1, source_target_pairs={{0,2},{2,0},{4,6},{6,4},{1,3},{3,1},{5,7},{7,5},{8,10},{10,8},{12,... | collective-permute-start | bytes 1179656 | tf_op jit(solution)/shard_map/ppermute | solution.py:461
  39.6 2.3 %collective-permute-start.7 = (f32[128,768]{1,0:T(8,128)S(1)}, f32[128,768]{1,0:T(8,128)S(1)}, u32[]{:S(2)}, u32[]{:S(2)}) collective-permute-start(f32[128,768]{1,0:T(8,128)S(1)} %get-tuple-element.126), channel_id=1, source_target_pairs={{0,2},{2,0},{4,6},{6,4},{1,3},{3,1},{5,7},{7,5},{8,10},{10,8},{12,... | collective-permute-start | bytes 1179656 | tf_op jit(solution)/shard_map/ppermute | solution.py:461
  41.9 7.0 %collective-permute-start.9 = (f32[64,768]{1,0:T(8,128)S(1)}, f32[64,768]{1,0:T(8,128)S(1)}, u32[]{:S(2)}, u32[]{:S(2)}) collective-permute-start(f32[64,768]{1,0:T(8,128)S(1)} %get-tuple-element.143), channel_id=1, source_target_pairs={{0,4},{2,6},{4,0},{6,2},{1,5},{3,7},{5,1},{7,3},{8,12},{10,14},{12... | collective-permute-start | bytes 589832 | tf_op jit(solution)/shard_map/ppermute | solution.py:465
  43.5 11.6 %collective-permute-start.8 = (bf16[2,208,256]{2,1,0:T(8,128)(2,1)S(1)}, bf16[2,208,256]{2,1,0:T(8,128)(2,1)S(1)}, u32[]{:S(2)}, u32[]{:S(2)}) collective-permute-start(bf16[2,208,256]{2,1,0:T(8,128)(2,1)S(1)} %get-tuple-element.168.a_ref), channel_id=1, source_target_pairs={{0,24},{8,16},{16,8},{24,0},{1,25},{9,17},{17,9},{25,1},{2,26},{10... | collective-permute-start | bytes 638984 | tf_op jit(solution)/shard_map/ppermute | solution.py:457
  47.3 6.4 %collective-permute-start.11 = (f32[64,768]{1,0:T(8,128)S(1)}, f32[64,768]{1,0:T(8,128)S(1)}, u32[]{:S(2)}, u32[]{:S(2)}) collective-permute-start(f32[64,768]{1,0:T(8,128)S(1)} %get-tuple-element.148), channel_id=1, source_target_pairs={{0,4},{2,6},{4,0},{6,2},{1,5},{3,7},{5,1},{7,3},{8,12},{10,14},{12... | collective-permute-start | bytes 589832 | tf_op jit(solution)/shard_map/ppermute | solution.py:465
  48.9 6.2 %collective-permute-start.10 = (f32[32,768]{1,0:T(8,128)S(1)}, f32[32,768]{1,0:T(8,128)S(1)}, u32[]{:S(2)}, u32[]{:S(2)}) collective-permute-start(f32[32,768]{1,0:T(8,128)S(1)} %get-tuple-element.147), channel_id=1, source_target_pairs={{0,8},{8,0},{16,24},{24,16},{1,9},{9,1},{17,25},{25,17},{2,10},{10... | collective-permute-start | bytes 294920 | tf_op jit(solution)/shard_map/ppermute | solution.py:457
  53.7 4.7 %collective-permute-start.13 = (f32[32,768]{1,0:T(8,128)S(1)}, f32[32,768]{1,0:T(8,128)S(1)}, u32[]{:S(2)}, u32[]{:S(2)}) collective-permute-start(f32[32,768]{1,0:T(8,128)S(1)} %get-tuple-element.157), channel_id=1, source_target_pairs={{0,8},{8,0},{16,24},{24,16},{1,9},{9,1},{17,25},{25,17},{2,10},{10... | collective-permute-start | bytes 294920 | tf_op jit(solution)/shard_map/ppermute | solution.py:457
  55.1 6.6 %collective-permute-start.12 = (f32[32,768]{1,0:T(8,128)S(1)}, f32[32,768]{1,0:T(8,128)S(1)}, u32[]{:S(2)}, u32[]{:S(2)}) collective-permute-start(f32[32,768]{1,0:T(8,128)S(1)} %add.4.own_ref), channel_id=1, source_target_pairs={{0,24},{8,16},{16,8},{24,0},{1,25},{9,17},{17,9},{25,1},{2,26},{10... | collective-permute-start | bytes 294920 | tf_op jit(solution)/shard_map/ppermute | solution.py:457
  58.4 8.0 %collective-permute-start.15 = (f32[32,768]{1,0:T(8,128)S(1)}, f32[32,768]{1,0:T(8,128)S(1)}, u32[]{:S(2)}, u32[]{:S(2)}) collective-permute-start(f32[32,768]{1,0:T(8,128)S(1)} %add.5.own_ref), channel_id=1, source_target_pairs={{0,24},{8,16},{16,8},{24,0},{1,25},{9,17},{17,9},{25,1},{2,26},{10... | collective-permute-start | bytes 294920 | tf_op jit(solution)/shard_map/ppermute | solution.py:457
  61.8 8.1 %collective-permute-start.14 = (f32[32,768]{1,0:T(8,128)S(1)}, f32[32,768]{1,0:T(8,128)S(1)}, u32[]{:S(2)}, u32[]{:S(2)}) collective-permute-start(f32[32,768]{1,0:T(8,128)S(1)} %add.6.own_ref), channel_id=1, source_target_pairs={{0,8},{8,0},{16,24},{24,16},{1,9},{9,1},{17,25},{25,17},{2,10},{10... | collective-permute-start | bytes 294920 | tf_op jit(solution)/shard_map/ppermute | solution.py:457
  66.4 4.7 %collective-permute-start.17 = (f32[32,768]{1,0:T(8,128)S(1)}, f32[32,768]{1,0:T(8,128)S(1)}, u32[]{:S(2)}, u32[]{:S(2)}) collective-permute-start(f32[32,768]{1,0:T(8,128)S(1)} %add.7.own_ref), channel_id=1, source_target_pairs={{0,8},{8,0},{16,24},{24,16},{1,9},{9,1},{17,25},{25,17},{2,10},{10... | collective-permute-start | bytes 294920 | tf_op jit(solution)/shard_map/ppermute | solution.py:457
  69.8 7.6 %collective-permute-start.16 = (f32[64,768]{1,0:T(8,128)S(1)}, f32[64,768]{1,0:T(8,128)S(1)}, u32[]{:S(2)}, u32[]{:S(2)}) collective-permute-start(f32[64,768]{1,0:T(8,128)S(1)} %join.2.refs_0_), channel_id=1, source_target_pairs={{0,4},{2,6},{4,0},{6,2},{1,5},{3,7},{5,1},{7,3},{8,12},{10,14},{12... | collective-permute-start | bytes 589832 | tf_op jit(solution)/shard_map/ppermute | solution.py:465
  71.2 13.0 %collective-permute-start.18 = (bf16[2,2,208,256]{3,2,1,0:T(8,128)(2,1)S(1)}, bf16[2,2,208,256]{3,2,1,0:T(8,128)(2,1)S(1)}, u32[]{:S(2)}, u32[]{:S(2)}) collective-permute-start(bf16[2,2,208,256]{3,2,1,0:T(8,128)(2,1)S(1)} %stack.1), channel_id=1, source_target_pairs={{0,8},{8,0},{16,24},{24,16},{1,9},{9,1},{17,25},{25,17},{2,10},{10... | collective-permute-start | bytes 1277960 | tf_op jit(solution)/shard_map/ppermute | solution.py:457
  72.7 7.1 %collective-permute-start.19 = (f32[64,768]{1,0:T(8,128)S(1)}, f32[64,768]{1,0:T(8,128)S(1)}, u32[]{:S(2)}, u32[]{:S(2)}) collective-permute-start(f32[64,768]{1,0:T(8,128)S(1)} %join.3.refs_2_), channel_id=1, source_target_pairs={{0,4},{2,6},{4,0},{6,2},{1,5},{3,7},{5,1},{7,3},{8,12},{10,14},{12... | collective-permute-start | bytes 589832 | tf_op jit(solution)/shard_map/ppermute | solution.py:465
  84.0 2.4 %collective-permute-start.20 = (f32[768,256]{1,0:T(8,128)S(1)}, f32[768,256]{1,0:T(8,128)S(1)}, u32[]{:S(2)}, u32[]{:S(2)}) collective-permute-start(f32[768,256]{1,0:T(8,128)S(1)} %get-tuple-element.181), channel_id=1, source_target_pairs={{0,2},{2,0},{4,6},{6,4},{1,3},{3,1},{5,7},{7,5},{8,10},{10,8},{12,... | collective-permute-start | bytes 2359304 | tf_op jit(solution)/shard_map/ppermute | solution.py:461

commit v5 on v4

--- a/solution.py
+++ b/solution.py
@@ -145,29 +145,31 @@
     return jnp.where(code < 0, -size, size)
 
 
-def prepare_kernel(basis_hbm, high_ref, low_ref, buffer, sems):
+def prepare_kernel(grads_hbm, basis_hbm, grads_ref, high_ref, low_ref, buffer, sems):
     layers = buffer.shape[0]
     copies = [pltpu.make_async_copy(basis_hbm.at[layer], buffer.at[layer], sems.at[layer]) for layer in range(layers)]
+    copies += [pltpu.make_async_copy(grads_hbm.at[0, layer], grads_ref.at[0, layer], sems.at[layers + layer]) for layer in range(layers)]
     for copy in copies:
         copy.start()
-    for layer, copy in enumerate(copies):
+    for layer in range(layers):
+        copies[layer].wait()
+        high_ref[layer], low_ref[layer] = split(buffer[layer])
+    for copy in copies[layers:]:
         copy.wait()
-        high_ref[layer], low_ref[layer] = split(buffer[layer])
-
-
-def prepare_basis(basis):
+
+
+def prepare(grads, basis):
     layers = basis.shape[0]
-    vmem = pl.BlockSpec(memory_space=pltpu.VMEM)
+    vmem, hbm = pl.BlockSpec(memory_space=pltpu.VMEM), pl.BlockSpec(memory_space=pltpu.HBM)
     return pl.pallas_call(
         prepare_kernel,
-        out_shape=[pltpu.VMEM(basis.shape, jnp.bfloat16)] * 2,
-        in_specs=[pl.BlockSpec(memory_space=pltpu.HBM)],
-        out_specs=[vmem] * 2,
-        scratch_shapes=[pltpu.VMEM(basis.shape, jnp.float32), pltpu.SemaphoreType.DMA((layers,))],
+        out_shape=[pltpu.VMEM(grads.shape, grads.dtype)] + [pltpu.VMEM(basis.shape, jnp.bfloat16)] * 2,
+        in_specs=[hbm, hbm],
+        out_specs=[vmem] * 3,
+        scratch_shapes=[pltpu.VMEM(basis.shape, jnp.float32), pltpu.SemaphoreType.DMA((2 * layers,))],
         compiler_params=params(12),
-        cost_estimate=cost(3e9),
-        name="prepare_basis",
-    )(pltpu.with_memory_space_constraint(basis, pltpu.HBM))
+        name="prepare",
+    )(*[pltpu.with_memory_space_constraint(x, pltpu.HBM) for x in (grads, basis)])
 
 
 def fetch_kernel(weights_hbm, high_ref, low_ref, weights_ref, high_t_ref, low_t_ref, sems):
@@ -217,18 +219,55 @@
     return dot(a[0], b) + dot(a[1], b) if isinstance(a, tuple) else dot(a, b[0]) + dot(a, b[1])
 
 
-def project_kernel(turn, grads_ref, high_ref, low_ref, out_ref, code_ref):
+def give_kernel(grads_hbm, basis_hbm, code_ref, blocks, basis_ref, sems):
+    place = Place()
+    layer, rows = place.layer(0), blocks.shape[1]
+    copies = [pltpu.make_async_copy(basis_hbm.at[layer], basis_ref, sems.at[2])]
+    for j in range(2):
+        source = grads_hbm.at[0, layer, pl.ds(pl.multiple_of(place.gives(j) * rows, rows), rows)]
+        copies.append(pltpu.make_async_copy(source, blocks.at[j], sems.at[j]))
+    for copy in copies:
+        copy.start()
+    copies[0].wait()
+    basis = split(basis_ref[...])
+    parts = []
+    for j in range(2):
+        copies[1 + j].wait()
+        parts.append(exact_dot(blocks[j], basis))
+    code_blocks(code_ref, parts)
+
+
+def give(grads, basis):
+    rows, (_, width, rank) = grads.shape[2] // 4, basis.shape
+    vmem, hbm = pl.BlockSpec(memory_space=pltpu.VMEM), pl.BlockSpec(memory_space=pltpu.HBM)
+    return pl.pallas_call(
+        give_kernel,
+        out_shape=pltpu.VMEM((2 * (rows + 16), rank), jnp.bfloat16),
+        in_specs=[hbm, hbm],
+        out_specs=vmem,
+        scratch_shapes=[
+            pltpu.VMEM((2, rows, width), grads.dtype),
+            pltpu.VMEM((width, rank), jnp.float32),
+            pltpu.SemaphoreType.DMA((3,)),
+        ],
+        compiler_params=params(8),
+        name="give",
+    )(*[pltpu.with_memory_space_constraint(x, pltpu.HBM) for x in (grads, basis)])
+
+
+def project_kernel(turn, grads_ref, high_ref, low_ref, out_ref, *code_refs):
     place = Place()
     layer, rows = place.layer(turn), out_ref.shape[0] // 2
     basis = high_ref[layer], low_ref[layer]
-    code_blocks(code_ref, [exact_dot(rows_of(grads_ref, layer, place.gives(j), rows), basis) for j in range(2)])
+    for code_ref in code_refs:
+        code_blocks(code_ref, [exact_dot(rows_of(grads_ref, layer, place.gives(j), rows), basis) for j in range(2)])
     for j in range(2):
         out_ref[j * rows : (j + 1) * rows] = exact_dot(rows_of(grads_ref, layer, place.keeps(j), rows), basis)
 
 
 def project(grads, basis, turn):
     rows, rank = grads.shape[2] // 4, basis[0].shape[2]
-    outs = [((2 * rows, rank), jnp.float32), ((2 * (rows + 16), rank), jnp.bfloat16)]
+    outs = [((2 * rows, rank), jnp.float32)] + [((2 * (rows + 16), rank), jnp.bfloat16)] * turn
     return local_call(functools.partial(project_kernel, turn), outs, grads, *basis, name="project")
 
 
@@ -294,7 +333,7 @@
         + [pltpu.SemaphoreType.DMA((2,))],
         input_output_aliases={count: HALVES, count + 1: HALVES + 1} if before else {},
         compiler_params=params(12),
-        cost_estimate=cost(5e9),
+        cost_estimate=cost(5e9 * turn),
         name="power",
     )(*operands, *before[:2], *in_vmem(*before[2:]))
 
@@ -485,7 +524,6 @@
     layers, rows = grads.shape[1], first_moment.shape[1]
     order = Order()
 
-    high, low = prepare_basis(basis)
 
     def product(turn, kept, given, *before):
         *halves, one, two, code = power_product(
@@ -513,18 +551,18 @@
     next_z = lambda x: over_z(x, 1)
     opposite_z = lambda x: over_z(x, 3)
 
-    codes = []
-    kept = []
-    for turn in range(2):
-        x, code = project(order.step(grads)[0], (high, low), turn)
-        kept.append(order.through(x))
-        codes.append(code)
-    first, code = add_code(kept[0], next_z(codes[0]))
-    first = first, opposite_z(code)
-    second, code = add_code(kept[1], next_z(order.step(codes[1])[0]))
-    second = second, opposite_z(code)
+    code = order.through(give(grads, basis))
+    received = next_z(code)
+    grads, high, low = prepare(*order.step(grads, basis))
+    (kept,) = project(grads, (high, low), 0)
+    second, second_code = project(*order.step(grads, order.through(kept))[:1], (high, low), 1)
+    order.through(second)
     weights, *turned = fetch(*order.step(weights, high, low))
     order.through(weights)
+    first, code = add_code(kept, received)
+    first = first, opposite_z(code)
+    second, code = add_code(second, next_z(order.step(second_code)[0]))
+    second = second, opposite_z(code)
     sums = []
     for pair in (first, second):
         x, code = add_code(*pair)

time: 87.4 us -> 84.1 us (0.962)
  waiting for transfers between devices: 22.8 us -> 19.9 us
  Pallas kernels: 19 us -> 21.5 us
  starting transfers between devices: 44.1 us -> 41.6 us
    ppermute x14, starting transfers between devices: 40.3 us -> 36 us  [over_z(): return lax.ppermute(x, 'shard', xor_pairs(k))]
    ppermute x4, waiting for transfers between devices: 6.91 us -> 3.43 us  [over_y(): return lax.ppermute(x, 'tensor', xor_pairs(2))]
    pallas_call x1 -> x2, Pallas kernels: 1.68 us -> 4.42 us  [the longest x1 2.28 us: give(): pl.pallas_call(give_kernel, out_shape=pltpu.VMEM((2 * (rows + 16), rank),...]
    ppermute x4, starting transfers between devices: 3.22 us -> 4.97 us  [over_y(): return lax.ppermute(x, 'tensor', xor_pairs(2))]
  transfers between devices with their start and end apart: 21 -> 21, of which waited for: 14 -> 14; matrix products, arithmetic and copies ran while one was open for 0% -> 0% of each run, Pallas kernels for 17% -> 21%
where the time goes in v5:
time: 84.1 us; the launch traced here: 83.9 us
  starting transfers between devices  41.6 us (49%)
  Pallas kernels  21.5 us (26%)
  waiting for transfers between devices  19.9 us (24%)
  between operations  0.86 us (1%)
    ppermute x14, starting transfers between devices, over_z(): return lax.ppermute(x, 'shard', xor_pairs(k))  36 us
    ppermute x14, waiting for transfers between devices, over_z(): return lax.ppermute(x, 'shard', xor_pairs(k))  16.4 us
    ppermute x4, starting transfers between devices, over_y(): return lax.ppermute(x, 'tensor', xor_pairs(2))  4.97 us
    pallas_call x2, Pallas kernels, update_weights(): pl.pallas_call(functools.partial(update_kernel, factor, blocks), out_shap...  4.34 us
    pallas_call x1, Pallas kernels, newton_schulz_power(): pl.pallas_call(newton_schulz_kernel, out_shape=[jax.ShapeDtypeStruct((lay...  4.23 us
    ppermute x4, waiting for transfers between devices, over_y(): return lax.ppermute(x, 'tensor', xor_pairs(2))  3.43 us
    pallas_call x2, Pallas kernels, power_product(): pl.pallas_call(functools.partial(power_kernel, turn, scale), out_shape=[p...  3.01 us
    pallas_call x17, Pallas kernels, local_call(): pl.pallas_call(kernel, out_shape=[pltpu.VMEM(shape, dtype) for shape, dty...  2.88 us
  transfers between devices with their start and end apart: 21, of which 14 were waited for; matrix products, arithmetic and copies ran while one was open for 0% of the time, Pallas kernels for 21%

profile of v5, /device:TPU:0, one launch (start us, length us, event | category | flops | bytes accessed | tf_op | source)
XLA Modules:
  0.0 83.9 jit_solution(2069563992238663331)
XLA Ops:
  0.6 2.3 %give.1 = bf16[416,256]{1,0:T(8,128)(2,1)S(1)} custom-call(bf16[1,2,768,768]{3,2,1,0:T(8,128)(2,1)} %grads_hbm.2, f32[2,768,256]{2,1,0:T(8,128)} %basis_hbm.2), custom_call_target="tpu_custom_call" | custom-call | tf_op jit(solution)/shard_map/give/pallas_call | solution.py:243
  2.9 3.1 %collective-permute-start = (bf16[416,256]{1,0:T(8,128)(2,1)S(1)}, bf16[416,256]{1,0:T(8,128)(2,1)S(1)}, u32[]{:S(2)}, u32[]{:S(2)}) collective-permute-start(bf16[416,256]{1,0:T(8,128)(2,1)S(1)} %give.1), channel_id=1, source_target_pairs={{0,8},{8,0},{16,24},{24,16},{1,9},{9,1},{17,25},{25,17},{2,10},{10... | collective-permute-start | bytes 638984 | tf_op jit(solution)/shard_map/ppermute | solution.py:496
  6.0 2.1 %prepare.1 = (bf16[1,2,768,768]{3,2,1,0:T(8,128)(2,1)S(1)}, bf16[2,768,256]{2,1,0:T(8,128)(2,1)S(1)}, bf16[2,768,256]{2,1,0:T(8,128)(2,1)S(1)}) custom-call(bf16[1,2,768,768]{3,2,1,0:T(8,128)(2,1)} %grads_hbm.2, f32[2,768,256]{2,1,0:T(8,128)} %basis_hbm.2), custom_call_target="tpu_custom_call" | custom-call | tf_op jit(solution)/shard_map/prepare/pallas_call | solution.py:164
  8.2 0.5 project.2.own_ref
  8.6 0.8 project.3
  9.5 1.7 %fetch.1 = (bf16[2,768,768]{2,1,0:T(8,128)(2,1)S(1)}, bf16[2,256,768]{2,1,0:T(8,128)(2,1)S(1)}, bf16[2,256,768]{2,1,0:T(8,128)(2,1)S(1)}) custom-call(bf16[2,768,768]{2,1,0:T(8,128)(2,1)} %weights_hbm, bf16[2,768,256]{2,1,0:T(8,128)(2,1)S(1)} %get-tuple-element.106.high_ref, bf16[2,768,256]{2,1,0:T(8,128)(2,1)S(1)} %get-tuple-element.107.low_ref), custom_call_target="tpu_custom_call" | custom-call | tf_op jit(solution)/shard_map/fetch/pallas_call | solution.py:190
  11.3 0.3 add_coded.4
  11.6 1.8 %collective-permute-start.1 = (bf16[416,256]{1,0:T(8,128)(2,1)S(1)}, bf16[416,256]{1,0:T(8,128)(2,1)S(1)}, u32[]{:S(2)}, u32[]{:S(2)}) collective-permute-start(bf16[416,256]{1,0:T(8,128)(2,1)S(1)} %get-tuple-element.112), channel_id=1, source_target_pairs={{0,8},{8,0},{16,24},{24,16},{1,9},{9,1},{17,25},{25,17},{2,10},{10... | collective-permute-start | bytes 638984 | tf_op jit(solution)/shard_map/ppermute | solution.py:496
  13.4 2.5 %collective-permute-start.3 = (bf16[416,256]{1,0:T(8,128)(2,1)S(1)}, bf16[416,256]{1,0:T(8,128)(2,1)S(1)}, u32[]{:S(2)}, u32[]{:S(2)}) collective-permute-start(bf16[416,256]{1,0:T(8,128)(2,1)S(1)} %get-tuple-element.117), channel_id=1, source_target_pairs={{0,24},{8,16},{16,8},{24,0},{1,25},{9,17},{17,9},{25,1},{2,26},{10... | collective-permute-start | bytes 638984 | tf_op jit(solution)/shard_map/ppermute | solution.py:496
  15.9 3.1 %collective-permute-done.1.received_ref = bf16[416,256]{1,0:T(8,128)(2,1)S(1)} collective-permute-done((bf16[416,256]{1,0:T(8,128)(2,1)S(1)}, bf16[416,256]{1,0:T(8,128)(2,1)S(1)}, u32[]{:S(2)}, u32[]{:S(2)}) %collective-permute-start.1) | collective-permute-done | bytes 213024 | tf_op jit(solution)/shard_map/ppermute | solution.py:496
  19.0 0.3 add_coded.5
  19.4 9.5 %collective-permute-start.2 = (bf16[416,256]{1,0:T(8,128)(2,1)S(1)}, bf16[416,256]{1,0:T(8,128)(2,1)S(1)}, u32[]{:S(2)}, u32[]{:S(2)}) collective-permute-start(bf16[416,256]{1,0:T(8,128)(2,1)S(1)} %get-tuple-element.116), channel_id=1, source_target_pairs={{0,24},{8,16},{16,8},{24,0},{1,25},{9,17},{17,9},{25,1},{2,26},{10... | collective-permute-start | bytes 638984 | tf_op jit(solution)/shard_map/ppermute | solution.py:496
  28.8 0.3 add_coded.6
  29.3 3.5 %collective-permute-done.2.received_ref = bf16[416,256]{1,0:T(8,128)(2,1)S(1)} collective-permute-done((bf16[416,256]{1,0:T(8,128)(2,1)S(1)}, bf16[416,256]{1,0:T(8,128)(2,1)S(1)}, u32[]{:S(2)}, u32[]{:S(2)}) %collective-permute-start.2) | collective-permute-done | bytes 213024 | tf_op jit(solution)/shard_map/ppermute | solution.py:496
  32.8 0.3 add_coded.7
  33.1 1.7 %collective-permute-start.4 = (bf16[416,256]{1,0:T(8,128)(2,1)S(1)}, bf16[416,256]{1,0:T(8,128)(2,1)S(1)}, u32[]{:S(2)}, u32[]{:S(2)}) collective-permute-start(bf16[416,256]{1,0:T(8,128)(2,1)S(1)} %get-tuple-element.124), channel_id=1, source_target_pairs={{0,8},{8,0},{16,24},{24,16},{1,9},{9,1},{17,25},{25,17},{2,10},{10... | collective-permute-start | bytes 638984 | tf_op jit(solution)/shard_map/ppermute | solution.py:496
  34.8 0.3 collective-permute-done.5.given_ref
  35.1 1.5 %power.2 = (f32[128,768]{1,0:T(8,128)S(1)}, f32[128,768]{1,0:T(8,128)S(1)}, f32[2,192,256]{2,1,0:T(8,128)}, f32[2,192,256]{2,1,0:T(8,128)}, bf16[208,256]{1,0:T(8,128)(2,1)S(1)}) custom-call(bf16[1,2,768,768]{3,2,1,0:T(8,128)(2,1)S(1)} %get-tuple-element.102.grads_ref, f32[2,192,256]{2,1,0:T(8,128)S(1)} %copy-done, f32[2,192,256]{2,1,0:T(8,128)S(1)} %copy-done.1, ...), custom_call_target="tpu_custom_call" | custom-call | tf_op jit(solution)/shard_map/power/pallas_call | solution.py:324
  36.6 0.1 collective-permute-start.6
  36.7 0.5 collective-permute-start.7
  37.2 2.7 %collective-permute-done.4.given_ref = bf16[416,256]{1,0:T(8,128)(2,1)S(1)} collective-permute-done((bf16[416,256]{1,0:T(8,128)(2,1)S(1)}, bf16[416,256]{1,0:T(8,128)(2,1)S(1)}, u32[]{:S(2)}, u32[]{:S(2)}) %collective-permute-start.4) | collective-permute-done | bytes 213024 | tf_op jit(solution)/shard_map/ppermute | solution.py:496
  39.9 1.5 %power.3 = (f32[128,768]{1,0:T(8,128)S(1)}, f32[128,768]{1,0:T(8,128)S(1)}, f32[2,192,256]{2,1,0:T(8,128)}, f32[2,192,256]{2,1,0:T(8,128)}, bf16[2,208,256]{2,1,0:T(8,128)(2,1)S(1)}) custom-call(bf16[1,2,768,768]{3,2,1,0:T(8,128)(2,1)S(1)} %get-tuple-element.102.grads_ref, f32[2,192,256]{2,1,0:T(8,128)S(1)} %copy-done, ...), custom_call_target="tpu_custom_call", output_to_operand_aliasing={{2}: (5, {}), {3}: (6, {})} | custom-call | flops 5000000000 | tf_op jit(solution)/shard_map/power/pallas_call | solution.py:324
  41.4 1.6 %collective-permute-start.9 = (f32[64,768]{1,0:T(8,128)S(1)}, f32[64,768]{1,0:T(8,128)S(1)}, u32[]{:S(2)}, u32[]{:S(2)}) collective-permute-start(f32[64,768]{1,0:T(8,128)S(1)} %get-tuple-element.145), channel_id=1, source_target_pairs={{0,4},{2,6},{4,0},{6,2},{1,5},{3,7},{5,1},{7,3},{8,12},{10,14},{12... | collective-permute-start | bytes 589832 | tf_op jit(solution)/shard_map/ppermute | solution.py:504
  43.1 3.0 %collective-permute-start.8 = (bf16[2,208,256]{2,1,0:T(8,128)(2,1)S(1)}, bf16[2,208,256]{2,1,0:T(8,128)(2,1)S(1)}, u32[]{:S(2)}, u32[]{:S(2)}) collective-permute-start(bf16[2,208,256]{2,1,0:T(8,128)(2,1)S(1)} %get-tuple-element.170.a_ref), channel_id=1, source_target_pairs={{0,24},{8,16},{16,8},{24,0},{1,25},{9,17},{17,9},{25,1},{2,26},{10... | collective-permute-start | bytes 638984 | tf_op jit(solution)/shard_map/ppermute | solution.py:496
  46.1 0.5 collective-permute-start.11
  46.6 0.6 collective-permute-done.9.received_ref
  47.2 3.8 %collective-permute-start.10 = (f32[32,768]{1,0:T(8,128)S(1)}, f32[32,768]{1,0:T(8,128)S(1)}, u32[]{:S(2)}, u32[]{:S(2)}) collective-permute-start(f32[32,768]{1,0:T(8,128)S(1)} %get-tuple-element.149), channel_id=1, source_target_pairs={{0,8},{8,0},{16,24},{24,16},{1,9},{9,1},{17,25},{25,17},{2,10},{10... | collective-permute-start | bytes 294920 | tf_op jit(solution)/shard_map/ppermute | solution.py:496
  51.0 0.7 collective-permute-done.11.received_ref
  51.8 1.3 %collective-permute-start.13 = (f32[32,768]{1,0:T(8,128)S(1)}, f32[32,768]{1,0:T(8,128)S(1)}, u32[]{:S(2)}, u32[]{:S(2)}) collective-permute-start(f32[32,768]{1,0:T(8,128)S(1)} %get-tuple-element.159), channel_id=1, source_target_pairs={{0,8},{8,0},{16,24},{24,16},{1,9},{9,1},{17,25},{25,17},{2,10},{10... | collective-permute-start | bytes 294920 | tf_op jit(solution)/shard_map/ppermute | solution.py:496
  53.1 1.1 %collective-permute-done.10.received_ref = f32[32,768]{1,0:T(8,128)S(1)} collective-permute-done((f32[32,768]{1,0:T(8,128)S(1)}, f32[32,768]{1,0:T(8,128)S(1)}, u32[]{:S(2)}, u32[]{:S(2)}) %collective-permute-start.10) | collective-permute-done | bytes 98336 | tf_op jit(solution)/shard_map/ppermute | solution.py:496
  54.3 3.4 %collective-permute-start.12 = (f32[32,768]{1,0:T(8,128)S(1)}, f32[32,768]{1,0:T(8,128)S(1)}, u32[]{:S(2)}, u32[]{:S(2)}) collective-permute-start(f32[32,768]{1,0:T(8,128)S(1)} %add.4.own_ref), channel_id=1, source_target_pairs={{0,24},{8,16},{16,8},{24,0},{1,25},{9,17},{17,9},{25,1},{2,26},{10... | collective-permute-start | bytes 294920 | tf_op jit(solution)/shard_map/ppermute | solution.py:496
  57.6 2.1 %collective-permute-start.15 = (f32[32,768]{1,0:T(8,128)S(1)}, f32[32,768]{1,0:T(8,128)S(1)}, u32[]{:S(2)}, u32[]{:S(2)}) collective-permute-start(f32[32,768]{1,0:T(8,128)S(1)} %add.5.own_ref), channel_id=1, source_target_pairs={{0,24},{8,16},{16,8},{24,0},{1,25},{9,17},{17,9},{25,1},{2,26},{10... | collective-permute-start | bytes 294920 | tf_op jit(solution)/shard_map/ppermute | solution.py:496
  59.7 1.4 %collective-permute-done.12.received_ref = f32[32,768]{1,0:T(8,128)S(1)} collective-permute-done((f32[32,768]{1,0:T(8,128)S(1)}, f32[32,768]{1,0:T(8,128)S(1)}, u32[]{:S(2)}, u32[]{:S(2)}) %collective-permute-start.12) | collective-permute-done | bytes 98336 | tf_op jit(solution)/shard_map/ppermute | solution.py:496
  61.1 1.9 %collective-permute-start.14 = (f32[32,768]{1,0:T(8,128)S(1)}, f32[32,768]{1,0:T(8,128)S(1)}, u32[]{:S(2)}, u32[]{:S(2)}) collective-permute-start(f32[32,768]{1,0:T(8,128)S(1)} %add.6.own_ref), channel_id=1, source_target_pairs={{0,8},{8,0},{16,24},{24,16},{1,9},{9,1},{17,25},{25,17},{2,10},{10... | collective-permute-start | bytes 294920 | tf_op jit(solution)/shard_map/ppermute | solution.py:496
  63.0 1.3 %collective-permute-done.15.received_ref = f32[32,768]{1,0:T(8,128)S(1)} collective-permute-done((f32[32,768]{1,0:T(8,128)S(1)}, f32[32,768]{1,0:T(8,128)S(1)}, u32[]{:S(2)}, u32[]{:S(2)}) %collective-permute-start.15) | collective-permute-done | bytes 98336 | tf_op jit(solution)/shard_map/ppermute | solution.py:496
  64.3 0.8 collective-permute-start.17
  65.1 1.2 %collective-permute-done.14.received_ref = f32[32,768]{1,0:T(8,128)S(1)} collective-permute-done((f32[32,768]{1,0:T(8,128)S(1)}, f32[32,768]{1,0:T(8,128)S(1)}, u32[]{:S(2)}, u32[]{:S(2)}) %collective-permute-start.14) | collective-permute-done | bytes 98336 | tf_op jit(solution)/shard_map/ppermute | solution.py:496
  66.3 1.5 %collective-permute-start.16 = (f32[64,768]{1,0:T(8,128)S(1)}, f32[64,768]{1,0:T(8,128)S(1)}, u32[]{:S(2)}, u32[]{:S(2)}) collective-permute-start(f32[64,768]{1,0:T(8,128)S(1)} %join.2.refs_0_), channel_id=1, source_target_pairs={{0,4},{2,6},{4,0},{6,2},{1,5},{3,7},{5,1},{7,3},{8,12},{10,14},{12... | collective-permute-start | bytes 589832 | tf_op jit(solution)/shard_map/ppermute | solution.py:504
  67.9 1.7 %collective-permute-done.17.received_ref = f32[32,768]{1,0:T(8,128)S(1)} collective-permute-done((f32[32,768]{1,0:T(8,128)S(1)}, f32[32,768]{1,0:T(8,128)S(1)}, u32[]{:S(2)}, u32[]{:S(2)}) %collective-permute-start.17) | collective-permute-done | bytes 98336 | tf_op jit(solution)/shard_map/ppermute | solution.py:496
  69.6 1.2 %collective-permute-start.18 = (bf16[2,2,208,256]{3,2,1,0:T(8,128)(2,1)S(1)}, bf16[2,2,208,256]{3,2,1,0:T(8,128)(2,1)S(1)}, u32[]{:S(2)}, u32[]{:S(2)}) collective-permute-start(bf16[2,2,208,256]{3,2,1,0:T(8,128)(2,1)S(1)} %stack.1), channel_id=1, source_target_pairs={{0,8},{8,0},{16,24},{24,16},{1,9},{9,1},{17,25},{25,17},{2,10},{10... | collective-permute-start | bytes 1277960 | tf_op jit(solution)/shard_map/ppermute | solution.py:496
  70.8 1.4 %collective-permute-start.19 = (f32[64,768]{1,0:T(8,128)S(1)}, f32[64,768]{1,0:T(8,128)S(1)}, u32[]{:S(2)}, u32[]{:S(2)}) collective-permute-start(f32[64,768]{1,0:T(8,128)S(1)} %join.3.refs_2_), channel_id=1, source_target_pairs={{0,4},{2,6},{4,0},{6,2},{1,5},{3,7},{5,1},{7,3},{8,12},{10,14},{12... | collective-permute-start | bytes 589832 | tf_op jit(solution)/shard_map/ppermute | solution.py:504
  72.1 0.7 collective-permute-done.16.refs_1_
  72.8 2.2 %update_weights.2.refs_2_ = bf16[2,768,768]{2,1,0:T(8,128)(2,1)} custom-call(bf16[2,768,768]{2,1,0:T(8,128)(2,1)S(1)} %get-tuple-element.172.weights_ref, bf16[2,256,768]{2,1,0:T(8,128)(2,1)S(1)} %get-tuple-element.173.high_ref, bf16[2,256,768]{2,1,0:T(8,128)(2,1)S(1)} %get-tuple-element.174.low_ref, bf16[1,2,208,256]{3,2,1,0:T(8,128)(2,1)S(1)} %bitcast.2, ...), custom_call_target="tpu_custom_call" | custom-call | flops 3000000000 | tf_op jit(solution)/shard_map/update_weights/pallas_call | solution.py:478
  75.0 1.4 %collective-permute-done.19.refs_3_ = f32[64,768]{1,0:T(8,128)S(1)} collective-permute-done((f32[64,768]{1,0:T(8,128)S(1)}, f32[64,768]{1,0:T(8,128)S(1)}, u32[]{:S(2)}, u32[]{:S(2)}) %collective-permute-start.19) | collective-permute-done | bytes 196640 | tf_op jit(solution)/shard_map/ppermute | solution.py:504
  76.4 4.2 %newton_schulz.1 = (f32[2,768,256]{2,1,0:T(8,128)}, f32[768,256]{1,0:T(8,128)S(1)}) custom-call(f32[64,768]{1,0:T(8,128)S(1)} %join.2.refs_0_, f32[64,768]{1,0:T(8,128)S(1)} %collective-permute-done.16.refs_1_, f32[64,768]{1,0:T(8,128)S(1)} %join.3.refs_2_, f32[64,768]{1,0:T(8,128)S(1)} %collective-permute-done.19.refs_3_), custom_call_target="tpu_custom_call" | custom-call | tf_op jit(solution)/shard_map/newton_schulz/pallas_call | solution.py:409
  80.8 2.2 %update_weights.3 = bf16[2,768,768]{2,1,0:T(8,128)(2,1)} custom-call(bf16[2,768,768]{2,1,0:T(8,128)(2,1)S(1)} %get-tuple-element.172.weights_ref, bf16[2,256,768]{2,1,0:T(8,128)(2,1)S(1)} %get-tuple-element.173.high_ref, bf16[2,256,768]{2,1,0:T(8,128)(2,1)S(1)} %get-tuple-element.174.low_ref, ...), custom_call_target="tpu_custom_call", output_to_operand_aliasing={{}: (5, {})} | custom-call | flops 8000000000 | tf_op jit(solution)/shard_map/update_weights/pallas_call | solution.py:478
  83.0 0.1 collective-permute-done.20.layer_ref
  83.0 0.9 %put_layer.1 = f32[2,768,256]{2,1,0:T(8,128)} custom-call(f32[768,256]{1,0:T(8,128)S(1)} %collective-permute-done.20.layer_ref, f32[2,768,256]{2,1,0:T(8,128)} %get-tuple-element.187.whole_ref), custom_call_target="tpu_custom_call", output_to_operand_aliasing={{}: (1, {})} | custom-call | tf_op jit(solution)/shard_map/put_layer/pallas_call | solution.py:435
  (24 shorter events, 0.5 us)
Async XLA Ops:
  2.9 8.3 %collective-permute-start = (bf16[416,256]{1,0:T(8,128)(2,1)S(1)}, bf16[416,256]{1,0:T(8,128)(2,1)S(1)}, u32[]{:S(2)}, u32[]{:S(2)}) collective-permute-start(bf16[416,256]{1,0:T(8,128)(2,1)S(1)} %give.1), channel_id=1, source_target_pairs={{0,8},{8,0},{16,24},{24,16},{1,9},{9,1},{17,25},{25,17},{2,10},{10... | collective-permute-start | bytes 638984 | tf_op jit(solution)/shard_map/ppermute | solution.py:496
  9.5 25.6 %copy-start = (f32[2,192,256]{2,1,0:T(8,128)S(1)}, f32[2,192,256]{2,1,0:T(8,128)}, u32[]{:S(2)}) copy-start(f32[2,192,256]{2,1,0:T(8,128)} %first_ref.3) | copy-start | bytes 1179652
  9.5 25.6 %copy-start.1 = (f32[2,192,256]{2,1,0:T(8,128)S(1)}, f32[2,192,256]{2,1,0:T(8,128)}, u32[]{:S(2)}) copy-start(f32[2,192,256]{2,1,0:T(8,128)} %second_ref.3) | copy-start | bytes 1179652
  11.6 7.4 %collective-permute-start.1 = (bf16[416,256]{1,0:T(8,128)(2,1)S(1)}, bf16[416,256]{1,0:T(8,128)(2,1)S(1)}, u32[]{:S(2)}, u32[]{:S(2)}) collective-permute-start(bf16[416,256]{1,0:T(8,128)(2,1)S(1)} %get-tuple-element.112), channel_id=1, source_target_pairs={{0,8},{8,0},{16,24},{24,16},{1,9},{9,1},{17,25},{25,17},{2,10},{10... | collective-permute-start | bytes 638984 | tf_op jit(solution)/shard_map/ppermute | solution.py:496
  13.4 15.4 %collective-permute-start.3 = (bf16[416,256]{1,0:T(8,128)(2,1)S(1)}, bf16[416,256]{1,0:T(8,128)(2,1)S(1)}, u32[]{:S(2)}, u32[]{:S(2)}) collective-permute-start(bf16[416,256]{1,0:T(8,128)(2,1)S(1)} %get-tuple-element.117), channel_id=1, source_target_pairs={{0,24},{8,16},{16,8},{24,0},{1,25},{9,17},{17,9},{25,1},{2,26},{10... | collective-permute-start | bytes 638984 | tf_op jit(solution)/shard_map/ppermute | solution.py:496
  19.4 13.4 %collective-permute-start.2 = (bf16[416,256]{1,0:T(8,128)(2,1)S(1)}, bf16[416,256]{1,0:T(8,128)(2,1)S(1)}, u32[]{:S(2)}, u32[]{:S(2)}) collective-permute-start(bf16[416,256]{1,0:T(8,128)(2,1)S(1)} %get-tuple-element.116), channel_id=1, source_target_pairs={{0,24},{8,16},{16,8},{24,0},{1,25},{9,17},{17,9},{25,1},{2,26},{10... | collective-permute-start | bytes 638984 | tf_op jit(solution)/shard_map/ppermute | solution.py:496
  29.2 5.9 %collective-permute-start.5 = (bf16[416,256]{1,0:T(8,128)(2,1)S(1)}, bf16[416,256]{1,0:T(8,128)(2,1)S(1)}, u32[]{:S(2)}, u32[]{:S(2)}) collective-permute-start(bf16[416,256]{1,0:T(8,128)(2,1)S(1)} %get-tuple-element.125), channel_id=1, source_target_pairs={{0,8},{8,0},{16,24},{24,16},{1,9},{9,1},{17,25},{25,17},{2,10},{10... | collective-permute-start | bytes 638984 | tf_op jit(solution)/shard_map/ppermute | solution.py:496
  33.1 6.8 %collective-permute-start.4 = (bf16[416,256]{1,0:T(8,128)(2,1)S(1)}, bf16[416,256]{1,0:T(8,128)(2,1)S(1)}, u32[]{:S(2)}, u32[]{:S(2)}) collective-permute-start(bf16[416,256]{1,0:T(8,128)(2,1)S(1)} %get-tuple-element.124), channel_id=1, source_target_pairs={{0,8},{8,0},{16,24},{24,16},{1,9},{9,1},{17,25},{25,17},{2,10},{10... | collective-permute-start | bytes 638984 | tf_op jit(solution)/shard_map/ppermute | solution.py:496
  36.6 4.8 %collective-permute-start.6 = (f32[128,768]{1,0:T(8,128)S(1)}, f32[128,768]{1,0:T(8,128)S(1)}, u32[]{:S(2)}, u32[]{:S(2)}) collective-permute-start(f32[128,768]{1,0:T(8,128)S(1)} %get-tuple-element.136), channel_id=1, source_target_pairs={{0,2},{2,0},{4,6},{6,4},{1,3},{3,1},{5,7},{7,5},{8,10},{10,8},{12,... | collective-permute-start | bytes 1179656 | tf_op jit(solution)/shard_map/ppermute | solution.py:500
  36.7 4.7 %collective-permute-start.7 = (f32[128,768]{1,0:T(8,128)S(1)}, f32[128,768]{1,0:T(8,128)S(1)}, u32[]{:S(2)}, u32[]{:S(2)}) collective-permute-start(f32[128,768]{1,0:T(8,128)S(1)} %get-tuple-element.128), channel_id=1, source_target_pairs={{0,2},{2,0},{4,6},{6,4},{1,3},{3,1},{5,7},{7,5},{8,10},{10,8},{12,... | collective-permute-start | bytes 1179656 | tf_op jit(solution)/shard_map/ppermute | solution.py:500
  41.4 5.7 %collective-permute-start.9 = (f32[64,768]{1,0:T(8,128)S(1)}, f32[64,768]{1,0:T(8,128)S(1)}, u32[]{:S(2)}, u32[]{:S(2)}) collective-permute-start(f32[64,768]{1,0:T(8,128)S(1)} %get-tuple-element.145), channel_id=1, source_target_pairs={{0,4},{2,6},{4,0},{6,2},{1,5},{3,7},{5,1},{7,3},{8,12},{10,14},{12... | collective-permute-start | bytes 589832 | tf_op jit(solution)/shard_map/ppermute | solution.py:504
  43.1 10.1 %collective-permute-start.8 = (bf16[2,208,256]{2,1,0:T(8,128)(2,1)S(1)}, bf16[2,208,256]{2,1,0:T(8,128)(2,1)S(1)}, u32[]{:S(2)}, u32[]{:S(2)}) collective-permute-start(bf16[2,208,256]{2,1,0:T(8,128)(2,1)S(1)} %get-tuple-element.170.a_ref), channel_id=1, source_target_pairs={{0,24},{8,16},{16,8},{24,0},{1,25},{9,17},{17,9},{25,1},{2,26},{10... | collective-permute-start | bytes 638984 | tf_op jit(solution)/shard_map/ppermute | solution.py:496
  46.1 5.7 %collective-permute-start.11 = (f32[64,768]{1,0:T(8,128)S(1)}, f32[64,768]{1,0:T(8,128)S(1)}, u32[]{:S(2)}, u32[]{:S(2)}) collective-permute-start(f32[64,768]{1,0:T(8,128)S(1)} %get-tuple-element.150), channel_id=1, source_target_pairs={{0,4},{2,6},{4,0},{6,2},{1,5},{3,7},{5,1},{7,3},{8,12},{10,14},{12... | collective-permute-start | bytes 589832 | tf_op jit(solution)/shard_map/ppermute | solution.py:504
  47.2 7.0 %collective-permute-start.10 = (f32[32,768]{1,0:T(8,128)S(1)}, f32[32,768]{1,0:T(8,128)S(1)}, u32[]{:S(2)}, u32[]{:S(2)}) collective-permute-start(f32[32,768]{1,0:T(8,128)S(1)} %get-tuple-element.149), channel_id=1, source_target_pairs={{0,8},{8,0},{16,24},{24,16},{1,9},{9,1},{17,25},{25,17},{2,10},{10... | collective-permute-start | bytes 294920 | tf_op jit(solution)/shard_map/ppermute | solution.py:496
  51.8 5.8 %collective-permute-start.13 = (f32[32,768]{1,0:T(8,128)S(1)}, f32[32,768]{1,0:T(8,128)S(1)}, u32[]{:S(2)}, u32[]{:S(2)}) collective-permute-start(f32[32,768]{1,0:T(8,128)S(1)} %get-tuple-element.159), channel_id=1, source_target_pairs={{0,8},{8,0},{16,24},{24,16},{1,9},{9,1},{17,25},{25,17},{2,10},{10... | collective-permute-start | bytes 294920 | tf_op jit(solution)/shard_map/ppermute | solution.py:496
  54.3 6.9 %collective-permute-start.12 = (f32[32,768]{1,0:T(8,128)S(1)}, f32[32,768]{1,0:T(8,128)S(1)}, u32[]{:S(2)}, u32[]{:S(2)}) collective-permute-start(f32[32,768]{1,0:T(8,128)S(1)} %add.4.own_ref), channel_id=1, source_target_pairs={{0,24},{8,16},{16,8},{24,0},{1,25},{9,17},{17,9},{25,1},{2,26},{10... | collective-permute-start | bytes 294920 | tf_op jit(solution)/shard_map/ppermute | solution.py:496
  57.6 6.7 %collective-permute-start.15 = (f32[32,768]{1,0:T(8,128)S(1)}, f32[32,768]{1,0:T(8,128)S(1)}, u32[]{:S(2)}, u32[]{:S(2)}) collective-permute-start(f32[32,768]{1,0:T(8,128)S(1)} %add.5.own_ref), channel_id=1, source_target_pairs={{0,24},{8,16},{16,8},{24,0},{1,25},{9,17},{17,9},{25,1},{2,26},{10... | collective-permute-start | bytes 294920 | tf_op jit(solution)/shard_map/ppermute | solution.py:496
  61.1 5.2 %collective-permute-start.14 = (f32[32,768]{1,0:T(8,128)S(1)}, f32[32,768]{1,0:T(8,128)S(1)}, u32[]{:S(2)}, u32[]{:S(2)}) collective-permute-start(f32[32,768]{1,0:T(8,128)S(1)} %add.6.own_ref), channel_id=1, source_target_pairs={{0,8},{8,0},{16,24},{24,16},{1,9},{9,1},{17,25},{25,17},{2,10},{10... | collective-permute-start | bytes 294920 | tf_op jit(solution)/shard_map/ppermute | solution.py:496
  64.3 5.2 %collective-permute-start.17 = (f32[32,768]{1,0:T(8,128)S(1)}, f32[32,768]{1,0:T(8,128)S(1)}, u32[]{:S(2)}, u32[]{:S(2)}) collective-permute-start(f32[32,768]{1,0:T(8,128)S(1)} %add.7.own_ref), channel_id=1, source_target_pairs={{0,8},{8,0},{16,24},{24,16},{1,9},{9,1},{17,25},{25,17},{2,10},{10... | collective-permute-start | bytes 294920 | tf_op jit(solution)/shard_map/ppermute | solution.py:496
  66.3 6.5 %collective-permute-start.16 = (f32[64,768]{1,0:T(8,128)S(1)}, f32[64,768]{1,0:T(8,128)S(1)}, u32[]{:S(2)}, u32[]{:S(2)}) collective-permute-start(f32[64,768]{1,0:T(8,128)S(1)} %join.2.refs_0_), channel_id=1, source_target_pairs={{0,4},{2,6},{4,0},{6,2},{1,5},{3,7},{5,1},{7,3},{8,12},{10,14},{12... | collective-permute-start | bytes 589832 | tf_op jit(solution)/shard_map/ppermute | solution.py:504
  69.6 11.2 %collective-permute-start.18 = (bf16[2,2,208,256]{3,2,1,0:T(8,128)(2,1)S(1)}, bf16[2,2,208,256]{3,2,1,0:T(8,128)(2,1)S(1)}, u32[]{:S(2)}, u32[]{:S(2)}) collective-permute-start(bf16[2,2,208,256]{3,2,1,0:T(8,128)(2,1)S(1)} %stack.1), channel_id=1, source_target_pairs={{0,8},{8,0},{16,24},{24,16},{1,9},{9,1},{17,25},{25,17},{2,10},{10... | collective-permute-start | bytes 1277960 | tf_op jit(solution)/shard_map/ppermute | solution.py:496
  70.8 5.7 %collective-permute-start.19 = (f32[64,768]{1,0:T(8,128)S(1)}, f32[64,768]{1,0:T(8,128)S(1)}, u32[]{:S(2)}, u32[]{:S(2)}) collective-permute-start(f32[64,768]{1,0:T(8,128)S(1)} %join.3.refs_2_), channel_id=1, source_target_pairs={{0,4},{2,6},{4,0},{6,2},{1,5},{3,7},{5,1},{7,3},{8,12},{10,14},{12... | collective-permute-start | bytes 589832 | tf_op jit(solution)/shard_map/ppermute | solution.py:504
  80.7 2.4 %collective-permute-start.20 = (f32[768,256]{1,0:T(8,128)S(1)}, f32[768,256]{1,0:T(8,128)S(1)}, u32[]{:S(2)}, u32[]{:S(2)}) collective-permute-start(f32[768,256]{1,0:T(8,128)S(1)} %get-tuple-element.183), channel_id=1, source_target_pairs={{0,2},{2,0},{4,6},{6,4},{1,3},{3,1},{5,7},{7,5},{8,10},{10,8},{12,... | collective-permute-start | bytes 2359304 | tf_op jit(solution)/shard_map/ppermute | solution.py:500

commit v6 on v5

--- a/solution.py
+++ b/solution.py
@@ -370,7 +370,7 @@
 
 def newton_schulz_kernel(*refs):
     place = Place()
-    parts, (out_ref, result_ref, power_ref, sems) = refs[:-4], refs[-4:]
+    parts, (result_ref, power_ref) = refs[:-2], refs[-2:]
     piece = parts[0].shape[0] // 2
     for h in range(HALVES):
         for k in range(4):
@@ -393,28 +393,15 @@
     iterate = split(dot3(product, unscaled))
     g = split(gram)
     last = split((diagonal + coeff_b * gram + coeff_c * dot3(g, g)) * (scale * width**0.5))
-    copies = []
     for i in range(width // rank):
         columns = slice(i * rank, (i + 1) * rank)
         result_ref[columns] = dot3(last, [term[:, columns] for term in iterate]).T
-        copies.append(pltpu.make_async_copy(result_ref.at[columns], out_ref.at[place.core, columns], sems.at[i]))
-        copies[-1].start()
-    for copy in copies:
-        copy.wait()
-
-
-def newton_schulz_power(layers, *parts):
+
+
+def newton_schulz_power(*parts):
     rank, width = 2 * HALVES * parts[0].shape[0], parts[0].shape[1]
-    vmem = pl.BlockSpec(memory_space=pltpu.VMEM)
-    return pl.pallas_call(
-        newton_schulz_kernel,
-        out_shape=[jax.ShapeDtypeStruct((layers, width, rank), jnp.float32), pltpu.VMEM((width, rank), jnp.float32)],
-        in_specs=[vmem] * len(parts),
-        out_specs=[pl.BlockSpec(memory_space=pl.ANY), vmem],
-        scratch_shapes=[pltpu.VMEM((rank, width), jnp.float32), pltpu.SemaphoreType.DMA((width // rank,))],
-        compiler_params=params(12),
-        name="newton_schulz",
-    )(*in_vmem(*parts))
+    scratch = [pltpu.VMEM((rank, width), jnp.float32)]
+    return local_call(newton_schulz_kernel, [((width, rank), jnp.float32)], *parts, name="newton_schulz", scratch=scratch)[0]
 
 
 def put_layer_kernel(layer_ref, whole_ref, out_ref, sems):
@@ -454,10 +441,16 @@
 
 
 def update_kernel(factor, blocks, weights_ref, high_ref, low_ref, *refs):
-    directions, (out_ref, buffer, sems) = refs[:2], refs[-3:]
+    directions, (buffer, sems) = refs[:2], refs[-2:]
     place = Place()
     layers, rows = weights_ref.shape[0], buffer.shape[2]
     copies = []
+    if len(refs) == 5:
+        out_ref = refs[2]
+    else:
+        own_ref, _, out_ref, basis_ref = refs[2:6]
+        copies.append(pltpu.make_async_copy(own_ref, basis_ref.at[place.core], sems.at[layers, 0]))
+        copies[0].start()
     for layer in range(layers):
         basis = high_ref[layer], low_ref[layer]
         for i, (direction, (k, source)) in enumerate(zip(directions, blocks)):
@@ -471,21 +464,25 @@
         copy.wait()
 
 
-def update_weights(weights, basis, directions, blocks, factor, flops, before=()):
+def update_weights(weights, basis, directions, blocks, factor, flops, own=None, before=None):
     layers, height, width = weights.shape
     vmem, anywhere = pl.BlockSpec(memory_space=pltpu.VMEM), pl.BlockSpec(memory_space=pl.ANY)
-    operands = in_vmem(weights, *basis, *directions)
+    last = before is not None
+    operands = in_vmem(weights, *basis, *directions, *([own] if last else []))
+    outs = [jax.ShapeDtypeStruct(weights.shape, weights.dtype)]
+    if last:
+        outs.append(jax.ShapeDtypeStruct((layers,) + own.shape, own.dtype))
     return pl.pallas_call(
         functools.partial(update_kernel, factor, blocks),
-        out_shape=jax.ShapeDtypeStruct(weights.shape, weights.dtype),
-        in_specs=[vmem] * len(operands) + [anywhere] * len(before),
-        out_specs=anywhere,
-        scratch_shapes=[pltpu.VMEM((layers, 2, height // 4, width), weights.dtype), pltpu.SemaphoreType.DMA((layers, 2))],
-        input_output_aliases={5: 0} if before else {},
+        out_shape=outs,
+        in_specs=[vmem] * len(operands) + [anywhere] * last,
+        out_specs=[anywhere] * len(outs),
+        scratch_shapes=[pltpu.VMEM((layers, 2, height // 4, width), weights.dtype), pltpu.SemaphoreType.DMA((layers + 1, 2))],
+        input_output_aliases={6: 0} if last else {},
         compiler_params=params(12),
         cost_estimate=cost(flops),
         name="update_weights",
-    )(*operands, *before)
+    )(*operands, *([before] if last else []))
 
 
 def xor_pairs(k):
@@ -581,15 +578,15 @@
     pair = next_z(order.through(stack(*order.step(code, opposite))))
     factor = learn_rate * galore_scale * scale_factor
     code, opposite, weights, *parts[0] = order.step(code[None], opposite[None], weights, *parts[0])
-    weights_next = order.through(update_weights(weights, turned, (code, opposite), ((0, 0), (3, 0)), factor, 3e9))
+    (weights_next,) = update_weights(weights, turned, (code, opposite), ((0, 0), (3, 0)), factor, 3e9)
+    order.through(weights_next)
     parts = order.step(*[x for part in parts for x in part])
-    basis_next, own = newton_schulz_power(layers, *parts)
+    own = newton_schulz_power(*parts)
     order.through(own)
     other = over_core(own)
     (pair,) = order.step(pair)
-    weights_next = order.through(
-        update_weights(weights, turned, (pair, pair), ((1, 0), (2, 1)), factor, 8e9, (weights_next,))
-    )
+    weights_next, basis_next = update_weights(weights, turned, (pair, pair), ((1, 0), (2, 1)), factor, 8e9, own, weights_next)
+    order.through(weights_next)
     basis_next = put_layer(*order.step(other, basis_next))
     return (weights_next, basis_next, moment_one, moment_two)
 

time: 84.1 us -> 83.4 us (level)
    pallas_call x1 -> x0, Pallas kernels: 4.23 us -> none  [newton_schulz_power(): pl.pallas_call(newton_schulz_kernel, out_shape=[jax.ShapeDtypeStruct((lay...]
    pallas_call x17 -> x18, Pallas kernels: 2.88 us -> 6.38 us  [local_call(): pl.pallas_call(kernel, out_shape=[pltpu.VMEM(shape, dtype) for shape, dty...]
where the time goes in v6:
time: 83.4 us; the launch traced here: 83.2 us
  starting transfers between devices  41.6 us (50%)
  Pallas kernels  20.8 us (25%)
  waiting for transfers between devices  19.9 us (24%)
  between operations  0.86 us (1%)
    ppermute x14, starting transfers between devices, over_z(): return lax.ppermute(x, 'shard', xor_pairs(k))  36 us
    ppermute x14, waiting for transfers between devices, over_z(): return lax.ppermute(x, 'shard', xor_pairs(k))  16.4 us
    pallas_call x18, Pallas kernels, local_call(): pl.pallas_call(kernel, out_shape=[pltpu.VMEM(shape, dtype) for shape, dty...  6.38 us
    ppermute x4, starting transfers between devices, over_y(): return lax.ppermute(x, 'tensor', xor_pairs(2))  4.95 us
    pallas_call x2, Pallas kernels, update_weights(): pl.pallas_call(functools.partial(update_kernel, factor, blocks), out_shap...  4.38 us
    ppermute x4, waiting for transfers between devices, over_y(): return lax.ppermute(x, 'tensor', xor_pairs(2))  3.43 us
    pallas_call x2, Pallas kernels, power_product(): pl.pallas_call(functools.partial(power_kernel, turn, scale), out_shape=[p...  3.01 us
    pallas_call x1, Pallas kernels, give(): pl.pallas_call(give_kernel, out_shape=pltpu.VMEM((2 * (rows + 16), rank),...  2.28 us
  transfers between devices with their start and end apart: 21, of which 14 were waited for; matrix products, arithmetic and copies ran while one was open for 0% of the time, Pallas kernels for 21%

profile of v6, /device:TPU:0, one launch (start us, length us, event | category | flops | bytes accessed | tf_op | source)
XLA Modules:
  0.0 83.2 jit_solution(14983429079115144100)
XLA Ops:
  0.6 2.3 %give.1 = bf16[416,256]{1,0:T(8,128)(2,1)S(1)} custom-call(bf16[1,2,768,768]{3,2,1,0:T(8,128)(2,1)} %grads_hbm.2, f32[2,768,256]{2,1,0:T(8,128)} %basis_hbm.2), custom_call_target="tpu_custom_call" | custom-call | tf_op jit(solution)/shard_map/give/pallas_call | solution.py:243
  2.9 3.1 %collective-permute-start = (bf16[416,256]{1,0:T(8,128)(2,1)S(1)}, bf16[416,256]{1,0:T(8,128)(2,1)S(1)}, u32[]{:S(2)}, u32[]{:S(2)}) collective-permute-start(bf16[416,256]{1,0:T(8,128)(2,1)S(1)} %give.1), channel_id=1, source_target_pairs={{0,8},{8,0},{16,24},{24,16},{1,9},{9,1},{17,25},{25,17},{2,10},{10... | collective-permute-start | bytes 638984 | tf_op jit(solution)/shard_map/ppermute | solution.py:493
  6.0 2.1 %prepare.1 = (bf16[1,2,768,768]{3,2,1,0:T(8,128)(2,1)S(1)}, bf16[2,768,256]{2,1,0:T(8,128)(2,1)S(1)}, bf16[2,768,256]{2,1,0:T(8,128)(2,1)S(1)}) custom-call(bf16[1,2,768,768]{3,2,1,0:T(8,128)(2,1)} %grads_hbm.2, f32[2,768,256]{2,1,0:T(8,128)} %basis_hbm.2), custom_call_target="tpu_custom_call" | custom-call | tf_op jit(solution)/shard_map/prepare/pallas_call | solution.py:164
  8.2 0.5 project.2.own_ref
  8.6 0.8 project.3
  9.5 1.7 %fetch.1 = (bf16[2,768,768]{2,1,0:T(8,128)(2,1)S(1)}, bf16[2,256,768]{2,1,0:T(8,128)(2,1)S(1)}, bf16[2,256,768]{2,1,0:T(8,128)(2,1)S(1)}) custom-call(bf16[2,768,768]{2,1,0:T(8,128)(2,1)} %weights_hbm, bf16[2,768,256]{2,1,0:T(8,128)(2,1)S(1)} %get-tuple-element.106.high_ref, bf16[2,768,256]{2,1,0:T(8,128)(2,1)S(1)} %get-tuple-element.107.low_ref), custom_call_target="tpu_custom_call" | custom-call | tf_op jit(solution)/shard_map/fetch/pallas_call | solution.py:190
  11.3 0.3 add_coded.4
  11.6 1.8 %collective-permute-start.1 = (bf16[416,256]{1,0:T(8,128)(2,1)S(1)}, bf16[416,256]{1,0:T(8,128)(2,1)S(1)}, u32[]{:S(2)}, u32[]{:S(2)}) collective-permute-start(bf16[416,256]{1,0:T(8,128)(2,1)S(1)} %get-tuple-element.112), channel_id=1, source_target_pairs={{0,8},{8,0},{16,24},{24,16},{1,9},{9,1},{17,25},{25,17},{2,10},{10... | collective-permute-start | bytes 638984 | tf_op jit(solution)/shard_map/ppermute | solution.py:493
  13.4 2.5 %collective-permute-start.3 = (bf16[416,256]{1,0:T(8,128)(2,1)S(1)}, bf16[416,256]{1,0:T(8,128)(2,1)S(1)}, u32[]{:S(2)}, u32[]{:S(2)}) collective-permute-start(bf16[416,256]{1,0:T(8,128)(2,1)S(1)} %get-tuple-element.117), channel_id=1, source_target_pairs={{0,24},{8,16},{16,8},{24,0},{1,25},{9,17},{17,9},{25,1},{2,26},{10... | collective-permute-start | bytes 638984 | tf_op jit(solution)/shard_map/ppermute | solution.py:493
  15.9 3.1 %collective-permute-done.1.received_ref = bf16[416,256]{1,0:T(8,128)(2,1)S(1)} collective-permute-done((bf16[416,256]{1,0:T(8,128)(2,1)S(1)}, bf16[416,256]{1,0:T(8,128)(2,1)S(1)}, u32[]{:S(2)}, u32[]{:S(2)}) %collective-permute-start.1) | collective-permute-done | bytes 213024 | tf_op jit(solution)/shard_map/ppermute | solution.py:493
  19.0 0.3 add_coded.5
  19.4 9.5 %collective-permute-start.2 = (bf16[416,256]{1,0:T(8,128)(2,1)S(1)}, bf16[416,256]{1,0:T(8,128)(2,1)S(1)}, u32[]{:S(2)}, u32[]{:S(2)}) collective-permute-start(bf16[416,256]{1,0:T(8,128)(2,1)S(1)} %get-tuple-element.116), channel_id=1, source_target_pairs={{0,24},{8,16},{16,8},{24,0},{1,25},{9,17},{17,9},{25,1},{2,26},{10... | collective-permute-start | bytes 638984 | tf_op jit(solution)/shard_map/ppermute | solution.py:493
  28.8 0.3 add_coded.6
  29.2 0.1 collective-permute-start.5
  29.3 3.5 %collective-permute-done.2.received_ref = bf16[416,256]{1,0:T(8,128)(2,1)S(1)} collective-permute-done((bf16[416,256]{1,0:T(8,128)(2,1)S(1)}, bf16[416,256]{1,0:T(8,128)(2,1)S(1)}, u32[]{:S(2)}, u32[]{:S(2)}) %collective-permute-start.2) | collective-permute-done | bytes 213024 | tf_op jit(solution)/shard_map/ppermute | solution.py:493
  32.8 0.3 add_coded.7
  33.1 1.7 %collective-permute-start.4 = (bf16[416,256]{1,0:T(8,128)(2,1)S(1)}, bf16[416,256]{1,0:T(8,128)(2,1)S(1)}, u32[]{:S(2)}, u32[]{:S(2)}) collective-permute-start(bf16[416,256]{1,0:T(8,128)(2,1)S(1)} %get-tuple-element.124), channel_id=1, source_target_pairs={{0,8},{8,0},{16,24},{24,16},{1,9},{9,1},{17,25},{25,17},{2,10},{10... | collective-permute-start | bytes 638984 | tf_op jit(solution)/shard_map/ppermute | solution.py:493
  34.8 0.3 collective-permute-done.5.given_ref
  35.1 1.5 %power.2 = (f32[128,768]{1,0:T(8,128)S(1)}, f32[128,768]{1,0:T(8,128)S(1)}, f32[2,192,256]{2,1,0:T(8,128)}, f32[2,192,256]{2,1,0:T(8,128)}, bf16[208,256]{1,0:T(8,128)(2,1)S(1)}) custom-call(bf16[1,2,768,768]{3,2,1,0:T(8,128)(2,1)S(1)} %get-tuple-element.102.grads_ref, f32[2,192,256]{2,1,0:T(8,128)S(1)} %copy-done, f32[2,192,256]{2,1,0:T(8,128)S(1)} %copy-done.1, ...), custom_call_target="tpu_custom_call" | custom-call | tf_op jit(solution)/shard_map/power/pallas_call | solution.py:324
  36.7 0.5 collective-permute-start.7
  37.2 2.7 %collective-permute-done.4.given_ref = bf16[416,256]{1,0:T(8,128)(2,1)S(1)} collective-permute-done((bf16[416,256]{1,0:T(8,128)(2,1)S(1)}, bf16[416,256]{1,0:T(8,128)(2,1)S(1)}, u32[]{:S(2)}, u32[]{:S(2)}) %collective-permute-start.4) | collective-permute-done | bytes 213024 | tf_op jit(solution)/shard_map/ppermute | solution.py:493
  39.9 1.5 %power.3 = (f32[128,768]{1,0:T(8,128)S(1)}, f32[128,768]{1,0:T(8,128)S(1)}, f32[2,192,256]{2,1,0:T(8,128)}, f32[2,192,256]{2,1,0:T(8,128)}, bf16[2,208,256]{2,1,0:T(8,128)(2,1)S(1)}) custom-call(bf16[1,2,768,768]{3,2,1,0:T(8,128)(2,1)S(1)} %get-tuple-element.102.grads_ref, f32[2,192,256]{2,1,0:T(8,128)S(1)} %copy-done, ...), custom_call_target="tpu_custom_call", output_to_operand_aliasing={{2}: (5, {}), {3}: (6, {})} | custom-call | flops 5000000000 | tf_op jit(solution)/shard_map/power/pallas_call | solution.py:324
  41.4 1.6 %collective-permute-start.9 = (f32[64,768]{1,0:T(8,128)S(1)}, f32[64,768]{1,0:T(8,128)S(1)}, u32[]{:S(2)}, u32[]{:S(2)}) collective-permute-start(f32[64,768]{1,0:T(8,128)S(1)} %get-tuple-element.145), channel_id=1, source_target_pairs={{0,4},{2,6},{4,0},{6,2},{1,5},{3,7},{5,1},{7,3},{8,12},{10,14},{12... | collective-permute-start | bytes 589832 | tf_op jit(solution)/shard_map/ppermute | solution.py:501
  43.1 3.0 %collective-permute-start.8 = (bf16[2,208,256]{2,1,0:T(8,128)(2,1)S(1)}, bf16[2,208,256]{2,1,0:T(8,128)(2,1)S(1)}, u32[]{:S(2)}, u32[]{:S(2)}) collective-permute-start(bf16[2,208,256]{2,1,0:T(8,128)(2,1)S(1)} %get-tuple-element.170.a_ref), channel_id=1, source_target_pairs={{0,24},{8,16},{16,8},{24,0},{1,25},{9,17},{17,9},{25,1},{2,26},{10... | collective-permute-start | bytes 638984 | tf_op jit(solution)/shard_map/ppermute | solution.py:493
  46.1 0.5 collective-permute-start.11
  46.6 0.6 collective-permute-done.9.received_ref
  47.2 3.8 %collective-permute-start.10 = (f32[32,768]{1,0:T(8,128)S(1)}, f32[32,768]{1,0:T(8,128)S(1)}, u32[]{:S(2)}, u32[]{:S(2)}) collective-permute-start(f32[32,768]{1,0:T(8,128)S(1)} %get-tuple-element.149), channel_id=1, source_target_pairs={{0,8},{8,0},{16,24},{24,16},{1,9},{9,1},{17,25},{25,17},{2,10},{10... | collective-permute-start | bytes 294920 | tf_op jit(solution)/shard_map/ppermute | solution.py:493
  51.0 0.7 collective-permute-done.11.received_ref
  51.8 1.3 %collective-permute-start.13 = (f32[32,768]{1,0:T(8,128)S(1)}, f32[32,768]{1,0:T(8,128)S(1)}, u32[]{:S(2)}, u32[]{:S(2)}) collective-permute-start(f32[32,768]{1,0:T(8,128)S(1)} %get-tuple-element.159), channel_id=1, source_target_pairs={{0,8},{8,0},{16,24},{24,16},{1,9},{9,1},{17,25},{25,17},{2,10},{10... | collective-permute-start | bytes 294920 | tf_op jit(solution)/shard_map/ppermute | solution.py:493
  53.1 1.1 %collective-permute-done.10.received_ref = f32[32,768]{1,0:T(8,128)S(1)} collective-permute-done((f32[32,768]{1,0:T(8,128)S(1)}, f32[32,768]{1,0:T(8,128)S(1)}, u32[]{:S(2)}, u32[]{:S(2)}) %collective-permute-start.10) | collective-permute-done | bytes 98336 | tf_op jit(solution)/shard_map/ppermute | solution.py:493
  54.3 3.3 %collective-permute-start.12 = (f32[32,768]{1,0:T(8,128)S(1)}, f32[32,768]{1,0:T(8,128)S(1)}, u32[]{:S(2)}, u32[]{:S(2)}) collective-permute-start(f32[32,768]{1,0:T(8,128)S(1)} %add.4.own_ref), channel_id=1, source_target_pairs={{0,24},{8,16},{16,8},{24,0},{1,25},{9,17},{17,9},{25,1},{2,26},{10... | collective-permute-start | bytes 294920 | tf_op jit(solution)/shard_map/ppermute | solution.py:493
  57.6 2.1 %collective-permute-start.15 = (f32[32,768]{1,0:T(8,128)S(1)}, f32[32,768]{1,0:T(8,128)S(1)}, u32[]{:S(2)}, u32[]{:S(2)}) collective-permute-start(f32[32,768]{1,0:T(8,128)S(1)} %add.5.own_ref), channel_id=1, source_target_pairs={{0,24},{8,16},{16,8},{24,0},{1,25},{9,17},{17,9},{25,1},{2,26},{10... | collective-permute-start | bytes 294920 | tf_op jit(solution)/shard_map/ppermute | solution.py:493
  59.7 1.4 %collective-permute-done.12.received_ref = f32[32,768]{1,0:T(8,128)S(1)} collective-permute-done((f32[32,768]{1,0:T(8,128)S(1)}, f32[32,768]{1,0:T(8,128)S(1)}, u32[]{:S(2)}, u32[]{:S(2)}) %collective-permute-start.12) | collective-permute-done | bytes 98336 | tf_op jit(solution)/shard_map/ppermute | solution.py:493
  61.1 1.9 %collective-permute-start.14 = (f32[32,768]{1,0:T(8,128)S(1)}, f32[32,768]{1,0:T(8,128)S(1)}, u32[]{:S(2)}, u32[]{:S(2)}) collective-permute-start(f32[32,768]{1,0:T(8,128)S(1)} %add.6.own_ref), channel_id=1, source_target_pairs={{0,8},{8,0},{16,24},{24,16},{1,9},{9,1},{17,25},{25,17},{2,10},{10... | collective-permute-start | bytes 294920 | tf_op jit(solution)/shard_map/ppermute | solution.py:493
  63.0 1.3 %collective-permute-done.15.received_ref = f32[32,768]{1,0:T(8,128)S(1)} collective-permute-done((f32[32,768]{1,0:T(8,128)S(1)}, f32[32,768]{1,0:T(8,128)S(1)}, u32[]{:S(2)}, u32[]{:S(2)}) %collective-permute-start.15) | collective-permute-done | bytes 98336 | tf_op jit(solution)/shard_map/ppermute | solution.py:493
  64.3 0.8 collective-permute-start.17
  65.1 1.2 %collective-permute-done.14.received_ref = f32[32,768]{1,0:T(8,128)S(1)} collective-permute-done((f32[32,768]{1,0:T(8,128)S(1)}, f32[32,768]{1,0:T(8,128)S(1)}, u32[]{:S(2)}, u32[]{:S(2)}) %collective-permute-start.14) | collective-permute-done | bytes 98336 | tf_op jit(solution)/shard_map/ppermute | solution.py:493
  66.3 1.5 %collective-permute-start.16 = (f32[64,768]{1,0:T(8,128)S(1)}, f32[64,768]{1,0:T(8,128)S(1)}, u32[]{:S(2)}, u32[]{:S(2)}) collective-permute-start(f32[64,768]{1,0:T(8,128)S(1)} %join.2.refs_0_), channel_id=1, source_target_pairs={{0,4},{2,6},{4,0},{6,2},{1,5},{3,7},{5,1},{7,3},{8,12},{10,14},{12... | collective-permute-start | bytes 589832 | tf_op jit(solution)/shard_map/ppermute | solution.py:501
  67.9 1.7 %collective-permute-done.17.received_ref = f32[32,768]{1,0:T(8,128)S(1)} collective-permute-done((f32[32,768]{1,0:T(8,128)S(1)}, f32[32,768]{1,0:T(8,128)S(1)}, u32[]{:S(2)}, u32[]{:S(2)}) %collective-permute-start.17) | collective-permute-done | bytes 98336 | tf_op jit(solution)/shard_map/ppermute | solution.py:493
  69.6 1.2 %collective-permute-start.18 = (bf16[2,2,208,256]{3,2,1,0:T(8,128)(2,1)S(1)}, bf16[2,2,208,256]{3,2,1,0:T(8,128)(2,1)S(1)}, u32[]{:S(2)}, u32[]{:S(2)}) collective-permute-start(bf16[2,2,208,256]{3,2,1,0:T(8,128)(2,1)S(1)} %stack.1), channel_id=1, source_target_pairs={{0,8},{8,0},{16,24},{24,16},{1,9},{9,1},{17,25},{25,17},{2,10},{10... | collective-permute-start | bytes 1277960 | tf_op jit(solution)/shard_map/ppermute | solution.py:493
  70.8 1.3 %collective-permute-start.19 = (f32[64,768]{1,0:T(8,128)S(1)}, f32[64,768]{1,0:T(8,128)S(1)}, u32[]{:S(2)}, u32[]{:S(2)}) collective-permute-start(f32[64,768]{1,0:T(8,128)S(1)} %join.3.refs_2_), channel_id=1, source_target_pairs={{0,4},{2,6},{4,0},{6,2},{1,5},{3,7},{5,1},{7,3},{8,12},{10,14},{12... | collective-permute-start | bytes 589832 | tf_op jit(solution)/shard_map/ppermute | solution.py:501
  72.1 0.7 collective-permute-done.16.refs_1_
  72.8 2.2 %update_weights.2.refs_3_ = bf16[2,768,768]{2,1,0:T(8,128)(2,1)} custom-call(bf16[2,768,768]{2,1,0:T(8,128)(2,1)S(1)} %get-tuple-element.172.weights_ref, bf16[2,256,768]{2,1,0:T(8,128)(2,1)S(1)} %get-tuple-element.173.high_ref, bf16[2,256,768]{2,1,0:T(8,128)(2,1)S(1)} %get-tuple-element.174.low_ref, bf16[1,2,208,256]{3,2,1,0:T(8,128)(2,1)S(1)} %bitcast.2, ...), custom_call_target="tpu_custom_call" | custom-call | flops 3000000000 | tf_op jit(solution)/shard_map/update_weights/pallas_call | solution.py:475
  75.0 1.4 %collective-permute-done.19.refs_3_ = f32[64,768]{1,0:T(8,128)S(1)} collective-permute-done((f32[64,768]{1,0:T(8,128)S(1)}, f32[64,768]{1,0:T(8,128)S(1)}, u32[]{:S(2)}, u32[]{:S(2)}) %collective-permute-start.19) | collective-permute-done | bytes 196640 | tf_op jit(solution)/shard_map/ppermute | solution.py:501
  76.5 3.5 %newton_schulz.1.refs_2_ = f32[768,256]{1,0:T(8,128)S(1)} custom-call(f32[64,768]{1,0:T(8,128)S(1)} %join.2.refs_0_, f32[64,768]{1,0:T(8,128)S(1)} %collective-permute-done.16.refs_1_, f32[64,768]{1,0:T(8,128)S(1)} %join.3.refs_2_, f32[64,768]{1,0:T(8,128)S(1)} %collective-permute-done.19.refs_3_), custom_call_target="tpu_custom_call" | custom-call | tf_op jit(solution)/shard_map/newton_schulz/pallas_call | solution.py:115
  80.0 0.1 collective-permute-start.20
  80.0 2.2 %update_weights.3 = (bf16[2,768,768]{2,1,0:T(8,128)(2,1)}, f32[2,768,256]{2,1,0:T(8,128)}) custom-call(bf16[2,768,768]{2,1,0:T(8,128)(2,1)S(1)} %get-tuple-element.172.weights_ref, bf16[2,256,768]{2,1,0:T(8,128)(2,1)S(1)} %get-tuple-element.173.high_ref, bf16[2,256,768]{2,1,0:T(8,128)(2,1)S(1)} %get-tuple-element.174.low_ref, ...), custom_call_target="tpu_custom_call", output_to_operand_aliasing={{0}: (6, {})} | custom-call | flops 8000000000 | tf_op jit(solution)/shard_map/update_weights/pallas_call | solution.py:475
  82.3 0.9 %put_layer.1 = f32[2,768,256]{2,1,0:T(8,128)} custom-call(f32[768,256]{1,0:T(8,128)S(1)} %collective-permute-done.20.layer_ref, f32[2,768,256]{2,1,0:T(8,128)} %get-tuple-element.187.whole_ref), custom_call_target="tpu_custom_call", output_to_operand_aliasing={{}: (1, {})} | custom-call | tf_op jit(solution)/shard_map/put_layer/pallas_call | solution.py:422
  (24 shorter events, 0.5 us)
Async XLA Ops:
  2.9 8.3 %collective-permute-start = (bf16[416,256]{1,0:T(8,128)(2,1)S(1)}, bf16[416,256]{1,0:T(8,128)(2,1)S(1)}, u32[]{:S(2)}, u32[]{:S(2)}) collective-permute-start(bf16[416,256]{1,0:T(8,128)(2,1)S(1)} %give.1), channel_id=1, source_target_pairs={{0,8},{8,0},{16,24},{24,16},{1,9},{9,1},{17,25},{25,17},{2,10},{10... | collective-permute-start | bytes 638984 | tf_op jit(solution)/shard_map/ppermute | solution.py:493
  9.5 25.6 %copy-start = (f32[2,192,256]{2,1,0:T(8,128)S(1)}, f32[2,192,256]{2,1,0:T(8,128)}, u32[]{:S(2)}) copy-start(f32[2,192,256]{2,1,0:T(8,128)} %first_ref.3) | copy-start | bytes 1179652
  9.5 25.6 %copy-start.1 = (f32[2,192,256]{2,1,0:T(8,128)S(1)}, f32[2,192,256]{2,1,0:T(8,128)}, u32[]{:S(2)}) copy-start(f32[2,192,256]{2,1,0:T(8,128)} %second_ref.3) | copy-start | bytes 1179652
  11.6 7.4 %collective-permute-start.1 = (bf16[416,256]{1,0:T(8,128)(2,1)S(1)}, bf16[416,256]{1,0:T(8,128)(2,1)S(1)}, u32[]{:S(2)}, u32[]{:S(2)}) collective-permute-start(bf16[416,256]{1,0:T(8,128)(2,1)S(1)} %get-tuple-element.112), channel_id=1, source_target_pairs={{0,8},{8,0},{16,24},{24,16},{1,9},{9,1},{17,25},{25,17},{2,10},{10... | collective-permute-start | bytes 638984 | tf_op jit(solution)/shard_map/ppermute | solution.py:493
  13.4 15.4 %collective-permute-start.3 = (bf16[416,256]{1,0:T(8,128)(2,1)S(1)}, bf16[416,256]{1,0:T(8,128)(2,1)S(1)}, u32[]{:S(2)}, u32[]{:S(2)}) collective-permute-start(bf16[416,256]{1,0:T(8,128)(2,1)S(1)} %get-tuple-element.117), channel_id=1, source_target_pairs={{0,24},{8,16},{16,8},{24,0},{1,25},{9,17},{17,9},{25,1},{2,26},{10... | collective-permute-start | bytes 638984 | tf_op jit(solution)/shard_map/ppermute | solution.py:493
  19.4 13.4 %collective-permute-start.2 = (bf16[416,256]{1,0:T(8,128)(2,1)S(1)}, bf16[416,256]{1,0:T(8,128)(2,1)S(1)}, u32[]{:S(2)}, u32[]{:S(2)}) collective-permute-start(bf16[416,256]{1,0:T(8,128)(2,1)S(1)} %get-tuple-element.116), channel_id=1, source_target_pairs={{0,24},{8,16},{16,8},{24,0},{1,25},{9,17},{17,9},{25,1},{2,26},{10... | collective-permute-start | bytes 638984 | tf_op jit(solution)/shard_map/ppermute | solution.py:493
  29.2 5.9 %collective-permute-start.5 = (bf16[416,256]{1,0:T(8,128)(2,1)S(1)}, bf16[416,256]{1,0:T(8,128)(2,1)S(1)}, u32[]{:S(2)}, u32[]{:S(2)}) collective-permute-start(bf16[416,256]{1,0:T(8,128)(2,1)S(1)} %get-tuple-element.125), channel_id=1, source_target_pairs={{0,8},{8,0},{16,24},{24,16},{1,9},{9,1},{17,25},{25,17},{2,10},{10... | collective-permute-start | bytes 638984 | tf_op jit(solution)/shard_map/ppermute | solution.py:493
  33.1 6.8 %collective-permute-start.4 = (bf16[416,256]{1,0:T(8,128)(2,1)S(1)}, bf16[416,256]{1,0:T(8,128)(2,1)S(1)}, u32[]{:S(2)}, u32[]{:S(2)}) collective-permute-start(bf16[416,256]{1,0:T(8,128)(2,1)S(1)} %get-tuple-element.124), channel_id=1, source_target_pairs={{0,8},{8,0},{16,24},{24,16},{1,9},{9,1},{17,25},{25,17},{2,10},{10... | collective-permute-start | bytes 638984 | tf_op jit(solution)/shard_map/ppermute | solution.py:493
  36.6 4.8 %collective-permute-start.6 = (f32[128,768]{1,0:T(8,128)S(1)}, f32[128,768]{1,0:T(8,128)S(1)}, u32[]{:S(2)}, u32[]{:S(2)}) collective-permute-start(f32[128,768]{1,0:T(8,128)S(1)} %get-tuple-element.136), channel_id=1, source_target_pairs={{0,2},{2,0},{4,6},{6,4},{1,3},{3,1},{5,7},{7,5},{8,10},{10,8},{12,... | collective-permute-start | bytes 1179656 | tf_op jit(solution)/shard_map/ppermute | solution.py:497
  36.7 4.7 %collective-permute-start.7 = (f32[128,768]{1,0:T(8,128)S(1)}, f32[128,768]{1,0:T(8,128)S(1)}, u32[]{:S(2)}, u32[]{:S(2)}) collective-permute-start(f32[128,768]{1,0:T(8,128)S(1)} %get-tuple-element.128), channel_id=1, source_target_pairs={{0,2},{2,0},{4,6},{6,4},{1,3},{3,1},{5,7},{7,5},{8,10},{10,8},{12,... | collective-permute-start | bytes 1179656 | tf_op jit(solution)/shard_map/ppermute | solution.py:497
  41.4 5.7 %collective-permute-start.9 = (f32[64,768]{1,0:T(8,128)S(1)}, f32[64,768]{1,0:T(8,128)S(1)}, u32[]{:S(2)}, u32[]{:S(2)}) collective-permute-start(f32[64,768]{1,0:T(8,128)S(1)} %get-tuple-element.145), channel_id=1, source_target_pairs={{0,4},{2,6},{4,0},{6,2},{1,5},{3,7},{5,1},{7,3},{8,12},{10,14},{12... | collective-permute-start | bytes 589832 | tf_op jit(solution)/shard_map/ppermute | solution.py:501
  43.1 10.1 %collective-permute-start.8 = (bf16[2,208,256]{2,1,0:T(8,128)(2,1)S(1)}, bf16[2,208,256]{2,1,0:T(8,128)(2,1)S(1)}, u32[]{:S(2)}, u32[]{:S(2)}) collective-permute-start(bf16[2,208,256]{2,1,0:T(8,128)(2,1)S(1)} %get-tuple-element.170.a_ref), channel_id=1, source_target_pairs={{0,24},{8,16},{16,8},{24,0},{1,25},{9,17},{17,9},{25,1},{2,26},{10... | collective-permute-start | bytes 638984 | tf_op jit(solution)/shard_map/ppermute | solution.py:493
  46.1 5.7 %collective-permute-start.11 = (f32[64,768]{1,0:T(8,128)S(1)}, f32[64,768]{1,0:T(8,128)S(1)}, u32[]{:S(2)}, u32[]{:S(2)}) collective-permute-start(f32[64,768]{1,0:T(8,128)S(1)} %get-tuple-element.150), channel_id=1, source_target_pairs={{0,4},{2,6},{4,0},{6,2},{1,5},{3,7},{5,1},{7,3},{8,12},{10,14},{12... | collective-permute-start | bytes 589832 | tf_op jit(solution)/shard_map/ppermute | solution.py:501
  47.2 7.1 %collective-permute-start.10 = (f32[32,768]{1,0:T(8,128)S(1)}, f32[32,768]{1,0:T(8,128)S(1)}, u32[]{:S(2)}, u32[]{:S(2)}) collective-permute-start(f32[32,768]{1,0:T(8,128)S(1)} %get-tuple-element.149), channel_id=1, source_target_pairs={{0,8},{8,0},{16,24},{24,16},{1,9},{9,1},{17,25},{25,17},{2,10},{10... | collective-permute-start | bytes 294920 | tf_op jit(solution)/shard_map/ppermute | solution.py:493
  51.8 5.8 %collective-permute-start.13 = (f32[32,768]{1,0:T(8,128)S(1)}, f32[32,768]{1,0:T(8,128)S(1)}, u32[]{:S(2)}, u32[]{:S(2)}) collective-permute-start(f32[32,768]{1,0:T(8,128)S(1)} %get-tuple-element.159), channel_id=1, source_target_pairs={{0,8},{8,0},{16,24},{24,16},{1,9},{9,1},{17,25},{25,17},{2,10},{10... | collective-permute-start | bytes 294920 | tf_op jit(solution)/shard_map/ppermute | solution.py:493
  54.3 6.9 %collective-permute-start.12 = (f32[32,768]{1,0:T(8,128)S(1)}, f32[32,768]{1,0:T(8,128)S(1)}, u32[]{:S(2)}, u32[]{:S(2)}) collective-permute-start(f32[32,768]{1,0:T(8,128)S(1)} %add.4.own_ref), channel_id=1, source_target_pairs={{0,24},{8,16},{16,8},{24,0},{1,25},{9,17},{17,9},{25,1},{2,26},{10... | collective-permute-start | bytes 294920 | tf_op jit(solution)/shard_map/ppermute | solution.py:493
  57.6 6.7 %collective-permute-start.15 = (f32[32,768]{1,0:T(8,128)S(1)}, f32[32,768]{1,0:T(8,128)S(1)}, u32[]{:S(2)}, u32[]{:S(2)}) collective-permute-start(f32[32,768]{1,0:T(8,128)S(1)} %add.5.own_ref), channel_id=1, source_target_pairs={{0,24},{8,16},{16,8},{24,0},{1,25},{9,17},{17,9},{25,1},{2,26},{10... | collective-permute-start | bytes 294920 | tf_op jit(solution)/shard_map/ppermute | solution.py:493
  61.1 5.2 %collective-permute-start.14 = (f32[32,768]{1,0:T(8,128)S(1)}, f32[32,768]{1,0:T(8,128)S(1)}, u32[]{:S(2)}, u32[]{:S(2)}) collective-permute-start(f32[32,768]{1,0:T(8,128)S(1)} %add.6.own_ref), channel_id=1, source_target_pairs={{0,8},{8,0},{16,24},{24,16},{1,9},{9,1},{17,25},{25,17},{2,10},{10... | collective-permute-start | bytes 294920 | tf_op jit(solution)/shard_map/ppermute | solution.py:493
  64.3 5.2 %collective-permute-start.17 = (f32[32,768]{1,0:T(8,128)S(1)}, f32[32,768]{1,0:T(8,128)S(1)}, u32[]{:S(2)}, u32[]{:S(2)}) collective-permute-start(f32[32,768]{1,0:T(8,128)S(1)} %add.7.own_ref), channel_id=1, source_target_pairs={{0,8},{8,0},{16,24},{24,16},{1,9},{9,1},{17,25},{25,17},{2,10},{10... | collective-permute-start | bytes 294920 | tf_op jit(solution)/shard_map/ppermute | solution.py:493
  66.3 6.5 %collective-permute-start.16 = (f32[64,768]{1,0:T(8,128)S(1)}, f32[64,768]{1,0:T(8,128)S(1)}, u32[]{:S(2)}, u32[]{:S(2)}) collective-permute-start(f32[64,768]{1,0:T(8,128)S(1)} %join.2.refs_0_), channel_id=1, source_target_pairs={{0,4},{2,6},{4,0},{6,2},{1,5},{3,7},{5,1},{7,3},{8,12},{10,14},{12... | collective-permute-start | bytes 589832 | tf_op jit(solution)/shard_map/ppermute | solution.py:501
  69.6 10.4 %collective-permute-start.18 = (bf16[2,2,208,256]{3,2,1,0:T(8,128)(2,1)S(1)}, bf16[2,2,208,256]{3,2,1,0:T(8,128)(2,1)S(1)}, u32[]{:S(2)}, u32[]{:S(2)}) collective-permute-start(bf16[2,2,208,256]{3,2,1,0:T(8,128)(2,1)S(1)} %stack.1), channel_id=1, source_target_pairs={{0,8},{8,0},{16,24},{24,16},{1,9},{9,1},{17,25},{25,17},{2,10},{10... | collective-permute-start | bytes 1277960 | tf_op jit(solution)/shard_map/ppermute | solution.py:493
  70.8 5.7 %collective-permute-start.19 = (f32[64,768]{1,0:T(8,128)S(1)}, f32[64,768]{1,0:T(8,128)S(1)}, u32[]{:S(2)}, u32[]{:S(2)}) collective-permute-start(f32[64,768]{1,0:T(8,128)S(1)} %join.3.refs_2_), channel_id=1, source_target_pairs={{0,4},{2,6},{4,0},{6,2},{1,5},{3,7},{5,1},{7,3},{8,12},{10,14},{12... | collective-permute-start | bytes 589832 | tf_op jit(solution)/shard_map/ppermute | solution.py:501
  80.0 2.4 %collective-permute-start.20 = (f32[768,256]{1,0:T(8,128)S(1)}, f32[768,256]{1,0:T(8,128)S(1)}, u32[]{:S(2)}, u32[]{:S(2)}) collective-permute-start(f32[768,256]{1,0:T(8,128)S(1)} %newton_schulz.1.refs_2_), channel_id=1, source_target_pairs={{0,2},{2,0},{4,6},{6,4},{1,3},{3,1},{5,7},{7,5},{8,10},{10,8},{12,... | collective-permute-start | bytes 2359304 | tf_op jit(solution)/shard_map/ppermute | solution.py:497

commit v7 on v6

--- a/solution.py
+++ b/solution.py
@@ -333,7 +333,7 @@
         + [pltpu.SemaphoreType.DMA((2,))],
         input_output_aliases={count: HALVES, count + 1: HALVES + 1} if before else {},
         compiler_params=params(12),
-        cost_estimate=cost(5e9 * turn),
+        cost_estimate=cost(2e9 * turn),
         name="power",
     )(*operands, *before[:2], *in_vmem(*before[2:]))
 
@@ -453,11 +453,14 @@
         copies[0].start()
     for layer in range(layers):
         basis = high_ref[layer], low_ref[layer]
-        for i, (direction, (k, source)) in enumerate(zip(directions, blocks)):
+        exact = jnp.concatenate(
+            [decode(x[source, layer, 0:rows], x[source, layer, rows:]) for x, (_, source) in zip(directions, blocks)]
+        )
+        update = dot3(split(exact), basis)
+        for i, (k, _) in enumerate(blocks):
             where = pl.ds(pl.multiple_of((place.z ^ k) * rows, rows), rows)
-            exact = decode(direction[source, layer, 0:rows], direction[source, layer, rows:])
-            update = dot3(split(exact), basis)
-            buffer[layer, i] = (weights_ref[layer, where].astype(jnp.float32) - factor * update).astype(buffer.dtype)
+            part = update[i * rows : (i + 1) * rows]
+            buffer[layer, i] = (weights_ref[layer, where].astype(jnp.float32) - factor * part).astype(buffer.dtype)
             copies.append(pltpu.make_async_copy(buffer.at[layer, i], out_ref.at[layer, where], sems.at[layer, i]))
             copies[-1].start()
     for copy in copies:

time: 83.4 us -> 83.3 us (level)
  waiting for transfers between devices: 19.9 us -> 18.8 us
    ppermute x14, waiting for transfers between devices: 16.4 us -> 15.6 us  [over_z(): return lax.ppermute(x, 'shard', xor_pairs(k))]
where the time goes in v7:
time: 83.3 us; the launch traced here: 83.1 us
  starting transfers between devices  42.3 us (51%)
  Pallas kernels  21 us (25%)
  waiting for transfers between devices  18.8 us (23%)
  between operations  0.86 us (1%)
    ppermute x14, starting transfers between devices, over_z(): return lax.ppermute(x, 'shard', xor_pairs(k))  36 us
    ppermute x14, waiting for transfers between devices, over_z(): return lax.ppermute(x, 'shard', xor_pairs(k))  15.6 us
    pallas_call x18, Pallas kernels, local_call(): pl.pallas_call(kernel, out_shape=[pltpu.VMEM(shape, dtype) for shape, dty...  6.38 us
    ppermute x4, starting transfers between devices, over_y(): return lax.ppermute(x, 'tensor', xor_pairs(2))  5.68 us
    pallas_call x2, Pallas kernels, update_weights(): pl.pallas_call(functools.partial(update_kernel, factor, blocks), out_shap...  4.6 us
    ppermute x4, waiting for transfers between devices, over_y(): return lax.ppermute(x, 'tensor', xor_pairs(2))  3.25 us
    pallas_call x2, Pallas kernels, power_product(): pl.pallas_call(functools.partial(power_kernel, turn, scale), out_shape=[p...  3.01 us
    pallas_call x1, Pallas kernels, give(): pl.pallas_call(give_kernel, out_shape=pltpu.VMEM((2 * (rows + 16), rank),...  2.28 us
  transfers between devices with their start and end apart: 21, of which 14 were waited for; matrix products, arithmetic and copies ran while one was open for 0% of the time, Pallas kernels for 21%

profile of v7, /device:TPU:0, one launch (start us, length us, event | category | flops | bytes accessed | tf_op | source)
XLA Modules:
  0.0 83.1 jit_solution(14270062114338976496)
XLA Ops:
  0.6 2.3 %give.1 = bf16[416,256]{1,0:T(8,128)(2,1)S(1)} custom-call(bf16[1,2,768,768]{3,2,1,0:T(8,128)(2,1)} %grads_hbm.2, f32[2,768,256]{2,1,0:T(8,128)} %basis_hbm.2), custom_call_target="tpu_custom_call" | custom-call | tf_op jit(solution)/shard_map/give/pallas_call | solution.py:243
  2.9 3.1 %collective-permute-start = (bf16[416,256]{1,0:T(8,128)(2,1)S(1)}, bf16[416,256]{1,0:T(8,128)(2,1)S(1)}, u32[]{:S(2)}, u32[]{:S(2)}) collective-permute-start(bf16[416,256]{1,0:T(8,128)(2,1)S(1)} %give.1), channel_id=1, source_target_pairs={{0,8},{8,0},{16,24},{24,16},{1,9},{9,1},{17,25},{25,17},{2,10},{10... | collective-permute-start | bytes 638984 | tf_op jit(solution)/shard_map/ppermute | solution.py:496
  6.0 2.1 %prepare.1 = (bf16[1,2,768,768]{3,2,1,0:T(8,128)(2,1)S(1)}, bf16[2,768,256]{2,1,0:T(8,128)(2,1)S(1)}, bf16[2,768,256]{2,1,0:T(8,128)(2,1)S(1)}) custom-call(bf16[1,2,768,768]{3,2,1,0:T(8,128)(2,1)} %grads_hbm.2, f32[2,768,256]{2,1,0:T(8,128)} %basis_hbm.2), custom_call_target="tpu_custom_call" | custom-call | tf_op jit(solution)/shard_map/prepare/pallas_call | solution.py:164
  8.2 0.5 project.2.own_ref
  8.6 0.8 project.3
  9.5 1.7 %fetch.1 = (bf16[2,768,768]{2,1,0:T(8,128)(2,1)S(1)}, bf16[2,256,768]{2,1,0:T(8,128)(2,1)S(1)}, bf16[2,256,768]{2,1,0:T(8,128)(2,1)S(1)}) custom-call(bf16[2,768,768]{2,1,0:T(8,128)(2,1)} %weights_hbm, bf16[2,768,256]{2,1,0:T(8,128)(2,1)S(1)} %get-tuple-element.106.high_ref, bf16[2,768,256]{2,1,0:T(8,128)(2,1)S(1)} %get-tuple-element.107.low_ref), custom_call_target="tpu_custom_call" | custom-call | tf_op jit(solution)/shard_map/fetch/pallas_call | solution.py:190
  11.3 0.3 add_coded.4
  11.6 1.8 %collective-permute-start.1 = (bf16[416,256]{1,0:T(8,128)(2,1)S(1)}, bf16[416,256]{1,0:T(8,128)(2,1)S(1)}, u32[]{:S(2)}, u32[]{:S(2)}) collective-permute-start(bf16[416,256]{1,0:T(8,128)(2,1)S(1)} %get-tuple-element.112), channel_id=1, source_target_pairs={{0,8},{8,0},{16,24},{24,16},{1,9},{9,1},{17,25},{25,17},{2,10},{10... | collective-permute-start | bytes 638984 | tf_op jit(solution)/shard_map/ppermute | solution.py:496
  13.4 2.5 %collective-permute-start.3 = (bf16[416,256]{1,0:T(8,128)(2,1)S(1)}, bf16[416,256]{1,0:T(8,128)(2,1)S(1)}, u32[]{:S(2)}, u32[]{:S(2)}) collective-permute-start(bf16[416,256]{1,0:T(8,128)(2,1)S(1)} %get-tuple-element.117), channel_id=1, source_target_pairs={{0,24},{8,16},{16,8},{24,0},{1,25},{9,17},{17,9},{25,1},{2,26},{10... | collective-permute-start | bytes 638984 | tf_op jit(solution)/shard_map/ppermute | solution.py:496
  15.9 3.1 %collective-permute-done.1.received_ref = bf16[416,256]{1,0:T(8,128)(2,1)S(1)} collective-permute-done((bf16[416,256]{1,0:T(8,128)(2,1)S(1)}, bf16[416,256]{1,0:T(8,128)(2,1)S(1)}, u32[]{:S(2)}, u32[]{:S(2)}) %collective-permute-start.1) | collective-permute-done | bytes 213024 | tf_op jit(solution)/shard_map/ppermute | solution.py:496
  19.0 0.3 add_coded.5
  19.4 9.5 %collective-permute-start.2 = (bf16[416,256]{1,0:T(8,128)(2,1)S(1)}, bf16[416,256]{1,0:T(8,128)(2,1)S(1)}, u32[]{:S(2)}, u32[]{:S(2)}) collective-permute-start(bf16[416,256]{1,0:T(8,128)(2,1)S(1)} %get-tuple-element.116), channel_id=1, source_target_pairs={{0,24},{8,16},{16,8},{24,0},{1,25},{9,17},{17,9},{25,1},{2,26},{10... | collective-permute-start | bytes 638984 | tf_op jit(solution)/shard_map/ppermute | solution.py:496
  28.8 0.3 add_coded.6
  29.3 3.5 %collective-permute-done.2.received_ref = bf16[416,256]{1,0:T(8,128)(2,1)S(1)} collective-permute-done((bf16[416,256]{1,0:T(8,128)(2,1)S(1)}, bf16[416,256]{1,0:T(8,128)(2,1)S(1)}, u32[]{:S(2)}, u32[]{:S(2)}) %collective-permute-start.2) | collective-permute-done | bytes 213024 | tf_op jit(solution)/shard_map/ppermute | solution.py:496
  32.8 0.3 add_coded.7
  33.1 1.7 %collective-permute-start.4 = (bf16[416,256]{1,0:T(8,128)(2,1)S(1)}, bf16[416,256]{1,0:T(8,128)(2,1)S(1)}, u32[]{:S(2)}, u32[]{:S(2)}) collective-permute-start(bf16[416,256]{1,0:T(8,128)(2,1)S(1)} %get-tuple-element.124), channel_id=1, source_target_pairs={{0,8},{8,0},{16,24},{24,16},{1,9},{9,1},{17,25},{25,17},{2,10},{10... | collective-permute-start | bytes 638984 | tf_op jit(solution)/shard_map/ppermute | solution.py:496
  34.8 0.3 collective-permute-done.5.given_ref
  35.1 1.5 %power.2 = (f32[128,768]{1,0:T(8,128)S(1)}, f32[128,768]{1,0:T(8,128)S(1)}, f32[2,192,256]{2,1,0:T(8,128)}, f32[2,192,256]{2,1,0:T(8,128)}, bf16[208,256]{1,0:T(8,128)(2,1)S(1)}) custom-call(bf16[1,2,768,768]{3,2,1,0:T(8,128)(2,1)S(1)} %get-tuple-element.102.grads_ref, f32[2,192,256]{2,1,0:T(8,128)S(1)} %copy-done, f32[2,192,256]{2,1,0:T(8,128)S(1)} %copy-done.1, ...), custom_call_target="tpu_custom_call" | custom-call | tf_op jit(solution)/shard_map/power/pallas_call | solution.py:324
  36.6 0.1 collective-permute-start.7
  36.7 0.5 collective-permute-start.6
  37.2 2.7 %collective-permute-done.4.given_ref = bf16[416,256]{1,0:T(8,128)(2,1)S(1)} collective-permute-done((bf16[416,256]{1,0:T(8,128)(2,1)S(1)}, bf16[416,256]{1,0:T(8,128)(2,1)S(1)}, u32[]{:S(2)}, u32[]{:S(2)}) %collective-permute-start.4) | collective-permute-done | bytes 213024 | tf_op jit(solution)/shard_map/ppermute | solution.py:496
  39.9 1.5 %power.3 = (f32[128,768]{1,0:T(8,128)S(1)}, f32[128,768]{1,0:T(8,128)S(1)}, f32[2,192,256]{2,1,0:T(8,128)}, f32[2,192,256]{2,1,0:T(8,128)}, bf16[2,208,256]{2,1,0:T(8,128)(2,1)S(1)}) custom-call(bf16[1,2,768,768]{3,2,1,0:T(8,128)(2,1)S(1)} %get-tuple-element.102.grads_ref, f32[2,192,256]{2,1,0:T(8,128)S(1)} %copy-done, ...), custom_call_target="tpu_custom_call", output_to_operand_aliasing={{2}: (5, {}), {3}: (6, {})} | custom-call | flops 2000000000 | tf_op jit(solution)/shard_map/power/pallas_call | solution.py:324
  41.4 1.6 %collective-permute-start.9 = (f32[64,768]{1,0:T(8,128)S(1)}, f32[64,768]{1,0:T(8,128)S(1)}, u32[]{:S(2)}, u32[]{:S(2)}) collective-permute-start(f32[64,768]{1,0:T(8,128)S(1)} %get-tuple-element.145), channel_id=1, source_target_pairs={{0,4},{2,6},{4,0},{6,2},{1,5},{3,7},{5,1},{7,3},{8,12},{10,14},{12... | collective-permute-start | bytes 589832 | tf_op jit(solution)/shard_map/ppermute | solution.py:504
  43.1 3.0 %collective-permute-start.8 = (bf16[2,208,256]{2,1,0:T(8,128)(2,1)S(1)}, bf16[2,208,256]{2,1,0:T(8,128)(2,1)S(1)}, u32[]{:S(2)}, u32[]{:S(2)}) collective-permute-start(bf16[2,208,256]{2,1,0:T(8,128)(2,1)S(1)} %get-tuple-element.170.a_ref), channel_id=1, source_target_pairs={{0,24},{8,16},{16,8},{24,0},{1,25},{9,17},{17,9},{25,1},{2,26},{10... | collective-permute-start | bytes 638984 | tf_op jit(solution)/shard_map/ppermute | solution.py:496
  46.1 0.5 collective-permute-start.11
  46.6 0.7 collective-permute-done.9.received_ref
  47.3 3.7 %collective-permute-start.10 = (f32[32,768]{1,0:T(8,128)S(1)}, f32[32,768]{1,0:T(8,128)S(1)}, u32[]{:S(2)}, u32[]{:S(2)}) collective-permute-start(f32[32,768]{1,0:T(8,128)S(1)} %get-tuple-element.149), channel_id=1, source_target_pairs={{0,8},{8,0},{16,24},{24,16},{1,9},{9,1},{17,25},{25,17},{2,10},{10... | collective-permute-start | bytes 294920 | tf_op jit(solution)/shard_map/ppermute | solution.py:496
  51.0 0.7 collective-permute-done.11.received_ref
  51.8 1.3 %collective-permute-start.13 = (f32[32,768]{1,0:T(8,128)S(1)}, f32[32,768]{1,0:T(8,128)S(1)}, u32[]{:S(2)}, u32[]{:S(2)}) collective-permute-start(f32[32,768]{1,0:T(8,128)S(1)} %get-tuple-element.159), channel_id=1, source_target_pairs={{0,8},{8,0},{16,24},{24,16},{1,9},{9,1},{17,25},{25,17},{2,10},{10... | collective-permute-start | bytes 294920 | tf_op jit(solution)/shard_map/ppermute | solution.py:496
  53.1 1.0 %collective-permute-done.10.received_ref = f32[32,768]{1,0:T(8,128)S(1)} collective-permute-done((f32[32,768]{1,0:T(8,128)S(1)}, f32[32,768]{1,0:T(8,128)S(1)}, u32[]{:S(2)}, u32[]{:S(2)}) %collective-permute-start.10) | collective-permute-done | bytes 98336 | tf_op jit(solution)/shard_map/ppermute | solution.py:496
  54.2 3.1 %collective-permute-start.12 = (f32[32,768]{1,0:T(8,128)S(1)}, f32[32,768]{1,0:T(8,128)S(1)}, u32[]{:S(2)}, u32[]{:S(2)}) collective-permute-start(f32[32,768]{1,0:T(8,128)S(1)} %add.4.own_ref), channel_id=1, source_target_pairs={{0,24},{8,16},{16,8},{24,0},{1,25},{9,17},{17,9},{25,1},{2,26},{10... | collective-permute-start | bytes 294920 | tf_op jit(solution)/shard_map/ppermute | solution.py:496
  57.4 0.2 collective-permute-done.13.received_ref
  57.5 2.1 %collective-permute-start.15 = (f32[32,768]{1,0:T(8,128)S(1)}, f32[32,768]{1,0:T(8,128)S(1)}, u32[]{:S(2)}, u32[]{:S(2)}) collective-permute-start(f32[32,768]{1,0:T(8,128)S(1)} %add.5.own_ref), channel_id=1, source_target_pairs={{0,24},{8,16},{16,8},{24,0},{1,25},{9,17},{17,9},{25,1},{2,26},{10... | collective-permute-start | bytes 294920 | tf_op jit(solution)/shard_map/ppermute | solution.py:496
  59.6 1.3 %collective-permute-done.12.received_ref = f32[32,768]{1,0:T(8,128)S(1)} collective-permute-done((f32[32,768]{1,0:T(8,128)S(1)}, f32[32,768]{1,0:T(8,128)S(1)}, u32[]{:S(2)}, u32[]{:S(2)}) %collective-permute-start.12) | collective-permute-done | bytes 98336 | tf_op jit(solution)/shard_map/ppermute | solution.py:496
  60.9 2.0 %collective-permute-start.14 = (f32[32,768]{1,0:T(8,128)S(1)}, f32[32,768]{1,0:T(8,128)S(1)}, u32[]{:S(2)}, u32[]{:S(2)}) collective-permute-start(f32[32,768]{1,0:T(8,128)S(1)} %add.6.own_ref), channel_id=1, source_target_pairs={{0,8},{8,0},{16,24},{24,16},{1,9},{9,1},{17,25},{25,17},{2,10},{10... | collective-permute-start | bytes 294920 | tf_op jit(solution)/shard_map/ppermute | solution.py:496
  62.9 1.3 %collective-permute-done.15.received_ref = f32[32,768]{1,0:T(8,128)S(1)} collective-permute-done((f32[32,768]{1,0:T(8,128)S(1)}, f32[32,768]{1,0:T(8,128)S(1)}, u32[]{:S(2)}, u32[]{:S(2)}) %collective-permute-start.15) | collective-permute-done | bytes 98336 | tf_op jit(solution)/shard_map/ppermute | solution.py:496
  64.2 0.8 collective-permute-start.17
  65.0 1.2 %collective-permute-done.14.received_ref = f32[32,768]{1,0:T(8,128)S(1)} collective-permute-done((f32[32,768]{1,0:T(8,128)S(1)}, f32[32,768]{1,0:T(8,128)S(1)}, u32[]{:S(2)}, u32[]{:S(2)}) %collective-permute-start.14) | collective-permute-done | bytes 98336 | tf_op jit(solution)/shard_map/ppermute | solution.py:496
  66.2 2.0 %collective-permute-start.16 = (f32[64,768]{1,0:T(8,128)S(1)}, f32[64,768]{1,0:T(8,128)S(1)}, u32[]{:S(2)}, u32[]{:S(2)}) collective-permute-start(f32[64,768]{1,0:T(8,128)S(1)} %join.2.refs_0_), channel_id=1, source_target_pairs={{0,4},{2,6},{4,0},{6,2},{1,5},{3,7},{5,1},{7,3},{8,12},{10,14},{12... | collective-permute-start | bytes 589832 | tf_op jit(solution)/shard_map/ppermute | solution.py:504
  68.3 1.0 %collective-permute-done.17.received_ref = f32[32,768]{1,0:T(8,128)S(1)} collective-permute-done((f32[32,768]{1,0:T(8,128)S(1)}, f32[32,768]{1,0:T(8,128)S(1)}, u32[]{:S(2)}, u32[]{:S(2)}) %collective-permute-start.17) | collective-permute-done | bytes 98336 | tf_op jit(solution)/shard_map/ppermute | solution.py:496
  69.3 1.3 %collective-permute-start.18 = (bf16[2,2,208,256]{3,2,1,0:T(8,128)(2,1)S(1)}, bf16[2,2,208,256]{3,2,1,0:T(8,128)(2,1)S(1)}, u32[]{:S(2)}, u32[]{:S(2)}) collective-permute-start(bf16[2,2,208,256]{3,2,1,0:T(8,128)(2,1)S(1)} %stack.1), channel_id=1, source_target_pairs={{0,8},{8,0},{16,24},{24,16},{1,9},{9,1},{17,25},{25,17},{2,10},{10... | collective-permute-start | bytes 1277960 | tf_op jit(solution)/shard_map/ppermute | solution.py:496
  70.6 1.6 %collective-permute-start.19 = (f32[64,768]{1,0:T(8,128)S(1)}, f32[64,768]{1,0:T(8,128)S(1)}, u32[]{:S(2)}, u32[]{:S(2)}) collective-permute-start(f32[64,768]{1,0:T(8,128)S(1)} %join.3.refs_2_), channel_id=1, source_target_pairs={{0,4},{2,6},{4,0},{6,2},{1,5},{3,7},{5,1},{7,3},{8,12},{10,14},{12... | collective-permute-start | bytes 589832 | tf_op jit(solution)/shard_map/ppermute | solution.py:504
  72.1 0.8 collective-permute-done.16.refs_1_
  72.9 2.3 %update_weights.2.refs_3_ = bf16[2,768,768]{2,1,0:T(8,128)(2,1)} custom-call(bf16[2,768,768]{2,1,0:T(8,128)(2,1)S(1)} %get-tuple-element.172.weights_ref, bf16[2,256,768]{2,1,0:T(8,128)(2,1)S(1)} %get-tuple-element.173.high_ref, bf16[2,256,768]{2,1,0:T(8,128)(2,1)S(1)} %get-tuple-element.174.low_ref, bf16[1,2,208,256]{3,2,1,0:T(8,128)(2,1)S(1)} %bitcast.2, ...), custom_call_target="tpu_custom_call" | custom-call | flops 3000000000 | tf_op jit(solution)/shard_map/update_weights/pallas_call | solution.py:478
  75.2 1.0 %collective-permute-done.19.refs_3_ = f32[64,768]{1,0:T(8,128)S(1)} collective-permute-done((f32[64,768]{1,0:T(8,128)S(1)}, f32[64,768]{1,0:T(8,128)S(1)}, u32[]{:S(2)}, u32[]{:S(2)}) %collective-permute-start.19) | collective-permute-done | bytes 196640 | tf_op jit(solution)/shard_map/ppermute | solution.py:504
  76.2 3.5 %newton_schulz.1.refs_2_ = f32[768,256]{1,0:T(8,128)S(1)} custom-call(f32[64,768]{1,0:T(8,128)S(1)} %join.2.refs_0_, f32[64,768]{1,0:T(8,128)S(1)} %collective-permute-done.16.refs_1_, f32[64,768]{1,0:T(8,128)S(1)} %join.3.refs_2_, f32[64,768]{1,0:T(8,128)S(1)} %collective-permute-done.19.refs_3_), custom_call_target="tpu_custom_call" | custom-call | tf_op jit(solution)/shard_map/newton_schulz/pallas_call | solution.py:115
  79.8 2.3 %update_weights.3 = (bf16[2,768,768]{2,1,0:T(8,128)(2,1)}, f32[2,768,256]{2,1,0:T(8,128)}) custom-call(bf16[2,768,768]{2,1,0:T(8,128)(2,1)S(1)} %get-tuple-element.172.weights_ref, bf16[2,256,768]{2,1,0:T(8,128)(2,1)S(1)} %get-tuple-element.173.high_ref, bf16[2,256,768]{2,1,0:T(8,128)(2,1)S(1)} %get-tuple-element.174.low_ref, ...), custom_call_target="tpu_custom_call", output_to_operand_aliasing={{0}: (6, {})} | custom-call | flops 8000000000 | tf_op jit(solution)/shard_map/update_weights/pallas_call | solution.py:478
  82.2 0.9 %put_layer.1 = f32[2,768,256]{2,1,0:T(8,128)} custom-call(f32[768,256]{1,0:T(8,128)S(1)} %collective-permute-done.20.layer_ref, f32[2,768,256]{2,1,0:T(8,128)} %get-tuple-element.187.whole_ref), custom_call_target="tpu_custom_call", output_to_operand_aliasing={{}: (1, {})} | custom-call | tf_op jit(solution)/shard_map/put_layer/pallas_call | solution.py:422
  (24 shorter events, 0.5 us)
Async XLA Ops:
  2.9 8.3 %collective-permute-start = (bf16[416,256]{1,0:T(8,128)(2,1)S(1)}, bf16[416,256]{1,0:T(8,128)(2,1)S(1)}, u32[]{:S(2)}, u32[]{:S(2)}) collective-permute-start(bf16[416,256]{1,0:T(8,128)(2,1)S(1)} %give.1), channel_id=1, source_target_pairs={{0,8},{8,0},{16,24},{24,16},{1,9},{9,1},{17,25},{25,17},{2,10},{10... | collective-permute-start | bytes 638984 | tf_op jit(solution)/shard_map/ppermute | solution.py:496
  9.5 25.6 %copy-start = (f32[2,192,256]{2,1,0:T(8,128)S(1)}, f32[2,192,256]{2,1,0:T(8,128)}, u32[]{:S(2)}) copy-start(f32[2,192,256]{2,1,0:T(8,128)} %first_ref.3) | copy-start | bytes 1179652
  9.5 25.6 %copy-start.1 = (f32[2,192,256]{2,1,0:T(8,128)S(1)}, f32[2,192,256]{2,1,0:T(8,128)}, u32[]{:S(2)}) copy-start(f32[2,192,256]{2,1,0:T(8,128)} %second_ref.3) | copy-start | bytes 1179652
  11.6 7.4 %collective-permute-start.1 = (bf16[416,256]{1,0:T(8,128)(2,1)S(1)}, bf16[416,256]{1,0:T(8,128)(2,1)S(1)}, u32[]{:S(2)}, u32[]{:S(2)}) collective-permute-start(bf16[416,256]{1,0:T(8,128)(2,1)S(1)} %get-tuple-element.112), channel_id=1, source_target_pairs={{0,8},{8,0},{16,24},{24,16},{1,9},{9,1},{17,25},{25,17},{2,10},{10... | collective-permute-start | bytes 638984 | tf_op jit(solution)/shard_map/ppermute | solution.py:496
  13.4 15.4 %collective-permute-start.3 = (bf16[416,256]{1,0:T(8,128)(2,1)S(1)}, bf16[416,256]{1,0:T(8,128)(2,1)S(1)}, u32[]{:S(2)}, u32[]{:S(2)}) collective-permute-start(bf16[416,256]{1,0:T(8,128)(2,1)S(1)} %get-tuple-element.117), channel_id=1, source_target_pairs={{0,24},{8,16},{16,8},{24,0},{1,25},{9,17},{17,9},{25,1},{2,26},{10... | collective-permute-start | bytes 638984 | tf_op jit(solution)/shard_map/ppermute | solution.py:496
  19.4 13.4 %collective-permute-start.2 = (bf16[416,256]{1,0:T(8,128)(2,1)S(1)}, bf16[416,256]{1,0:T(8,128)(2,1)S(1)}, u32[]{:S(2)}, u32[]{:S(2)}) collective-permute-start(bf16[416,256]{1,0:T(8,128)(2,1)S(1)} %get-tuple-element.116), channel_id=1, source_target_pairs={{0,24},{8,16},{16,8},{24,0},{1,25},{9,17},{17,9},{25,1},{2,26},{10... | collective-permute-start | bytes 638984 | tf_op jit(solution)/shard_map/ppermute | solution.py:496
  29.2 5.9 %collective-permute-start.5 = (bf16[416,256]{1,0:T(8,128)(2,1)S(1)}, bf16[416,256]{1,0:T(8,128)(2,1)S(1)}, u32[]{:S(2)}, u32[]{:S(2)}) collective-permute-start(bf16[416,256]{1,0:T(8,128)(2,1)S(1)} %get-tuple-element.125), channel_id=1, source_target_pairs={{0,8},{8,0},{16,24},{24,16},{1,9},{9,1},{17,25},{25,17},{2,10},{10... | collective-permute-start | bytes 638984 | tf_op jit(solution)/shard_map/ppermute | solution.py:496
  33.1 6.8 %collective-permute-start.4 = (bf16[416,256]{1,0:T(8,128)(2,1)S(1)}, bf16[416,256]{1,0:T(8,128)(2,1)S(1)}, u32[]{:S(2)}, u32[]{:S(2)}) collective-permute-start(bf16[416,256]{1,0:T(8,128)(2,1)S(1)} %get-tuple-element.124), channel_id=1, source_target_pairs={{0,8},{8,0},{16,24},{24,16},{1,9},{9,1},{17,25},{25,17},{2,10},{10... | collective-permute-start | bytes 638984 | tf_op jit(solution)/shard_map/ppermute | solution.py:496
  36.6 4.8 %collective-permute-start.7 = (f32[128,768]{1,0:T(8,128)S(1)}, f32[128,768]{1,0:T(8,128)S(1)}, u32[]{:S(2)}, u32[]{:S(2)}) collective-permute-start(f32[128,768]{1,0:T(8,128)S(1)} %get-tuple-element.128), channel_id=1, source_target_pairs={{0,2},{2,0},{4,6},{6,4},{1,3},{3,1},{5,7},{7,5},{8,10},{10,8},{12,... | collective-permute-start | bytes 1179656 | tf_op jit(solution)/shard_map/ppermute | solution.py:500
  36.7 4.7 %collective-permute-start.6 = (f32[128,768]{1,0:T(8,128)S(1)}, f32[128,768]{1,0:T(8,128)S(1)}, u32[]{:S(2)}, u32[]{:S(2)}) collective-permute-start(f32[128,768]{1,0:T(8,128)S(1)} %get-tuple-element.136), channel_id=1, source_target_pairs={{0,2},{2,0},{4,6},{6,4},{1,3},{3,1},{5,7},{7,5},{8,10},{10,8},{12,... | collective-permute-start | bytes 1179656 | tf_op jit(solution)/shard_map/ppermute | solution.py:500
  41.4 5.9 %collective-permute-start.9 = (f32[64,768]{1,0:T(8,128)S(1)}, f32[64,768]{1,0:T(8,128)S(1)}, u32[]{:S(2)}, u32[]{:S(2)}) collective-permute-start(f32[64,768]{1,0:T(8,128)S(1)} %get-tuple-element.145), channel_id=1, source_target_pairs={{0,4},{2,6},{4,0},{6,2},{1,5},{3,7},{5,1},{7,3},{8,12},{10,14},{12... | collective-permute-start | bytes 589832 | tf_op jit(solution)/shard_map/ppermute | solution.py:504
  43.1 10.1 %collective-permute-start.8 = (bf16[2,208,256]{2,1,0:T(8,128)(2,1)S(1)}, bf16[2,208,256]{2,1,0:T(8,128)(2,1)S(1)}, u32[]{:S(2)}, u32[]{:S(2)}) collective-permute-start(bf16[2,208,256]{2,1,0:T(8,128)(2,1)S(1)} %get-tuple-element.170.a_ref), channel_id=1, source_target_pairs={{0,24},{8,16},{16,8},{24,0},{1,25},{9,17},{17,9},{25,1},{2,26},{10... | collective-permute-start | bytes 638984 | tf_op jit(solution)/shard_map/ppermute | solution.py:496
  46.1 5.7 %collective-permute-start.11 = (f32[64,768]{1,0:T(8,128)S(1)}, f32[64,768]{1,0:T(8,128)S(1)}, u32[]{:S(2)}, u32[]{:S(2)}) collective-permute-start(f32[64,768]{1,0:T(8,128)S(1)} %get-tuple-element.150), channel_id=1, source_target_pairs={{0,4},{2,6},{4,0},{6,2},{1,5},{3,7},{5,1},{7,3},{8,12},{10,14},{12... | collective-permute-start | bytes 589832 | tf_op jit(solution)/shard_map/ppermute | solution.py:504
  47.3 6.9 %collective-permute-start.10 = (f32[32,768]{1,0:T(8,128)S(1)}, f32[32,768]{1,0:T(8,128)S(1)}, u32[]{:S(2)}, u32[]{:S(2)}) collective-permute-start(f32[32,768]{1,0:T(8,128)S(1)} %get-tuple-element.149), channel_id=1, source_target_pairs={{0,8},{8,0},{16,24},{24,16},{1,9},{9,1},{17,25},{25,17},{2,10},{10... | collective-permute-start | bytes 294920 | tf_op jit(solution)/shard_map/ppermute | solution.py:496
  51.8 5.7 %collective-permute-start.13 = (f32[32,768]{1,0:T(8,128)S(1)}, f32[32,768]{1,0:T(8,128)S(1)}, u32[]{:S(2)}, u32[]{:S(2)}) collective-permute-start(f32[32,768]{1,0:T(8,128)S(1)} %get-tuple-element.159), channel_id=1, source_target_pairs={{0,8},{8,0},{16,24},{24,16},{1,9},{9,1},{17,25},{25,17},{2,10},{10... | collective-permute-start | bytes 294920 | tf_op jit(solution)/shard_map/ppermute | solution.py:496
  54.2 6.7 %collective-permute-start.12 = (f32[32,768]{1,0:T(8,128)S(1)}, f32[32,768]{1,0:T(8,128)S(1)}, u32[]{:S(2)}, u32[]{:S(2)}) collective-permute-start(f32[32,768]{1,0:T(8,128)S(1)} %add.4.own_ref), channel_id=1, source_target_pairs={{0,24},{8,16},{16,8},{24,0},{1,25},{9,17},{17,9},{25,1},{2,26},{10... | collective-permute-start | bytes 294920 | tf_op jit(solution)/shard_map/ppermute | solution.py:496
  57.5 6.7 %collective-permute-start.15 = (f32[32,768]{1,0:T(8,128)S(1)}, f32[32,768]{1,0:T(8,128)S(1)}, u32[]{:S(2)}, u32[]{:S(2)}) collective-permute-start(f32[32,768]{1,0:T(8,128)S(1)} %add.5.own_ref), channel_id=1, source_target_pairs={{0,24},{8,16},{16,8},{24,0},{1,25},{9,17},{17,9},{25,1},{2,26},{10... | collective-permute-start | bytes 294920 | tf_op jit(solution)/shard_map/ppermute | solution.py:496
  60.9 5.3 %collective-permute-start.14 = (f32[32,768]{1,0:T(8,128)S(1)}, f32[32,768]{1,0:T(8,128)S(1)}, u32[]{:S(2)}, u32[]{:S(2)}) collective-permute-start(f32[32,768]{1,0:T(8,128)S(1)} %add.6.own_ref), channel_id=1, source_target_pairs={{0,8},{8,0},{16,24},{24,16},{1,9},{9,1},{17,25},{25,17},{2,10},{10... | collective-permute-start | bytes 294920 | tf_op jit(solution)/shard_map/ppermute | solution.py:496
  64.2 5.0 %collective-permute-start.17 = (f32[32,768]{1,0:T(8,128)S(1)}, f32[32,768]{1,0:T(8,128)S(1)}, u32[]{:S(2)}, u32[]{:S(2)}) collective-permute-start(f32[32,768]{1,0:T(8,128)S(1)} %add.7.own_ref), channel_id=1, source_target_pairs={{0,8},{8,0},{16,24},{24,16},{1,9},{9,1},{17,25},{25,17},{2,10},{10... | collective-permute-start | bytes 294920 | tf_op jit(solution)/shard_map/ppermute | solution.py:496
  66.2 6.7 %collective-permute-start.16 = (f32[64,768]{1,0:T(8,128)S(1)}, f32[64,768]{1,0:T(8,128)S(1)}, u32[]{:S(2)}, u32[]{:S(2)}) collective-permute-start(f32[64,768]{1,0:T(8,128)S(1)} %join.2.refs_0_), channel_id=1, source_target_pairs={{0,4},{2,6},{4,0},{6,2},{1,5},{3,7},{5,1},{7,3},{8,12},{10,14},{12... | collective-permute-start | bytes 589832 | tf_op jit(solution)/shard_map/ppermute | solution.py:504
  69.3 10.5 %collective-permute-start.18 = (bf16[2,2,208,256]{3,2,1,0:T(8,128)(2,1)S(1)}, bf16[2,2,208,256]{3,2,1,0:T(8,128)(2,1)S(1)}, u32[]{:S(2)}, u32[]{:S(2)}) collective-permute-start(bf16[2,2,208,256]{3,2,1,0:T(8,128)(2,1)S(1)} %stack.1), channel_id=1, source_target_pairs={{0,8},{8,0},{16,24},{24,16},{1,9},{9,1},{17,25},{25,17},{2,10},{10... | collective-permute-start | bytes 1277960 | tf_op jit(solution)/shard_map/ppermute | solution.py:496
  70.6 5.7 %collective-permute-start.19 = (f32[64,768]{1,0:T(8,128)S(1)}, f32[64,768]{1,0:T(8,128)S(1)}, u32[]{:S(2)}, u32[]{:S(2)}) collective-permute-start(f32[64,768]{1,0:T(8,128)S(1)} %join.3.refs_2_), channel_id=1, source_target_pairs={{0,4},{2,6},{4,0},{6,2},{1,5},{3,7},{5,1},{7,3},{8,12},{10,14},{12... | collective-permute-start | bytes 589832 | tf_op jit(solution)/shard_map/ppermute | solution.py:504
  79.7 2.4 %collective-permute-start.20 = (f32[768,256]{1,0:T(8,128)S(1)}, f32[768,256]{1,0:T(8,128)S(1)}, u32[]{:S(2)}, u32[]{:S(2)}) collective-permute-start(f32[768,256]{1,0:T(8,128)S(1)} %newton_schulz.1.refs_2_), channel_id=1, source_target_pairs={{0,2},{2,0},{4,6},{6,4},{1,3},{3,1},{5,7},{7,5},{8,10},{10,8},{12,... | collective-permute-start | bytes 2359304 | tf_op jit(solution)/shard_map/ppermute | solution.py:500

commit v8 on v7

--- a/solution.py
+++ b/solution.py
@@ -393,9 +393,7 @@
     iterate = split(dot3(product, unscaled))
     g = split(gram)
     last = split((diagonal + coeff_b * gram + coeff_c * dot3(g, g)) * (scale * width**0.5))
-    for i in range(width // rank):
-        columns = slice(i * rank, (i + 1) * rank)
-        result_ref[columns] = dot3(last, [term[:, columns] for term in iterate]).T
+    result_ref[...] = dot3(last, iterate).T
 
 
 def newton_schulz_power(*parts):
@@ -424,7 +422,7 @@
         out_shape=jax.ShapeDtypeStruct(whole.shape, whole.dtype),
         in_specs=[pl.BlockSpec(memory_space=pltpu.VMEM), hbm],
         out_specs=hbm,
-        scratch_shapes=[pltpu.SemaphoreType.DMA((4,))],
+        scratch_shapes=[pltpu.SemaphoreType.DMA((8,))],
         input_output_aliases={1: 0},
         compiler_params=params(4),
         name="put_layer",

time: 83.3 us -> 83.3 us (level)
  no operation moved by 1% of the time
where the time goes in v8:
time: 83.3 us; the launch traced here: 83.1 us
  starting transfers between devices  42.3 us (51%)
  Pallas kernels  21.1 us (25%)
  waiting for transfers between devices  18.8 us (23%)
  between operations  0.86 us (1%)
    ppermute x14, starting transfers between devices, over_z(): return lax.ppermute(x, 'shard', xor_pairs(k))  36 us
    ppermute x14, waiting for transfers between devices, over_z(): return lax.ppermute(x, 'shard', xor_pairs(k))  15.6 us
    pallas_call x18, Pallas kernels, local_call(): pl.pallas_call(kernel, out_shape=[pltpu.VMEM(shape, dtype) for shape, dty...  6.4 us
    ppermute x4, starting transfers between devices, over_y(): return lax.ppermute(x, 'tensor', xor_pairs(2))  5.68 us
    pallas_call x2, Pallas kernels, update_weights(): pl.pallas_call(functools.partial(update_kernel, factor, blocks), out_shap...  4.6 us
    ppermute x4, waiting for transfers between devices, over_y(): return lax.ppermute(x, 'tensor', xor_pairs(2))  3.25 us
    pallas_call x2, Pallas kernels, power_product(): pl.pallas_call(functools.partial(power_kernel, turn, scale), out_shape=[p...  3.01 us
    pallas_call x1, Pallas kernels, give(): pl.pallas_call(give_kernel, out_shape=pltpu.VMEM((2 * (rows + 16), rank),...  2.28 us
  transfers between devices with their start and end apart: 21, of which 14 were waited for; matrix products, arithmetic and copies ran while one was open for 0% of the time, Pallas kernels for 21%

profile of v8, /device:TPU:0, one launch (start us, length us, event | category | flops | bytes accessed | tf_op | source)
XLA Modules:
  0.0 83.1 jit_solution(17072067445396332640)
XLA Ops:
  0.6 2.3 %give.1 = bf16[416,256]{1,0:T(8,128)(2,1)S(1)} custom-call(bf16[1,2,768,768]{3,2,1,0:T(8,128)(2,1)} %grads_hbm.2, f32[2,768,256]{2,1,0:T(8,128)} %basis_hbm.2), custom_call_target="tpu_custom_call" | custom-call | tf_op jit(solution)/shard_map/give/pallas_call | solution.py:243
  2.9 3.1 %collective-permute-start = (bf16[416,256]{1,0:T(8,128)(2,1)S(1)}, bf16[416,256]{1,0:T(8,128)(2,1)S(1)}, u32[]{:S(2)}, u32[]{:S(2)}) collective-permute-start(bf16[416,256]{1,0:T(8,128)(2,1)S(1)} %give.1), channel_id=1, source_target_pairs={{0,8},{8,0},{16,24},{24,16},{1,9},{9,1},{17,25},{25,17},{2,10},{10... | collective-permute-start | bytes 638984 | tf_op jit(solution)/shard_map/ppermute | solution.py:494
  6.0 2.1 %prepare.1 = (bf16[1,2,768,768]{3,2,1,0:T(8,128)(2,1)S(1)}, bf16[2,768,256]{2,1,0:T(8,128)(2,1)S(1)}, bf16[2,768,256]{2,1,0:T(8,128)(2,1)S(1)}) custom-call(bf16[1,2,768,768]{3,2,1,0:T(8,128)(2,1)} %grads_hbm.2, f32[2,768,256]{2,1,0:T(8,128)} %basis_hbm.2), custom_call_target="tpu_custom_call" | custom-call | tf_op jit(solution)/shard_map/prepare/pallas_call | solution.py:164
  8.2 0.5 project.2.own_ref
  8.6 0.8 project.3
  9.5 1.7 %fetch.1 = (bf16[2,768,768]{2,1,0:T(8,128)(2,1)S(1)}, bf16[2,256,768]{2,1,0:T(8,128)(2,1)S(1)}, bf16[2,256,768]{2,1,0:T(8,128)(2,1)S(1)}) custom-call(bf16[2,768,768]{2,1,0:T(8,128)(2,1)} %weights_hbm, bf16[2,768,256]{2,1,0:T(8,128)(2,1)S(1)} %get-tuple-element.106.high_ref, bf16[2,768,256]{2,1,0:T(8,128)(2,1)S(1)} %get-tuple-element.107.low_ref), custom_call_target="tpu_custom_call" | custom-call | tf_op jit(solution)/shard_map/fetch/pallas_call | solution.py:190
  11.3 0.3 add_coded.4
  11.6 1.8 %collective-permute-start.1 = (bf16[416,256]{1,0:T(8,128)(2,1)S(1)}, bf16[416,256]{1,0:T(8,128)(2,1)S(1)}, u32[]{:S(2)}, u32[]{:S(2)}) collective-permute-start(bf16[416,256]{1,0:T(8,128)(2,1)S(1)} %get-tuple-element.112), channel_id=1, source_target_pairs={{0,8},{8,0},{16,24},{24,16},{1,9},{9,1},{17,25},{25,17},{2,10},{10... | collective-permute-start | bytes 638984 | tf_op jit(solution)/shard_map/ppermute | solution.py:494
  13.4 2.5 %collective-permute-start.3 = (bf16[416,256]{1,0:T(8,128)(2,1)S(1)}, bf16[416,256]{1,0:T(8,128)(2,1)S(1)}, u32[]{:S(2)}, u32[]{:S(2)}) collective-permute-start(bf16[416,256]{1,0:T(8,128)(2,1)S(1)} %get-tuple-element.117), channel_id=1, source_target_pairs={{0,24},{8,16},{16,8},{24,0},{1,25},{9,17},{17,9},{25,1},{2,26},{10... | collective-permute-start | bytes 638984 | tf_op jit(solution)/shard_map/ppermute | solution.py:494
  15.9 3.1 %collective-permute-done.1.received_ref = bf16[416,256]{1,0:T(8,128)(2,1)S(1)} collective-permute-done((bf16[416,256]{1,0:T(8,128)(2,1)S(1)}, bf16[416,256]{1,0:T(8,128)(2,1)S(1)}, u32[]{:S(2)}, u32[]{:S(2)}) %collective-permute-start.1) | collective-permute-done | bytes 213024 | tf_op jit(solution)/shard_map/ppermute | solution.py:494
  19.0 0.3 add_coded.5
  19.4 9.5 %collective-permute-start.2 = (bf16[416,256]{1,0:T(8,128)(2,1)S(1)}, bf16[416,256]{1,0:T(8,128)(2,1)S(1)}, u32[]{:S(2)}, u32[]{:S(2)}) collective-permute-start(bf16[416,256]{1,0:T(8,128)(2,1)S(1)} %get-tuple-element.116), channel_id=1, source_target_pairs={{0,24},{8,16},{16,8},{24,0},{1,25},{9,17},{17,9},{25,1},{2,26},{10... | collective-permute-start | bytes 638984 | tf_op jit(solution)/shard_map/ppermute | solution.py:494
  28.8 0.3 add_coded.6
  29.2 0.1 collective-permute-start.5
  29.3 3.5 %collective-permute-done.2.received_ref = bf16[416,256]{1,0:T(8,128)(2,1)S(1)} collective-permute-done((bf16[416,256]{1,0:T(8,128)(2,1)S(1)}, bf16[416,256]{1,0:T(8,128)(2,1)S(1)}, u32[]{:S(2)}, u32[]{:S(2)}) %collective-permute-start.2) | collective-permute-done | bytes 213024 | tf_op jit(solution)/shard_map/ppermute | solution.py:494
  32.8 0.3 add_coded.7
  33.1 1.7 %collective-permute-start.4 = (bf16[416,256]{1,0:T(8,128)(2,1)S(1)}, bf16[416,256]{1,0:T(8,128)(2,1)S(1)}, u32[]{:S(2)}, u32[]{:S(2)}) collective-permute-start(bf16[416,256]{1,0:T(8,128)(2,1)S(1)} %get-tuple-element.124), channel_id=1, source_target_pairs={{0,8},{8,0},{16,24},{24,16},{1,9},{9,1},{17,25},{25,17},{2,10},{10... | collective-permute-start | bytes 638984 | tf_op jit(solution)/shard_map/ppermute | solution.py:494
  34.8 0.3 collective-permute-done.5.given_ref
  35.1 1.5 %power.2 = (f32[128,768]{1,0:T(8,128)S(1)}, f32[128,768]{1,0:T(8,128)S(1)}, f32[2,192,256]{2,1,0:T(8,128)}, f32[2,192,256]{2,1,0:T(8,128)}, bf16[208,256]{1,0:T(8,128)(2,1)S(1)}) custom-call(bf16[1,2,768,768]{3,2,1,0:T(8,128)(2,1)S(1)} %get-tuple-element.102.grads_ref, f32[2,192,256]{2,1,0:T(8,128)S(1)} %copy-done, f32[2,192,256]{2,1,0:T(8,128)S(1)} %copy-done.1, ...), custom_call_target="tpu_custom_call" | custom-call | tf_op jit(solution)/shard_map/power/pallas_call | solution.py:324
  36.7 0.5 collective-permute-start.6
  37.2 2.7 %collective-permute-done.4.given_ref = bf16[416,256]{1,0:T(8,128)(2,1)S(1)} collective-permute-done((bf16[416,256]{1,0:T(8,128)(2,1)S(1)}, bf16[416,256]{1,0:T(8,128)(2,1)S(1)}, u32[]{:S(2)}, u32[]{:S(2)}) %collective-permute-start.4) | collective-permute-done | bytes 213024 | tf_op jit(solution)/shard_map/ppermute | solution.py:494
  39.9 1.5 %power.3 = (f32[128,768]{1,0:T(8,128)S(1)}, f32[128,768]{1,0:T(8,128)S(1)}, f32[2,192,256]{2,1,0:T(8,128)}, f32[2,192,256]{2,1,0:T(8,128)}, bf16[2,208,256]{2,1,0:T(8,128)(2,1)S(1)}) custom-call(bf16[1,2,768,768]{3,2,1,0:T(8,128)(2,1)S(1)} %get-tuple-element.102.grads_ref, f32[2,192,256]{2,1,0:T(8,128)S(1)} %copy-done, ...), custom_call_target="tpu_custom_call", output_to_operand_aliasing={{2}: (5, {}), {3}: (6, {})} | custom-call | flops 2000000000 | tf_op jit(solution)/shard_map/power/pallas_call | solution.py:324
  41.4 1.6 %collective-permute-start.9 = (f32[64,768]{1,0:T(8,128)S(1)}, f32[64,768]{1,0:T(8,128)S(1)}, u32[]{:S(2)}, u32[]{:S(2)}) collective-permute-start(f32[64,768]{1,0:T(8,128)S(1)} %get-tuple-element.145), channel_id=1, source_target_pairs={{0,4},{2,6},{4,0},{6,2},{1,5},{3,7},{5,1},{7,3},{8,12},{10,14},{12... | collective-permute-start | bytes 589832 | tf_op jit(solution)/shard_map/ppermute | solution.py:502
  43.1 3.0 %collective-permute-start.8 = (bf16[2,208,256]{2,1,0:T(8,128)(2,1)S(1)}, bf16[2,208,256]{2,1,0:T(8,128)(2,1)S(1)}, u32[]{:S(2)}, u32[]{:S(2)}) collective-permute-start(bf16[2,208,256]{2,1,0:T(8,128)(2,1)S(1)} %get-tuple-element.170.a_ref), channel_id=1, source_target_pairs={{0,24},{8,16},{16,8},{24,0},{1,25},{9,17},{17,9},{25,1},{2,26},{10... | collective-permute-start | bytes 638984 | tf_op jit(solution)/shard_map/ppermute | solution.py:494
  46.1 0.5 collective-permute-start.11
  46.6 0.7 collective-permute-done.9.received_ref
  47.3 3.7 %collective-permute-start.10 = (f32[32,768]{1,0:T(8,128)S(1)}, f32[32,768]{1,0:T(8,128)S(1)}, u32[]{:S(2)}, u32[]{:S(2)}) collective-permute-start(f32[32,768]{1,0:T(8,128)S(1)} %get-tuple-element.149), channel_id=1, source_target_pairs={{0,8},{8,0},{16,24},{24,16},{1,9},{9,1},{17,25},{25,17},{2,10},{10... | collective-permute-start | bytes 294920 | tf_op jit(solution)/shard_map/ppermute | solution.py:494
  51.0 0.7 collective-permute-done.11.received_ref
  51.8 1.3 %collective-permute-start.13 = (f32[32,768]{1,0:T(8,128)S(1)}, f32[32,768]{1,0:T(8,128)S(1)}, u32[]{:S(2)}, u32[]{:S(2)}) collective-permute-start(f32[32,768]{1,0:T(8,128)S(1)} %get-tuple-element.159), channel_id=1, source_target_pairs={{0,8},{8,0},{16,24},{24,16},{1,9},{9,1},{17,25},{25,17},{2,10},{10... | collective-permute-start | bytes 294920 | tf_op jit(solution)/shard_map/ppermute | solution.py:494
  53.1 1.0 %collective-permute-done.10.received_ref = f32[32,768]{1,0:T(8,128)S(1)} collective-permute-done((f32[32,768]{1,0:T(8,128)S(1)}, f32[32,768]{1,0:T(8,128)S(1)}, u32[]{:S(2)}, u32[]{:S(2)}) %collective-permute-start.10) | collective-permute-done | bytes 98336 | tf_op jit(solution)/shard_map/ppermute | solution.py:494
  54.2 3.1 %collective-permute-start.12 = (f32[32,768]{1,0:T(8,128)S(1)}, f32[32,768]{1,0:T(8,128)S(1)}, u32[]{:S(2)}, u32[]{:S(2)}) collective-permute-start(f32[32,768]{1,0:T(8,128)S(1)} %add.4.own_ref), channel_id=1, source_target_pairs={{0,24},{8,16},{16,8},{24,0},{1,25},{9,17},{17,9},{25,1},{2,26},{10... | collective-permute-start | bytes 294920 | tf_op jit(solution)/shard_map/ppermute | solution.py:494
  57.4 0.2 collective-permute-done.13.received_ref
  57.5 2.1 %collective-permute-start.15 = (f32[32,768]{1,0:T(8,128)S(1)}, f32[32,768]{1,0:T(8,128)S(1)}, u32[]{:S(2)}, u32[]{:S(2)}) collective-permute-start(f32[32,768]{1,0:T(8,128)S(1)} %add.5.own_ref), channel_id=1, source_target_pairs={{0,24},{8,16},{16,8},{24,0},{1,25},{9,17},{17,9},{25,1},{2,26},{10... | collective-permute-start | bytes 294920 | tf_op jit(solution)/shard_map/ppermute | solution.py:494
  59.6 1.3 %collective-permute-done.12.received_ref = f32[32,768]{1,0:T(8,128)S(1)} collective-permute-done((f32[32,768]{1,0:T(8,128)S(1)}, f32[32,768]{1,0:T(8,128)S(1)}, u32[]{:S(2)}, u32[]{:S(2)}) %collective-permute-start.12) | collective-permute-done | bytes 98336 | tf_op jit(solution)/shard_map/ppermute | solution.py:494
  60.9 2.0 %collective-permute-start.14 = (f32[32,768]{1,0:T(8,128)S(1)}, f32[32,768]{1,0:T(8,128)S(1)}, u32[]{:S(2)}, u32[]{:S(2)}) collective-permute-start(f32[32,768]{1,0:T(8,128)S(1)} %add.6.own_ref), channel_id=1, source_target_pairs={{0,8},{8,0},{16,24},{24,16},{1,9},{9,1},{17,25},{25,17},{2,10},{10... | collective-permute-start | bytes 294920 | tf_op jit(solution)/shard_map/ppermute | solution.py:494
  62.9 1.3 %collective-permute-done.15.received_ref = f32[32,768]{1,0:T(8,128)S(1)} collective-permute-done((f32[32,768]{1,0:T(8,128)S(1)}, f32[32,768]{1,0:T(8,128)S(1)}, u32[]{:S(2)}, u32[]{:S(2)}) %collective-permute-start.15) | collective-permute-done | bytes 98336 | tf_op jit(solution)/shard_map/ppermute | solution.py:494
  64.2 0.8 collective-permute-start.17
  65.0 1.2 %collective-permute-done.14.received_ref = f32[32,768]{1,0:T(8,128)S(1)} collective-permute-done((f32[32,768]{1,0:T(8,128)S(1)}, f32[32,768]{1,0:T(8,128)S(1)}, u32[]{:S(2)}, u32[]{:S(2)}) %collective-permute-start.14) | collective-permute-done | bytes 98336 | tf_op jit(solution)/shard_map/ppermute | solution.py:494
  66.2 2.0 %collective-permute-start.16 = (f32[64,768]{1,0:T(8,128)S(1)}, f32[64,768]{1,0:T(8,128)S(1)}, u32[]{:S(2)}, u32[]{:S(2)}) collective-permute-start(f32[64,768]{1,0:T(8,128)S(1)} %join.2.refs_0_), channel_id=1, source_target_pairs={{0,4},{2,6},{4,0},{6,2},{1,5},{3,7},{5,1},{7,3},{8,12},{10,14},{12... | collective-permute-start | bytes 589832 | tf_op jit(solution)/shard_map/ppermute | solution.py:502
  68.3 1.0 %collective-permute-done.17.received_ref = f32[32,768]{1,0:T(8,128)S(1)} collective-permute-done((f32[32,768]{1,0:T(8,128)S(1)}, f32[32,768]{1,0:T(8,128)S(1)}, u32[]{:S(2)}, u32[]{:S(2)}) %collective-permute-start.17) | collective-permute-done | bytes 98336 | tf_op jit(solution)/shard_map/ppermute | solution.py:494
  69.3 1.3 %collective-permute-start.18 = (bf16[2,2,208,256]{3,2,1,0:T(8,128)(2,1)S(1)}, bf16[2,2,208,256]{3,2,1,0:T(8,128)(2,1)S(1)}, u32[]{:S(2)}, u32[]{:S(2)}) collective-permute-start(bf16[2,2,208,256]{3,2,1,0:T(8,128)(2,1)S(1)} %stack.1), channel_id=1, source_target_pairs={{0,8},{8,0},{16,24},{24,16},{1,9},{9,1},{17,25},{25,17},{2,10},{10... | collective-permute-start | bytes 1277960 | tf_op jit(solution)/shard_map/ppermute | solution.py:494
  70.6 1.6 %collective-permute-start.19 = (f32[64,768]{1,0:T(8,128)S(1)}, f32[64,768]{1,0:T(8,128)S(1)}, u32[]{:S(2)}, u32[]{:S(2)}) collective-permute-start(f32[64,768]{1,0:T(8,128)S(1)} %join.3.refs_2_), channel_id=1, source_target_pairs={{0,4},{2,6},{4,0},{6,2},{1,5},{3,7},{5,1},{7,3},{8,12},{10,14},{12... | collective-permute-start | bytes 589832 | tf_op jit(solution)/shard_map/ppermute | solution.py:502
  72.1 0.8 collective-permute-done.16.refs_1_
  72.9 2.3 %update_weights.2.refs_3_ = bf16[2,768,768]{2,1,0:T(8,128)(2,1)} custom-call(bf16[2,768,768]{2,1,0:T(8,128)(2,1)S(1)} %get-tuple-element.172.weights_ref, bf16[2,256,768]{2,1,0:T(8,128)(2,1)S(1)} %get-tuple-element.173.high_ref, bf16[2,256,768]{2,1,0:T(8,128)(2,1)S(1)} %get-tuple-element.174.low_ref, bf16[1,2,208,256]{3,2,1,0:T(8,128)(2,1)S(1)} %bitcast.2, ...), custom_call_target="tpu_custom_call" | custom-call | flops 3000000000 | tf_op jit(solution)/shard_map/update_weights/pallas_call | solution.py:476
  75.2 1.0 %collective-permute-done.19.refs_3_ = f32[64,768]{1,0:T(8,128)S(1)} collective-permute-done((f32[64,768]{1,0:T(8,128)S(1)}, f32[64,768]{1,0:T(8,128)S(1)}, u32[]{:S(2)}, u32[]{:S(2)}) %collective-permute-start.19) | collective-permute-done | bytes 196640 | tf_op jit(solution)/shard_map/ppermute | solution.py:502
  76.2 3.5 %newton_schulz.1.refs_2_ = f32[768,256]{1,0:T(8,128)S(1)} custom-call(f32[64,768]{1,0:T(8,128)S(1)} %join.2.refs_0_, f32[64,768]{1,0:T(8,128)S(1)} %collective-permute-done.16.refs_1_, f32[64,768]{1,0:T(8,128)S(1)} %join.3.refs_2_, f32[64,768]{1,0:T(8,128)S(1)} %collective-permute-done.19.refs_3_), custom_call_target="tpu_custom_call" | custom-call | tf_op jit(solution)/shard_map/newton_schulz/pallas_call | solution.py:115
  79.8 2.3 %update_weights.3 = (bf16[2,768,768]{2,1,0:T(8,128)(2,1)}, f32[2,768,256]{2,1,0:T(8,128)}) custom-call(bf16[2,768,768]{2,1,0:T(8,128)(2,1)S(1)} %get-tuple-element.172.weights_ref, bf16[2,256,768]{2,1,0:T(8,128)(2,1)S(1)} %get-tuple-element.173.high_ref, bf16[2,256,768]{2,1,0:T(8,128)(2,1)S(1)} %get-tuple-element.174.low_ref, ...), custom_call_target="tpu_custom_call", output_to_operand_aliasing={{0}: (6, {})} | custom-call | flops 8000000000 | tf_op jit(solution)/shard_map/update_weights/pallas_call | solution.py:476
  82.2 1.0 %put_layer.1 = f32[2,768,256]{2,1,0:T(8,128)} custom-call(f32[768,256]{1,0:T(8,128)S(1)} %collective-permute-done.20.layer_ref, f32[2,768,256]{2,1,0:T(8,128)} %get-tuple-element.187.whole_ref), custom_call_target="tpu_custom_call", output_to_operand_aliasing={{}: (1, {})} | custom-call | tf_op jit(solution)/shard_map/put_layer/pallas_call | solution.py:420
  (24 shorter events, 0.5 us)
Async XLA Ops:
  2.9 8.3 %collective-permute-start = (bf16[416,256]{1,0:T(8,128)(2,1)S(1)}, bf16[416,256]{1,0:T(8,128)(2,1)S(1)}, u32[]{:S(2)}, u32[]{:S(2)}) collective-permute-start(bf16[416,256]{1,0:T(8,128)(2,1)S(1)} %give.1), channel_id=1, source_target_pairs={{0,8},{8,0},{16,24},{24,16},{1,9},{9,1},{17,25},{25,17},{2,10},{10... | collective-permute-start | bytes 638984 | tf_op jit(solution)/shard_map/ppermute | solution.py:494
  9.5 25.6 %copy-start = (f32[2,192,256]{2,1,0:T(8,128)S(1)}, f32[2,192,256]{2,1,0:T(8,128)}, u32[]{:S(2)}) copy-start(f32[2,192,256]{2,1,0:T(8,128)} %first_ref.3) | copy-start | bytes 1179652
  9.5 25.6 %copy-start.1 = (f32[2,192,256]{2,1,0:T(8,128)S(1)}, f32[2,192,256]{2,1,0:T(8,128)}, u32[]{:S(2)}) copy-start(f32[2,192,256]{2,1,0:T(8,128)} %second_ref.3) | copy-start | bytes 1179652
  11.6 7.4 %collective-permute-start.1 = (bf16[416,256]{1,0:T(8,128)(2,1)S(1)}, bf16[416,256]{1,0:T(8,128)(2,1)S(1)}, u32[]{:S(2)}, u32[]{:S(2)}) collective-permute-start(bf16[416,256]{1,0:T(8,128)(2,1)S(1)} %get-tuple-element.112), channel_id=1, source_target_pairs={{0,8},{8,0},{16,24},{24,16},{1,9},{9,1},{17,25},{25,17},{2,10},{10... | collective-permute-start | bytes 638984 | tf_op jit(solution)/shard_map/ppermute | solution.py:494
  13.4 15.4 %collective-permute-start.3 = (bf16[416,256]{1,0:T(8,128)(2,1)S(1)}, bf16[416,256]{1,0:T(8,128)(2,1)S(1)}, u32[]{:S(2)}, u32[]{:S(2)}) collective-permute-start(bf16[416,256]{1,0:T(8,128)(2,1)S(1)} %get-tuple-element.117), channel_id=1, source_target_pairs={{0,24},{8,16},{16,8},{24,0},{1,25},{9,17},{17,9},{25,1},{2,26},{10... | collective-permute-start | bytes 638984 | tf_op jit(solution)/shard_map/ppermute | solution.py:494
  19.4 13.4 %collective-permute-start.2 = (bf16[416,256]{1,0:T(8,128)(2,1)S(1)}, bf16[416,256]{1,0:T(8,128)(2,1)S(1)}, u32[]{:S(2)}, u32[]{:S(2)}) collective-permute-start(bf16[416,256]{1,0:T(8,128)(2,1)S(1)} %get-tuple-element.116), channel_id=1, source_target_pairs={{0,24},{8,16},{16,8},{24,0},{1,25},{9,17},{17,9},{25,1},{2,26},{10... | collective-permute-start | bytes 638984 | tf_op jit(solution)/shard_map/ppermute | solution.py:494
  29.2 5.9 %collective-permute-start.5 = (bf16[416,256]{1,0:T(8,128)(2,1)S(1)}, bf16[416,256]{1,0:T(8,128)(2,1)S(1)}, u32[]{:S(2)}, u32[]{:S(2)}) collective-permute-start(bf16[416,256]{1,0:T(8,128)(2,1)S(1)} %get-tuple-element.125), channel_id=1, source_target_pairs={{0,8},{8,0},{16,24},{24,16},{1,9},{9,1},{17,25},{25,17},{2,10},{10... | collective-permute-start | bytes 638984 | tf_op jit(solution)/shard_map/ppermute | solution.py:494
  33.1 6.8 %collective-permute-start.4 = (bf16[416,256]{1,0:T(8,128)(2,1)S(1)}, bf16[416,256]{1,0:T(8,128)(2,1)S(1)}, u32[]{:S(2)}, u32[]{:S(2)}) collective-permute-start(bf16[416,256]{1,0:T(8,128)(2,1)S(1)} %get-tuple-element.124), channel_id=1, source_target_pairs={{0,8},{8,0},{16,24},{24,16},{1,9},{9,1},{17,25},{25,17},{2,10},{10... | collective-permute-start | bytes 638984 | tf_op jit(solution)/shard_map/ppermute | solution.py:494
  36.6 4.8 %collective-permute-start.7 = (f32[128,768]{1,0:T(8,128)S(1)}, f32[128,768]{1,0:T(8,128)S(1)}, u32[]{:S(2)}, u32[]{:S(2)}) collective-permute-start(f32[128,768]{1,0:T(8,128)S(1)} %get-tuple-element.128), channel_id=1, source_target_pairs={{0,2},{2,0},{4,6},{6,4},{1,3},{3,1},{5,7},{7,5},{8,10},{10,8},{12,... | collective-permute-start | bytes 1179656 | tf_op jit(solution)/shard_map/ppermute | solution.py:498
  36.7 4.7 %collective-permute-start.6 = (f32[128,768]{1,0:T(8,128)S(1)}, f32[128,768]{1,0:T(8,128)S(1)}, u32[]{:S(2)}, u32[]{:S(2)}) collective-permute-start(f32[128,768]{1,0:T(8,128)S(1)} %get-tuple-element.136), channel_id=1, source_target_pairs={{0,2},{2,0},{4,6},{6,4},{1,3},{3,1},{5,7},{7,5},{8,10},{10,8},{12,... | collective-permute-start | bytes 1179656 | tf_op jit(solution)/shard_map/ppermute | solution.py:498
  41.4 5.9 %collective-permute-start.9 = (f32[64,768]{1,0:T(8,128)S(1)}, f32[64,768]{1,0:T(8,128)S(1)}, u32[]{:S(2)}, u32[]{:S(2)}) collective-permute-start(f32[64,768]{1,0:T(8,128)S(1)} %get-tuple-element.145), channel_id=1, source_target_pairs={{0,4},{2,6},{4,0},{6,2},{1,5},{3,7},{5,1},{7,3},{8,12},{10,14},{12... | collective-permute-start | bytes 589832 | tf_op jit(solution)/shard_map/ppermute | solution.py:502
  43.1 10.1 %collective-permute-start.8 = (bf16[2,208,256]{2,1,0:T(8,128)(2,1)S(1)}, bf16[2,208,256]{2,1,0:T(8,128)(2,1)S(1)}, u32[]{:S(2)}, u32[]{:S(2)}) collective-permute-start(bf16[2,208,256]{2,1,0:T(8,128)(2,1)S(1)} %get-tuple-element.170.a_ref), channel_id=1, source_target_pairs={{0,24},{8,16},{16,8},{24,0},{1,25},{9,17},{17,9},{25,1},{2,26},{10... | collective-permute-start | bytes 638984 | tf_op jit(solution)/shard_map/ppermute | solution.py:494
  46.1 5.7 %collective-permute-start.11 = (f32[64,768]{1,0:T(8,128)S(1)}, f32[64,768]{1,0:T(8,128)S(1)}, u32[]{:S(2)}, u32[]{:S(2)}) collective-permute-start(f32[64,768]{1,0:T(8,128)S(1)} %get-tuple-element.150), channel_id=1, source_target_pairs={{0,4},{2,6},{4,0},{6,2},{1,5},{3,7},{5,1},{7,3},{8,12},{10,14},{12... | collective-permute-start | bytes 589832 | tf_op jit(solution)/shard_map/ppermute | solution.py:502
  47.3 6.9 %collective-permute-start.10 = (f32[32,768]{1,0:T(8,128)S(1)}, f32[32,768]{1,0:T(8,128)S(1)}, u32[]{:S(2)}, u32[]{:S(2)}) collective-permute-start(f32[32,768]{1,0:T(8,128)S(1)} %get-tuple-element.149), channel_id=1, source_target_pairs={{0,8},{8,0},{16,24},{24,16},{1,9},{9,1},{17,25},{25,17},{2,10},{10... | collective-permute-start | bytes 294920 | tf_op jit(solution)/shard_map/ppermute | solution.py:494
  51.8 5.7 %collective-permute-start.13 = (f32[32,768]{1,0:T(8,128)S(1)}, f32[32,768]{1,0:T(8,128)S(1)}, u32[]{:S(2)}, u32[]{:S(2)}) collective-permute-start(f32[32,768]{1,0:T(8,128)S(1)} %get-tuple-element.159), channel_id=1, source_target_pairs={{0,8},{8,0},{16,24},{24,16},{1,9},{9,1},{17,25},{25,17},{2,10},{10... | collective-permute-start | bytes 294920 | tf_op jit(solution)/shard_map/ppermute | solution.py:494
  54.2 6.7 %collective-permute-start.12 = (f32[32,768]{1,0:T(8,128)S(1)}, f32[32,768]{1,0:T(8,128)S(1)}, u32[]{:S(2)}, u32[]{:S(2)}) collective-permute-start(f32[32,768]{1,0:T(8,128)S(1)} %add.4.own_ref), channel_id=1, source_target_pairs={{0,24},{8,16},{16,8},{24,0},{1,25},{9,17},{17,9},{25,1},{2,26},{10... | collective-permute-start | bytes 294920 | tf_op jit(solution)/shard_map/ppermute | solution.py:494
  57.5 6.7 %collective-permute-start.15 = (f32[32,768]{1,0:T(8,128)S(1)}, f32[32,768]{1,0:T(8,128)S(1)}, u32[]{:S(2)}, u32[]{:S(2)}) collective-permute-start(f32[32,768]{1,0:T(8,128)S(1)} %add.5.own_ref), channel_id=1, source_target_pairs={{0,24},{8,16},{16,8},{24,0},{1,25},{9,17},{17,9},{25,1},{2,26},{10... | collective-permute-start | bytes 294920 | tf_op jit(solution)/shard_map/ppermute | solution.py:494
  60.9 5.3 %collective-permute-start.14 = (f32[32,768]{1,0:T(8,128)S(1)}, f32[32,768]{1,0:T(8,128)S(1)}, u32[]{:S(2)}, u32[]{:S(2)}) collective-permute-start(f32[32,768]{1,0:T(8,128)S(1)} %add.6.own_ref), channel_id=1, source_target_pairs={{0,8},{8,0},{16,24},{24,16},{1,9},{9,1},{17,25},{25,17},{2,10},{10... | collective-permute-start | bytes 294920 | tf_op jit(solution)/shard_map/ppermute | solution.py:494
  64.2 5.0 %collective-permute-start.17 = (f32[32,768]{1,0:T(8,128)S(1)}, f32[32,768]{1,0:T(8,128)S(1)}, u32[]{:S(2)}, u32[]{:S(2)}) collective-permute-start(f32[32,768]{1,0:T(8,128)S(1)} %add.7.own_ref), channel_id=1, source_target_pairs={{0,8},{8,0},{16,24},{24,16},{1,9},{9,1},{17,25},{25,17},{2,10},{10... | collective-permute-start | bytes 294920 | tf_op jit(solution)/shard_map/ppermute | solution.py:494
  66.2 6.7 %collective-permute-start.16 = (f32[64,768]{1,0:T(8,128)S(1)}, f32[64,768]{1,0:T(8,128)S(1)}, u32[]{:S(2)}, u32[]{:S(2)}) collective-permute-start(f32[64,768]{1,0:T(8,128)S(1)} %join.2.refs_0_), channel_id=1, source_target_pairs={{0,4},{2,6},{4,0},{6,2},{1,5},{3,7},{5,1},{7,3},{8,12},{10,14},{12... | collective-permute-start | bytes 589832 | tf_op jit(solution)/shard_map/ppermute | solution.py:502
  69.3 10.5 %collective-permute-start.18 = (bf16[2,2,208,256]{3,2,1,0:T(8,128)(2,1)S(1)}, bf16[2,2,208,256]{3,2,1,0:T(8,128)(2,1)S(1)}, u32[]{:S(2)}, u32[]{:S(2)}) collective-permute-start(bf16[2,2,208,256]{3,2,1,0:T(8,128)(2,1)S(1)} %stack.1), channel_id=1, source_target_pairs={{0,8},{8,0},{16,24},{24,16},{1,9},{9,1},{17,25},{25,17},{2,10},{10... | collective-permute-start | bytes 1277960 | tf_op jit(solution)/shard_map/ppermute | solution.py:494
  70.6 5.7 %collective-permute-start.19 = (f32[64,768]{1,0:T(8,128)S(1)}, f32[64,768]{1,0:T(8,128)S(1)}, u32[]{:S(2)}, u32[]{:S(2)}) collective-permute-start(f32[64,768]{1,0:T(8,128)S(1)} %join.3.refs_2_), channel_id=1, source_target_pairs={{0,4},{2,6},{4,0},{6,2},{1,5},{3,7},{5,1},{7,3},{8,12},{10,14},{12... | collective-permute-start | bytes 589832 | tf_op jit(solution)/shard_map/ppermute | solution.py:502
  79.7 2.4 %collective-permute-start.20 = (f32[768,256]{1,0:T(8,128)S(1)}, f32[768,256]{1,0:T(8,128)S(1)}, u32[]{:S(2)}, u32[]{:S(2)}) collective-permute-start(f32[768,256]{1,0:T(8,128)S(1)} %newton_schulz.1.refs_2_), channel_id=1, source_target_pairs={{0,2},{2,0},{4,6},{6,4},{1,3},{3,1},{5,7},{7,5},{8,10},{10,8},{12,... | collective-permute-start | bytes 2359304 | tf_op jit(solution)/shard_map/ppermute | solution.py:498
